TPU v7x, 32 devices: a whole 2x2x4 slice. The times are simulated.
32 devices in a mesh: gx: 16 (over z, x, core), yz: 2 (over y).
Axes of the slice: x: 2, y: 2, z: 4, core: 2. Of those that a mesh axis runs over, the one named last changes fastest.
Arguments:
- conformation: float32 [3, 64, 384, 1024], P(None, 'gx', 'yz'), may hold values from -0.49 to 2.5, as said below
- velocity: float32 [3, 64, 384, 1024], P(None, 'gx', 'yz'), may hold values from -6 to 6
Outputs:
- updated: float32 [3, 64, 384, 1024], P(None, 'gx', 'yz')
Inputs may be any that keep to these rules, and one draw needn't show every extreme that they name: `conformation`: components 0 and 2 (c_xx, c_yy) lie in [0.5, 2.5] and component 1 (c_xy) in [-0.49, 0.49].
All inputs are finite; a program needn't handle non-finite values.
Results may differ from a plain program's by a relative error of at most 0.000076.
Values sent between devices are 32-bit elements; how exact they have to be, the bound alone decides.
No kernel may reach another device: no remote copies, remote signals or barrier semaphores. Data moves between devices by JAX's collectives and lax.ppermute only.
A program may use at most 256 MiB of HBM per device.

v0:
```python
import math

import jax
import jax.numpy as jnp
from jax import lax
from jax.sharding import PartitionSpec as P

stencil_coeffs = (0.8, -0.2, 4.0 / 105.0, -1.0 / 280.0)
extensibility = 10.0
relax_rate = 1.0 / 0.04
courant = 0.5


def padded_2(x, sides, width):
    for axis, dim in sides:
        count, length = (lax.axis_size(axis), x.shape[dim])
        up = [(i, (i + 1) % count) for i in range(count)]
        down = [(j, i) for i, j in up]
        last = lax.slice_in_dim(x, length - width, length, axis=dim)
        initial = lax.slice_in_dim(x, 0, width, axis=dim)
        before = lax.ppermute(last, axis, up)
        after = lax.ppermute(initial, axis, down)
        x = jnp.concatenate([before, x, after], axis=dim)
    return x


def storage_points(count, groups):
    index = jnp.arange(count, dtype=jnp.int32)
    per_group = count // groups
    return index % per_group * groups + index // per_group


def cheb_matrix(count, points):
    last = count - 1
    half_step = math.pi / (2.0 * last)
    weights = jnp.where((points == 0) | (points == last), 2.0, 1.0).astype(jnp.float32)
    same = points[:, None] == points[None, :]
    sums = (points[:, None] + points[None, :]).astype(jnp.float32) * half_step
    diffs = (points[:, None] - points[None, :]).astype(jnp.float32) * half_step
    signs = (1 - 2 * ((points[:, None] + points[None, :]) % 2)).astype(jnp.float32)
    apart = -2.0 * jnp.sin(sums) * jnp.sin(diffs)
    safe = jnp.where(same, 1.0, apart)
    offdiag = jnp.where(same, 0.0, weights[:, None] / weights[None, :] * signs / safe)
    return offdiag - jnp.diag(jnp.sum(offdiag, axis=1))


def centered(padded, width, count, axis, spacing):
    total = jnp.zeros_like(lax.slice_in_dim(padded, width, width + count, axis=axis))
    for offset, coeff in enumerate(stencil_coeffs, start=1):
        ahead = lax.slice_in_dim(padded, width + offset, width + offset + count, axis=axis)
        behind = lax.slice_in_dim(padded, width - offset, width - offset + count, axis=axis)
        total = total + coeff * (ahead - behind)
    return total / spacing


def wall_terms(comp, vel_v, dy_comp, dy_u, dy_v):
    term_xx = -vel_v * dy_comp[0] + 2.0 * dy_u * comp[1]
    term_xy = -vel_v * dy_comp[1] + dy_u * comp[2] + dy_v * comp[1]
    term_yy = -vel_v * dy_comp[2] + 2.0 * dy_v * comp[2]
    return jnp.stack([term_xx, term_xy, term_yy])


def local_terms(comp, vel, along_x, along_z):
    peterlin = (extensibility - 2.0) / (extensibility - comp[0] - comp[2])
    grad_ux = along_x[3]
    grad_vx = along_x[4]
    term_xx = (
        -vel[0] * along_x[0]
        - vel[2] * along_z[0]
        + 2.0 * grad_ux * comp[0]
        - relax_rate * (peterlin * comp[0] - 1.0)
    )
    term_xy = (
        -vel[0] * along_x[1]
        - vel[2] * along_z[1]
        + grad_ux * comp[1]
        + grad_vx * comp[0]
        - relax_rate * peterlin * comp[1]
    )
    term_yy = (
        -vel[0] * along_x[2]
        - vel[2] * along_z[2]
        + 2.0 * grad_vx * comp[1]
        - relax_rate * (peterlin * comp[2] - 1.0)
    )
    return jnp.stack([term_xx, term_xy, term_yy])


def shards(conformation, velocity):
    planes = conformation.shape[1]
    local_rows = conformation.shape[2]
    groups = lax.axis_size("yz")
    count = local_rows * groups
    spacing = math.pi / (count - 1)
    points = storage_points(count, groups)
    cheb = cheb_matrix(count, points)
    points_here = jnp.arange(local_rows, dtype=jnp.int32) * groups + lax.axis_index("yz")
    theta = math.pi * points_here.astype(jnp.float32) / (count - 1)
    step_size = courant * spacing * (jnp.sin(theta) + spacing)
    block = jnp.concatenate([conformation, velocity[0:2]], axis=0)
    derived = jnp.einsum(
        "ij,fkjz->fkiz",
        cheb,
        lax.all_to_all(block, "yz", split_axis=3, concat_axis=2, tiled=True),
        precision=lax.Precision.HIGHEST,
    )
    returned_back = lax.all_to_all(derived, "yz", split_axis=2, concat_axis=3, tiled=True)
    yterms = wall_terms(
        conformation, velocity[1], returned_back[0:3], returned_back[3], returned_back[4]
    )
    padded = padded_2(block, (("gx", 1),), 4)
    along_x = centered(padded, 4, planes, 1, spacing)
    padded_z = jnp.pad(conformation, ((0, 0), (0, 0), (0, 0), (4, 4)), mode="wrap")
    along_z = centered(padded_z, 4, conformation.shape[3], 3, spacing)
    other = local_terms(conformation, velocity, along_x, along_z)
    return conformation + step_size[None, None, :, None] * (other + yterms)


def solution(mesh):
    in_specs = (P(None, "gx", "yz", None), P(None, "gx", "yz", None))
    out_specs = P(None, "gx", "yz", None)
    return jax.shard_map(shards, mesh=mesh, in_specs=in_specs, out_specs=out_specs, check_vma=False)
```

profile of v0, /device:TPU:16, one launch (start us, length us, event | category | flops | bytes accessed | tf_op | source)
XLA Modules:
  0.0 632.3 jit_solution(1645302906625651038)
XLA Ops:
  0.0 3.5 slice.149
  3.5 2.0 copy-done
  5.5 6.6 %pad_maximum_fusion.1 = f32[5,4,192,1024]{3,2,1,0:T(8,128)} fusion(f32[2,4,192,1024]{3,2,1,0:T(8,128)S(1)} %slice.149, f32[3,4,192,1024]{3,2,1,0:T(8,128)S(1)} %copy-done), kind=kLoop, calls=%fused_computation.18 | loop fusion | flops 3932160 | bytes 31457280 | tf_op jit(solution)/shard_map/concatenate | solution.py:100
  12.1 0.8 copy-done.2
  12.9 0.8 collective-permute-start
  13.7 21.9 %copy.19 = f32[5,4,192,1024]{2,1,0,3:T(4,128)} copy(f32[5,4,192,1024]{3,2,1,0:T(8,128)} %pad_maximum_fusion.1) | data formatting | bytes 31457280 | tf_op jit(solution)/shard_map/concatenate | solution.py:100
  35.6 11.2 %all-to-all-start = ((f32[5,4,192,1024]{2,1,0,3:T(4,128)}), f32[5,4,192,1024]{2,1,0,3:T(4,128)}, u32[]{:S(2)}, u32[]{:S(2)}) async-start(f32[5,4,192,1024]{2,1,0,3:T(4,128)} %copy.19), calls=%async_computation | async-start | bytes 41943040 | tf_op jit(solution)/shard_map/all_to_all | solution.py:104
  46.8 0.6 add_multiply_fusion
  47.5 2.0 fusion.68
  49.5 4.8 fusion.51
  54.3 4.4 fusion.73
  58.8 36.3 %fusion.12 = f32[3,4,192,1024]{3,2,1,0:T(8,128)} fusion(f32[3,4,192,1024]{3,2,1,0:T(8,128)} %param.2, f32[3,4,192,4]{3,2,1,0:T(8,128)S(1)} %get-tuple-element.18, f32[3,4,192,4]{3,2,1,0:T(8,128)S(1)} %get-tuple-element.17), kind=kLoop, calls=%fused_computation.30 | loop fusion | flops 47185920 | bytes 18948096 | tf_op jit(solution)/shard_map/div | solution.py:53
  95.1 180.1 %all-to-all-done = f32[5,4,192,1024]{2,1,0,3:T(4,128)} async-done(((f32[5,4,192,1024]{2,1,0,3:T(4,128)}), f32[5,4,192,1024]{2,1,0,3:T(4,128)}, u32[]{:S(2)}, u32[]{:S(2)}) %all-to-all-start) | async-done | bytes 15728672 | tf_op jit(solution)/shard_map/all_to_all | solution.py:104
  275.2 30.9 %copy.32 = f32[5,4,192,2,512]{4,3,2,1,0:T(2,128)} copy(f32[5,4,192,2,512]{2,1,0,4,3:T(4,128)} %bitcast) | data formatting | bytes 31457280 | tf_op jit(solution)/shard_map/all_to_all | solution.py:104
  306.2 14.0 %copy.21 = f32[5,4,2,192,512]{4,3,2,1,0:T(8,128)} copy(f32[5,4,2,192,512]{4,2,3,1,0:T(2,128)} %bitcast.39) | data formatting | bytes 31457280 | tf_op jit(solution)/shard_map/all_to_all | solution.py:104
  320.1 54.2 %convolution_bitcast_fusion = f32[5,4,384,512]{2,3,1,0:T(8,128)} fusion(f32[5,4,384,512]{3,2,1,0:T(8,128)} %bitcast.38, f32[384,384,1,1]{1,0,3,2:T(8,128)S(1)} %fusion.73), kind=kOutput, calls=%fused_computation.48 | convolution fusion | flops 18119393280 | bytes 32047104 | tf_op jit(solution)/shard_map/ij,fkjz->fkiz/dot_general | solution.py:101
  374.4 19.4 %copy.23 = f32[5,4,384,512]{3,1,0,2:T(4,128)} copy(f32[5,4,384,512]{2,3,1,0:T(8,128)} %convolution_bitcast_fusion) | data formatting | bytes 31457280 | tf_op jit(solution)/shard_map/ij,fkjz->fkiz/transpose | solution.py:101
  393.8 9.4 %all-to-all-start.1 = ((f32[5,4,384,512]{3,1,0,2:T(4,128)}), f32[5,4,384,512]{3,1,0,2:T(4,128)}, u32[]{:S(2)}, u32[]{:S(2)}) async-start(f32[5,4,384,512]{3,1,0,2:T(4,128)} %copy.23), calls=%async_computation.1 | async-start | bytes 31457280 | tf_op jit(solution)/shard_map/all_to_all | solution.py:107
  403.3 41.9 %pad_maximum_fusion = (f32[5,8,192,1024]{3,2,1,0:T(8,128)}, f32[5,8,192,1024]{3,2,1,0:T(8,128)}) fusion(f32[5,4,192,1024]{3,2,1,0:T(8,128)} %collective-permute-done, f32[2,4,192,1024]{3,2,1,0:T(8,128)} %copy-done.2, f32[3,4,192,1024]{3,2,1,0:T(8,128)} %param.2, f32[5,4,192,1024]{3,2,1,0:T(8,128)} %collective-permute-done.1), kind=kLoop, calls=%fused_computation | loop fusion | flops 31457280 | bytes 110100480 | tf_op jit(solution)/shard_map/concatenate | solution.py:23
  445.2 46.8 %fusion.3 = f32[5,4,192,1024]{3,2,1,0:T(8,128)} fusion(f32[5,8,192,1024]{3,2,1,0:T(8,128)} %get-tuple-element.16, f32[5,8,192,1024]{3,2,1,0:T(8,128)} %get-tuple-element.15, f32[5,4,192,1024]{3,2,1,0:T(8,128)} %collective-permute-done, f32[5,4,192,1024]{3,2,1,0:T(8,128)} %collective-permute-done.1), kind=kLoop, calls=%fused_computation.12 | loop fusion | flops 47185920 | bytes 141557760 | tf_op jit(solution)/shard_map/div | solution.py:53
  492.0 13.0 %fusion.33 = f32[1,4,192,1024]{3,2,1,0:T(8,128)} fusion(f32[3,4,192,1024]{3,2,1,0:T(8,128)} %fusion.12, f32[5,4,192,1024]{3,2,1,0:T(8,128)} %fusion.3, f32[3,4,192,1024]{3,2,1,0:T(8,128)} %param.2, f32[3,4,192,1024]{3,2,1,0:T(8,128)} %param.3), kind=kLoop, calls=%fused_computation.63 | loop fusion | flops 11010048 | bytes 31457280 | tf_op jit(solution)/shard_map/sub | solution.py:74
  505.0 1.8 copy-done.1
  506.8 11.4 %fusion.36 = (f32[1,4,192,1024]{3,2,1,0:T(8,128)}, f32[1,4,192,1024]{3,2,1,0:T(8,128)}) fusion(f32[3,4,192,1024]{3,2,1,0:T(8,128)} %fusion.12, f32[5,4,192,1024]{3,2,1,0:T(8,128)S(1)} %copy-done.1, f32[3,4,192,1024]{3,2,1,0:T(8,128)} %param.2, f32[3,4,192,1024]{3,2,1,0:T(8,128)} %param.3), kind=kLoop, calls=%fused_computation.68 | loop fusion | flops 18874368 | bytes 40894464 | tf_op jit(solution)/shard_map/sub | solution.py:68
  518.2 56.4 %all-to-all-done.1 = f32[5,4,384,512]{3,1,0,2:T(4,128)} async-done(((f32[5,4,384,512]{3,1,0,2:T(4,128)}), f32[5,4,384,512]{3,1,0,2:T(4,128)}, u32[]{:S(2)}, u32[]{:S(2)}) %all-to-all-start.1) | async-done | bytes 15728672 | tf_op jit(solution)/shard_map/all_to_all | solution.py:107
  574.6 15.8 %copy.24 = f32[5,4,384,512]{3,2,1,0:T(8,128)} copy(f32[5,4,384,512]{3,1,0,2:T(4,128)} %all-to-all-done.1) | data formatting | bytes 31457280 | tf_op jit(solution)/shard_map/all_to_all | solution.py:107
  590.4 11.9 %slice_bitcast_fusion.4 = (f32[1,4,2,24,8,512]{5,4,3,2,1,0:T(8,128)}, f32[1,4,2,24,8,512]{5,4,3,2,1,0:T(8,128)}, f32[1,4,2,24,8,512]{5,4,3,2,1,0:T(8,128)}, f32[...) fusion(f32[5,4,192,2,512]{4,2,3,1,0:T(8,128)} %bitcast.37), kind=kLoop, calls=%fused_computation.53 | loop fusion | bytes 31457280
  602.3 2.4 copy.33
  604.8 2.4 copy.34
  607.9 2.0 copy.37
  609.9 1.4 slice-done.1
  611.6 8.3 %multiply_add_fusion.2 = (f32[1,4,192,1024]{3,2,1,0:T(8,128)}, f32[1,4,192,1024]{3,2,1,0:T(8,128)}, f32[1,4,192,1024]{3,2,1,0:T(8,128)}) fusion(f32[1,4,192,1024]{3,2,1,0:T(8,128)S(1)} %bitcast.41, f32[1,4,192,1024]{3,2,1,0:T(8,128)S(1)} %bitcast.40, f32[3,4,192,1024]{3,2,1,0:T(8,128)S(1)} %bitcast.36, f32[3,4,192,1024]{3,2,1,0:T(8,128)} %param.3, ...), kind=kLoop, calls=%fused_computation.72 | loop fusion | flops 11010048 | bytes 34603008 | tf_op jit(solution)/shard_map/add | solution.py:57
  619.9 11.9 %fusion.26 = f32[3,4,192,1024]{3,2,1,0:T(8,128)} fusion(f32[3,4,192,1024]{3,2,1,0:T(8,128)S(1)} %bitcast.36, f32[1,4,192,1024]{3,2,1,0:T(8,128)} %get-tuple-element.6, f32[1,4,192,1024]{3,2,1,0:T(8,128)} %fusion.33, f32[1,4,192,1024]{3,2,1,0:T(8,128)} %get-tuple-element.5, f32[1,4,192,1024]{3,2,1,0:T(8,128)} %get-tuple-element.9, ...), kind=kLoop, calls=%fused_computation.47 | loop fusion | flops 16515072 | bytes 37749504 | tf_op jit(solution)/shard_map/add | solution.py:116
  (22 shorter events, 1.0 us)
Async XLA Ops:
  0.0 5.5 copy-start
  5.5 7.4 %copy-start.2 = (f32[2,4,192,1024]{3,2,1,0:T(8,128)}, f32[2,4,192,1024]{3,2,1,0:T(8,128)S(1)}, u32[]{:S(2)}) copy-start(f32[2,4,192,1024]{3,2,1,0:T(8,128)S(1)} %slice.149) | copy-start | bytes 18874372
  12.9 390.4 %collective-permute-start = (f32[5,4,192,1024]{3,2,1,0:T(8,128)}, f32[5,4,192,1024]{3,2,1,0:T(8,128)}, u32[]{:S(2)}, u32[]{:S(2)}) collective-permute-start(f32[5,4,192,1024]{3,2,1,0:T(8,128)} %pad_maximum_fusion.1), channel_id=1, source_target_pairs={{2,0},{4,2},{6,4},{8,6},{10,8},{12,10},{14,12},{16,14},{18,16},{20... | collective-permute-start | bytes 47185928 | tf_op jit(solution)/shard_map/ppermute | solution.py:22
  13.7 389.6 %collective-permute-start.1 = (f32[5,4,192,1024]{3,2,1,0:T(8,128)}, f32[5,4,192,1024]{3,2,1,0:T(8,128)}, u32[]{:S(2)}, u32[]{:S(2)}) collective-permute-start(f32[5,4,192,1024]{3,2,1,0:T(8,128)} %pad_maximum_fusion.1), channel_id=1, source_target_pairs={{0,2},{2,4},{4,6},{6,8},{8,10},{10,12},{12,14},{14,16},{16,18},{18... | collective-permute-start | bytes 47185928 | tf_op jit(solution)/shard_map/ppermute | solution.py:21
  35.6 239.6 %all-to-all-start = ((f32[5,4,192,1024]{2,1,0,3:T(4,128)}), f32[5,4,192,1024]{2,1,0,3:T(4,128)}, u32[]{:S(2)}, u32[]{:S(2)}) async-start(f32[5,4,192,1024]{2,1,0,3:T(4,128)} %copy.19), calls=%async_computation | async-start | bytes 41943040 | tf_op jit(solution)/shard_map/all_to_all | solution.py:104
  393.8 180.8 %all-to-all-start.1 = ((f32[5,4,384,512]{3,1,0,2:T(4,128)}), f32[5,4,384,512]{3,1,0,2:T(4,128)}, u32[]{:S(2)}, u32[]{:S(2)}) async-start(f32[5,4,384,512]{3,1,0,2:T(4,128)} %copy.23), calls=%async_computation.1 | async-start | bytes 31457280 | tf_op jit(solution)/shard_map/all_to_all | solution.py:107
  492.0 14.7 %copy-start.1 = (f32[5,4,192,1024]{3,2,1,0:T(8,128)S(1)}, f32[5,4,192,1024]{3,2,1,0:T(8,128)}, u32[]{:S(2)}) copy-start(f32[5,4,192,1024]{3,2,1,0:T(8,128)} %fusion.3) | copy-start | bytes 47185924
  602.3 5.2 copy-start.4
  604.7 3.2 copy-start.3
  604.7 5.2 slice-start
  607.2 4.2 slice-start.1
  607.5 4.0 slice-start.2
  611.6 8.4 %copy-start.5 = (f32[192]{0:T(256)S(1)}, f32[192]{0:T(256)}, u32[]{:S(2)}) copy-start(f32[192]{0:T(256)} %add_multiply_fusion) | copy-start | bytes 2308
where the time goes:
time: 641 us; the launch traced here: 632 us
  waiting for transfers between devices  237 us (37%)
  other arithmetic  186 us (29%)
  local copies, waits for them, and re-layouts  133 us (21%)
  matrix products  54.2 us (8%)
  starting transfers between devices  21.4 us (3%)
    all_to_all x1, waiting for transfers between devices, shards(): lax.all_to_all(block, 'yz', split_axis=3, concat_axis=2, tiled=True)  180 us
    div x2, other arithmetic, centered(): return total / spacing  83.1 us
    all_to_all x1, waiting for transfers between devices, shards(): lax.all_to_all(derived, 'yz', split_axis=2, concat_axis=3, tiled=True)  56.4 us
    dot_general x1, matrix products, shards(): jnp.einsum('ij,fkjz->fkiz', cheb, lax.all_to_all(block, 'yz', split_axis=...  54.2 us
    all_to_all x2, local copies, waits for them, and re-layouts, shards(): lax.all_to_all(block, 'yz', split_axis=3, concat_axis=2, tiled=True)  44.9 us
    concatenate x1, other arithmetic, padded_2(): x = jnp.concatenate([before, x, after], axis=dim)  41.9 us
    concatenate x1, local copies, waits for them, and re-layouts, shards(): block = jnp.concatenate([conformation, velocity[0:2]], axis=0)  21.9 us
    transpose x1, local copies, waits for them, and re-layouts, shards(): jnp.einsum('ij,fkjz->fkiz', cheb, lax.all_to_all(block, 'yz', split_axis=...  19.4 us
  transfers between devices with their start and end apart: 4, of which 2 were waited for; matrix products, arithmetic and copies ran while one was open for 48% of the time, Pallas kernels for 0%

commit v1 on v0

v1 whole, which is shorter than its diff:
```python
import functools
import math

import jax
import jax.numpy as jnp
from jax import lax
from jax.experimental import pallas as pl
from jax.experimental.pallas import tpu as pltpu
from jax.sharding import PartitionSpec as P

stencil_coeffs = (0.8, -0.2, 4.0 / 105.0, -1.0 / 280.0)
width = 4
extensibility = 10.0
relax_rate = 1.0 / 0.04
courant = 0.5
row_block = 8
chunks = 2
vmem_bytes = 40 * 1024 * 1024


def cheb_matrix(count, points):
    last = count - 1
    half_step = math.pi / (2.0 * last)
    weights = jnp.where((points == 0) | (points == last), 2.0, 1.0).astype(jnp.float32)
    same = points[:, None] == points[None, :]
    sums = (points[:, None] + points[None, :]).astype(jnp.float32) * half_step
    diffs = (points[:, None] - points[None, :]).astype(jnp.float32) * half_step
    signs = (1 - 2 * ((points[:, None] + points[None, :]) % 2)).astype(jnp.float32)
    apart = -2.0 * jnp.sin(sums) * jnp.sin(diffs)
    safe = jnp.where(same, 1.0, apart)
    offdiag = jnp.where(same, 0.0, weights[:, None] / weights[None, :] * signs / safe)
    return offdiag - jnp.diag(jnp.sum(offdiag, axis=1))


def params():
    return pltpu.CompilerParams(vmem_limit_bytes=vmem_bytes)


def x_terms(u, c_xx, c_xy, sums):
    term_xx = 2.0 * sums[3] * c_xx - u * sums[0]
    term_xy = sums[3] * c_xy + sums[4] * c_xx - u * sums[1]
    term_yy = 2.0 * sums[4] * c_xy - u * sums[2]
    return term_xx, term_xy, term_yy


def from_after(planes, i, coeffs):
    return sum(coeffs[k - 1] * planes[i + k - width] for k in range(width - i, width + 1))


def from_before(planes, i, coeffs):
    return -sum(coeffs[k - 1] * planes[width + i - k] for k in range(i + 1, width + 1))


def inside(planes, i, coeffs):
    total = None
    for k in range(1, width):
        for at, sign in ((i + k, 1.0), (i - k, -1.0)):
            if 0 <= at < width:
                term = (sign * coeffs[k - 1]) * planes[at]
                total = term if total is None else total + term
    return total


def local_kernel(coeffs, lanes, step_ref, comp_ref, vel_ref, out_ref):
    step = step_ref[:, 0:1]
    for i in range(width):
        comp = [comp_ref[f, i] for f in range(3)]
        along_z = []
        for f in range(3):
            total = None
            for k in range(1, width + 1):
                ahead = pltpu.roll(comp[f], lanes - k, 1)
                behind = pltpu.roll(comp[f], k, 1)
                term = coeffs[k - 1] * (ahead - behind)
                total = term if total is None else total + term
            along_z.append(total)
        sums = [inside([comp_ref[f, j] for j in range(width)], i, coeffs) for f in range(3)]
        sums += [inside([vel_ref[f, j] for j in range(width)], i, coeffs) for f in range(2)]
        terms = x_terms(vel_ref[0, i], comp[0], comp[1], sums)
        peterlin = (extensibility - 2.0) / (extensibility - comp[0] - comp[2])
        rest = (1.0, 0.0, 1.0)
        w = vel_ref[2, i]
        for f in range(3):
            relax = relax_rate * (peterlin * comp[f] - rest[f])
            out_ref[f, i] = comp[f] + step * (terms[f] - w * along_z[f] - relax)


def local_part(coeffs, step, comp, vel):
    fields, planes, rows, lanes = comp.shape
    block = pl.BlockSpec((3, planes, row_block, lanes), lambda r: (0, 0, r, 0))
    return pl.pallas_call(
        functools.partial(local_kernel, coeffs, lanes),
        grid=(rows // row_block,),
        in_specs=[pl.BlockSpec((row_block, 128), lambda r: (r, 0)), block, block],
        out_specs=block,
        out_shape=jax.ShapeDtypeStruct(comp.shape, jnp.float32),
        compiler_params=params(),
        cost_estimate=pl.CostEstimate(
            flops=150 * comp.size, bytes_accessed=12 * comp.size, transcendentals=0
        ),
        name="local_part",
    )(step, comp, vel)


def wall_kernel(groups, rows, *refs):
    comp_ref, vel_ref = refs[1:3]
    received = refs[3 : 2 + groups]
    matrix_ref, acc_ref = refs[2 + groups : 4 + groups]
    out_ref = refs[4 + groups]
    back = refs[5 + groups :]
    matrix = matrix_ref[...]
    fields, slopes = [], []
    for f in range(5):
        own = comp_ref[f, 0] if f < 3 else vel_ref[f - 3, 0]
        column = jnp.concatenate([own] + [r[f, 0] for r in received], axis=0)
        high = column.astype(jnp.bfloat16)
        low = (column - high.astype(jnp.float32)).astype(jnp.bfloat16)
        stacked = jnp.concatenate([high, low, high], axis=0)
        slopes.append(jnp.dot(matrix, stacked, preferred_element_type=jnp.float32))
        fields.append(column)
    c_xy, c_yy, v = fields[1], fields[2], fields[4]
    terms = (
        2.0 * slopes[3] * c_xy - v * slopes[0],
        slopes[3] * c_yy + slopes[4] * c_xy - v * slopes[1],
        2.0 * slopes[4] * c_yy - v * slopes[2],
    )
    for f in range(3):
        out_ref[f, 0] = acc_ref[f, 0] + terms[f][0:rows]
        for g in range(1, groups):
            back[g - 1][f, 0] = terms[f][g * rows : (g + 1) * rows]


def wall_part(first, place, comp, vel, received, matrix, acc):
    groups = len(received) + 1
    rows, lanes = comp.shape[2:]
    planes = received[0].shape[1]
    columns = lanes // groups
    tile = min(columns, 256)
    tiles = columns // tile
    own = lambda p, i, s: (0, first + p, 0, s[0] * tiles + i)
    own_block = pl.BlockSpec((3, 1, rows, tile), own)
    sent = lambda p, i, s: (0, p, 0, i)
    grid_spec = pltpu.PrefetchScalarGridSpec(
        num_scalar_prefetch=1,
        grid=(planes, tiles),
        in_specs=[own_block, pl.BlockSpec((2, 1, rows, tile), own)]
        + [pl.BlockSpec((5, 1, rows, tile), sent)] * (groups - 1)
        + [pl.BlockSpec(matrix.shape, lambda p, i, s: (0, 0)), own_block],
        out_specs=[own_block] + [pl.BlockSpec((3, 1, rows, tile), sent)] * (groups - 1),
    )
    count = rows * groups
    shapes = [jax.ShapeDtypeStruct(acc.shape, jnp.float32)]
    shapes += [jax.ShapeDtypeStruct((3, planes, rows, columns), jnp.float32)] * (groups - 1)
    out = pl.pallas_call(
        functools.partial(wall_kernel, groups, rows),
        grid_spec=grid_spec,
        out_shape=shapes,
        input_output_aliases={3 + groups: 0},
        compiler_params=params(),
        cost_estimate=pl.CostEstimate(
            flops=30 * count * count * columns * planes,
            bytes_accessed=44 * count * columns * planes,
            transcendentals=0,
        ),
        name="wall_part",
    )(place, comp, vel, *received, matrix, acc)
    return out[0], out[1:]


def border_kernel(coeffs, returns, lanes, flag_ref, step_ref, comp_ref, vel_ref, received_ref, acc_ref, out_ref, *back_ref):
    tile = min(lanes, 256)

    def run(after):
        step = step_ref[:, 0:1]
        for at in range(0, lanes, tile):
            here = slice(at, at + tile)
            own = [[(comp_ref[f, i, :, here] if f < 3 else vel_ref[f - 3, i, :, here]) for i in range(width)] for f in range(5)]
            other = [[received_ref[f, i, :, here] for i in range(width)] for f in range(5)]
            to_mine, to_theirs = (from_after, from_before) if after else (from_before, from_after)
            for i in range(width):
                mine = [to_mine(other[f], i, coeffs) for f in range(5)]
                terms = x_terms(own[3][i], own[0][i], own[1][i], mine)
                for f in range(3):
                    out_ref[f, i, :, here] = acc_ref[f, i, :, here] + step * terms[f]
                if returns:
                    theirs = [to_theirs(own[f], i, coeffs) for f in range(5)]
                    returned = x_terms(other[3][i], other[0][i], other[1][i], theirs)
                    for f in range(3):
                        back_ref[0][f, i, :, here] = step * returned[f]

    pl.when(flag_ref[0] == 1)(lambda: run(True))
    pl.when(flag_ref[0] == 0)(lambda: run(False))


def border_part(returns, flags, coeffs, step, comp, vel, received, acc):
    planes, size, lanes = received.shape[1:]
    here = lambda r, s: (0, 0, s[1] + r, 0)
    block = pl.BlockSpec((3, planes, row_block, lanes), here)
    sent = lambda r, s: (0, 0, r, 0)
    grid_spec = pltpu.PrefetchScalarGridSpec(
        num_scalar_prefetch=1,
        grid=(size // row_block,),
        in_specs=[
            pl.BlockSpec((row_block, 128), lambda r, s: (s[1] + r, 0)),
            block,
            pl.BlockSpec((2, planes, row_block, lanes), here),
            pl.BlockSpec((5, planes, row_block, lanes), sent),
            block,
        ],
        out_specs=[block] + [pl.BlockSpec((3, planes, row_block, lanes), sent)] * returns,
    )
    out = pl.pallas_call(
        functools.partial(border_kernel, coeffs, returns, lanes),
        grid_spec=grid_spec,
        out_shape=[jax.ShapeDtypeStruct(acc.shape, jnp.float32)]
        + [jax.ShapeDtypeStruct((3, planes, size, lanes), jnp.float32)] * returns,
        input_output_aliases={5: 0},
        compiler_params=params(),
        cost_estimate=pl.CostEstimate(
            flops=64 * 3 * planes * size * lanes,
            bytes_accessed=4 * 19 * planes * size * lanes,
            transcendentals=0,
        ),
        name="border_part",
    )(flags, step, comp, vel, received, acc)
    return out


def add_kernel(place_ref, part_ref, acc_ref, out_ref):
    out_ref[...] = acc_ref[...] + part_ref[...]


def add_part(place, part, acc, block, grid, part_at, acc_at, name):
    grid_spec = pltpu.PrefetchScalarGridSpec(
        num_scalar_prefetch=1,
        grid=grid,
        in_specs=[pl.BlockSpec(block, part_at), pl.BlockSpec(block, acc_at)],
        out_specs=pl.BlockSpec(block, acc_at),
    )
    return pl.pallas_call(
        add_kernel,
        grid_spec=grid_spec,
        out_shape=jax.ShapeDtypeStruct(acc.shape, jnp.float32),
        input_output_aliases={2: 0},
        compiler_params=params(),
        cost_estimate=pl.CostEstimate(flops=part.size, bytes_accessed=12 * part.size, transcendentals=0),
        name=name,
    )(place, part, acc)


def add_wall(first, place, part, acc):
    fields, planes, rows, columns = part.shape
    block = (fields, 1, rows, columns)
    return add_part(
        place, part, acc, block, (planes,), lambda p, s: (0, p, 0, 0), lambda p, s: (0, first + p, 0, s[0]), "add_wall"
    )


def add_border(place, part, acc):
    fields, planes, size, lanes = part.shape
    block = (fields, planes, row_block, lanes)
    return add_part(
        place, part, acc, block, (size // row_block,), lambda r, s: (0, 0, r, 0), lambda r, s: (0, 0, s[0] + r, 0), "add_border"
    )


def shares(total, unit, parts):
    units = total // unit
    sizes = [unit * (units // parts + (k < units % parts)) for k in range(parts)]
    starts = [sum(sizes[:k]) for k in range(parts)]
    return [(at, size) for at, size in zip(starts, sizes) if size]


def shards(conformation, velocity):
    planes, rows, lanes = conformation.shape[1:]
    groups, slabs = lax.axis_size("yz"), lax.axis_size("gx")
    me, slab = lax.axis_index("yz"), lax.axis_index("gx")
    odd = (slab % 2).astype(jnp.int32)
    count = rows * groups
    columns = lanes // groups
    spacing = math.pi / (count - 1)
    coeffs = tuple(c / spacing for c in stencil_coeffs)
    half = rows // 2
    wall_cuts = shares(planes, 1, chunks)
    border_cuts = shares(half, row_block, chunks)
    near = [(i, i ^ 1) for i in range(slabs)]
    far = [(i, (i + 1 if i % 2 else i - 1) % slabs) for i in range(slabs)]

    def along_yz(x, by):
        return lax.ppermute(x, "yz", [(i, (i + by) % groups) for i in range(groups)])

    def cut(plane, n_planes, row, n_rows, lane, n_lanes):
        at = (0, plane, row, lane)
        return jnp.concatenate(
            [
                lax.dynamic_slice(conformation, at, (3, n_planes, n_rows, n_lanes)),
                lax.dynamic_slice(velocity, at, (2, n_planes, n_rows, n_lanes)),
            ],
            axis=0,
        )

    walls, borders = [], []
    for (plane, n_planes), (row, n_rows) in zip(wall_cuts, border_cuts):
        pieces = [None] * groups
        for g in range(1, groups):
            piece = cut(plane, n_planes, 0, rows, (me + g) % groups * columns, columns)
            pieces[groups - g] = along_yz(piece, g)
        walls.append(pieces[1:])
        piece = cut(0, planes, odd * half + row, n_rows, 0, lanes)
        borders.append(lax.ppermute(piece, "gx", far))
    beside = lax.ppermute(cut(0, planes, 0, rows, 0, lanes), "gx", near)

    index = jnp.arange(count, dtype=jnp.int32)
    points = index % rows * groups + (index // rows + me) % groups
    theta = math.pi * points.astype(jnp.float32) / (count - 1)
    step_size = courant * spacing * (jnp.sin(theta) + spacing)
    cheb = step_size[:, None] * cheb_matrix(count, points)
    high = lax.reduce_precision(cheb, 8, 7)
    low = lax.reduce_precision(cheb - high, 8, 7)
    matrix = jnp.concatenate([high, high, low], axis=1).astype(jnp.bfloat16)
    step = jnp.broadcast_to(step_size[:rows, None], (rows, 128))

    acc = local_part(coeffs, step, conformation, velocity)
    near_flags = jnp.stack([1 - odd, jnp.zeros_like(odd)])
    (acc,) = border_part(False, near_flags, coeffs, step, conformation, velocity, beside, acc)
    place = me.astype(jnp.int32).reshape(1)
    wall_back, border_back = [], []
    for k, ((plane, _), (row, _)) in enumerate(zip(wall_cuts, border_cuts)):
        acc, back = wall_part(plane, place, conformation, velocity, walls[k], matrix, acc)
        wall_back.append([along_yz(b, g) for g, b in enumerate(back, 1)])
        far_flags = jnp.stack([odd, ((1 - odd) * half + row) // row_block])
        acc, back = border_part(True, far_flags, coeffs, step, conformation, velocity, borders[k], acc)
        border_back.append(lax.ppermute(back, "gx", far))
    for k, ((plane, _), (row, _)) in enumerate(zip(wall_cuts, border_cuts)):
        for g, part in enumerate(wall_back[k], 1):
            source = ((me - g) % groups).astype(jnp.int32).reshape(1)
            acc = add_wall(plane, source, part, acc)
        acc = add_border(((odd * half + row) // row_block).reshape(1), border_back[k], acc)
    return acc


def solution(mesh):
    in_specs = (P(None, "gx", "yz", None), P(None, "gx", "yz", None))
    out_specs = P(None, "gx", "yz", None)
    return jax.shard_map(shards, mesh=mesh, in_specs=in_specs, out_specs=out_specs, check_vma=False)
```

time: 641 us -> 310 us (0.48)
  the two profiles are of different devices: /device:TPU:16 before, /device:TPU:1 now
where the time goes in v1:
time: 310 us; the launch traced here: 308 us
  waiting for transfers between devices  151 us (49%)
  Pallas kernels  103 us (33%)
  other arithmetic  25.3 us (8%)
  local copies, waits for them, and re-layouts  20.5 us (7%)
  starting transfers between devices  8.37 us (3%)
    ppermute x2, waiting for transfers between devices, shards(): borders.append(lax.ppermute(piece, 'gx', far))  113 us
    pallas_call x3, Pallas kernels, border_part(): pl.pallas_call(functools.partial(border_kernel, coeffs, returns, lanes),...  39.6 us
    pallas_call x1, Pallas kernels, local_part(): pl.pallas_call(functools.partial(local_kernel, coeffs, lanes), grid=(rows...  26.5 us
    pallas_call x2, Pallas kernels, wall_part(): pl.pallas_call(functools.partial(wall_kernel, groups, rows), grid_spec=gr...  20 us
    ppermute x4, waiting for transfers between devices, along_yz(): lax.ppermute(x, 'yz', [(i, (i + by) % groups) for i in range(groups)])  19.2 us
    ppermute x2, waiting for transfers between devices, shards(): border_back.append(lax.ppermute(back, 'gx', far))  18.4 us
    pallas_call x4, Pallas kernels, add_part(): pl.pallas_call(add_kernel, grid_spec=grid_spec, out_shape=jax.ShapeDtypeS...  17.1 us
    concatenate x5, other arithmetic, cut(): jnp.concatenate([lax.dynamic_slice(conformation, at, (3, n_planes, n_rows...  15.1 us
  transfers between devices with their start and end apart: 9, of which 6 were waited for; matrix products, arithmetic and copies ran while one was open for 10% of the time, Pallas kernels for 32%

profile of v1, /device:TPU:1, one launch (start us, length us, event | category | flops | bytes accessed | tf_op | source)
XLA Modules:
  0.0 308.2 jit_solution(8174194905287378685)
XLA Ops:
  0.0 3.5 %dynamic_slice.35 = f32[2,4,192,1024]{3,2,1,0:T(8,128)S(1)} slice(f32[3,4,192,1024]{3,2,1,0:T(8,128)} %vel_ref.7), slice={[0:2], [0:4], [0:192], [0:1024]} | slice | bytes 12582912 | tf_op jit(solution)/shard_map/dynamic_slice | solution.py:297
  3.5 2.0 copy-done
  5.5 5.8 %pad_maximum_fusion = f32[5,4,192,1024]{3,2,1,0:T(8,128)} fusion(f32[2,4,192,1024]{3,2,1,0:T(8,128)S(1)} %dynamic_slice.35, f32[3,4,192,1024]{3,2,1,0:T(8,128)S(1)} %copy-done), kind=kLoop, calls=%fused_computation | loop fusion | flops 3932160 | bytes 31457280 | tf_op jit(solution)/shard_map/concatenate | solution.py:294
  11.3 3.4 %constant_dynamic-slice_fusion = (f32[2,2,192,512]{3,2,1,0:T(8,128)S(1)}, f32[2,2,192,512]{3,2,1,0:T(8,128)}) fusion(f32[3,4,192,1024]{3,2,1,0:T(8,128)} %vel_ref.7, s32[]{:T(128)S(6)} %select_n.150), kind=kLoop, calls=%fused_computation.47 | loop fusion | bytes 6291460 | tf_op jit(solution)/shard_map/dynamic_slice | solution.py:297
  14.7 3.0 constant_dynamic-slice_fusion.1
  17.7 2.3 pad_maximum_fusion.4
  20.1 2.7 collective-permute-start.3
  22.8 2.8 constant_dynamic-slice_fusion.3
  25.5 2.1 constant_dynamic-slice_fusion.2
  27.6 2.2 pad_maximum_fusion.3
  29.8 1.4 collective-permute-start.2
  31.2 2.7 pad_maximum_fusion.2
  34.1 2.2 pad_maximum_fusion.1
  36.9 3.7 %copy-done.1 = f32[3,4,192,1024]{3,2,1,0:T(8,128)S(1)} copy-done((f32[3,4,192,1024]{3,2,1,0:T(8,128)S(1)}, f32[3,4,192,1024]{3,2,1,0:T(8,128)}, u32[]{:S(2)}) %copy-start.1) | copy-done | bytes 9437208
  40.6 26.5 %local_part.1.acc_ref = f32[3,4,192,1024]{3,2,1,0:T(8,128)} custom-call(f32[192,128]{1,0:T(8,128)S(1)} %broadcast_in_dim.48.step_ref, f32[3,4,192,1024]{3,2,1,0:T(8,128)S(1)} %copy-done.1, f32[3,4,192,1024]{3,2,1,0:T(8,128)} %vel_ref.7), custom_call_target="tpu_custom_call" | custom-call | flops 353894400 | bytes 28311552 | tf_op jit(solution)/shard_map/local_part/pallas_call | solution.py:91
  67.4 4.8 %fusion.11 = f32[384]{0:T(512)S(1)} fusion(f32[384]{0:T(512)S(1)} %get-tuple-element.32, s32[384]{0:T(512)S(1)} %fusion.14), kind=kLoop, calls=%fused_computation.30 | loop fusion | flops 4275840 | bytes 4608 | tf_op jit(solution)/shard_map/reduce_sum | solution.py:32
  72.2 5.0 %reduce-precision_convert_fusion = (bf16[384,384]{1,0:T(8,128)(2,1)S(1)}, bf16[384,384]{1,0:T(8,128)(2,1)S(1)}) fusion(f32[384]{0:T(512)S(1)} %fusion.11, f32[384]{0:T(512)S(1)} %get-tuple-element.31, f32[384]{0:T(512)S(1)} %get-tuple-element.32, s32[384]{0:T(512)S(1)} %fusion.14), kind=kLoop, calls=%fused_computation.13 | loop fusion | flops 5455872 | bytes 595968 | tf_op jit(solution)/shard_map/convert
  77.3 22.6 %border_part.3.refs_5_ = f32[3,4,192,1024]{3,2,1,0:T(8,128)} custom-call(s32[2]{0:T(128)S(1)} %pad_add_fusion.2.flag_ref, f32[192,128]{1,0:T(8,128)S(1)} %broadcast_in_dim.48.step_ref, f32[3,4,192,1024]{3,2,1,0:T(8,128)S(1)} %copy-done.1, f32[3,4,192,1024]{3,2,1,0:T(8,128)} %vel_ref.7, ...), custom_call_target="tpu_custom_call", output_to_operand_aliasing={{}: (5, {})} | custom-call | flops 150994944 | bytes 59768832 | tf_op jit(solution)/shard_map/border_part/pallas_call | solution.py:212
  99.8 8.5 %collective-permute-done.3.refs_3_ = f32[5,2,192,512]{3,2,1,0:T(8,128)} collective-permute-done((f32[5,2,192,512]{3,2,1,0:T(8,128)}, f32[5,2,192,512]{3,2,1,0:T(8,128)}, u32[]{:S(2)}, u32[]{:S(2)}) %collective-permute-start.3) | collective-permute-done | bytes 3932192 | tf_op jit(solution)/shard_map/ppermute | solution.py:290
  108.4 9.9 %wall_part.2 = (f32[3,4,192,1024]{3,2,1,0:T(8,128)}, f32[3,2,192,512]{3,2,1,0:T(8,128)}) custom-call(s32[1]{0:T(128)} %bitcast.3.refs_0_, f32[3,4,192,1024]{3,2,1,0:T(8,128)} %comp_ref.7, f32[3,4,192,1024]{3,2,1,0:T(8,128)} %vel_ref.7, f32[5,2,192,512]{3,2,1,0:T(8,128)} %collective-permute-done.3.refs_3_, ...), custom_call_target="tpu_custom_call", output_to_operand_aliasing={{0}: (5, {})} | custom-call | flops 4529848320 | bytes 17301504 | tf_op jit(solution)/shard_map/wall_part/pallas_call | solution.py:154
  119.6 65.6 %collective-permute-done.2.received_ref = f32[5,4,48,1024]{3,2,1,0:T(8,128)} collective-permute-done((f32[5,4,48,1024]{3,2,1,0:T(8,128)}, f32[5,4,48,1024]{3,2,1,0:T(8,128)}, u32[]{:S(2)}, u32[]{:S(2)}) %collective-permute-start.2) | collective-permute-done | bytes 3932192 | tf_op jit(solution)/shard_map/ppermute | solution.py:310
  185.1 8.5 %border_part.4 = (f32[3,4,192,1024]{3,2,1,0:T(8,128)}, f32[3,4,48,1024]{3,2,1,0:T(8,128)}) custom-call(s32[2]{0:T(128)S(1)} %pad_add_fusion.1.flag_ref, f32[192,128]{1,0:T(8,128)S(1)} %broadcast_in_dim.48.step_ref, f32[3,4,192,1024]{3,2,1,0:T(8,128)} %comp_ref.7, f32[3,4,192,1024]{3,2,1,0:T(8,128)} %vel_ref.7, ...), custom_call_target="tpu_custom_call", output_to_operand_aliasing={{0}: (5, {})} | custom-call | flops 37748736 | bytes 14942208 | tf_op jit(solution)/shard_map/border_part/pallas_call | solution.py:212
  194.7 10.1 %wall_part.3 = (f32[3,4,192,1024]{3,2,1,0:T(8,128)}, f32[3,2,192,512]{3,2,1,0:T(8,128)}) custom-call(s32[1]{0:T(128)} %bitcast.3.refs_0_, f32[3,4,192,1024]{3,2,1,0:T(8,128)} %comp_ref.7, f32[3,4,192,1024]{3,2,1,0:T(8,128)} %vel_ref.7, f32[5,2,192,512]{3,2,1,0:T(8,128)} %collective-permute-done.1.refs_3_, ...), custom_call_target="tpu_custom_call", output_to_operand_aliasing={{0}: (5, {})} | custom-call | flops 4529848320 | bytes 17301504 | tf_op jit(solution)/shard_map/wall_part/pallas_call | solution.py:154
  205.0 47.5 %collective-permute-done.received_ref = f32[5,4,48,1024]{3,2,1,0:T(8,128)} collective-permute-done((f32[5,4,48,1024]{3,2,1,0:T(8,128)}, f32[5,4,48,1024]{3,2,1,0:T(8,128)}, u32[]{:S(2)}, u32[]{:S(2)}) %collective-permute-start) | collective-permute-done | bytes 3932192 | tf_op jit(solution)/shard_map/ppermute | solution.py:310
  252.5 8.5 %border_part.5 = (f32[3,4,192,1024]{3,2,1,0:T(8,128)}, f32[3,4,48,1024]{3,2,1,0:T(8,128)}) custom-call(s32[2]{0:T(128)S(1)} %pad_add_fusion.flag_ref, f32[192,128]{1,0:T(8,128)S(1)} %broadcast_in_dim.48.step_ref, f32[3,4,192,1024]{3,2,1,0:T(8,128)} %comp_ref.7, f32[3,4,192,1024]{3,2,1,0:T(8,128)} %vel_ref.7, ...), custom_call_target="tpu_custom_call", output_to_operand_aliasing={{0}: (5, {})} | custom-call | flops 37748736 | bytes 14942208 | tf_op jit(solution)/shard_map/border_part/pallas_call | solution.py:212
  262.1 2.9 add_wall.2.acc_ref
  265.0 12.8 %collective-permute-done.7.part_ref = f32[3,4,48,1024]{3,2,1,0:T(8,128)} collective-permute-done((f32[3,4,48,1024]{3,2,1,0:T(8,128)}, f32[3,4,48,1024]{3,2,1,0:T(8,128)}, u32[]{:S(2)}, u32[]{:S(2)}) %collective-permute-start.7) | collective-permute-done | bytes 2359328 | tf_op jit(solution)/shard_map/ppermute | solution.py:333
  277.8 5.4 %add_border.2.acc_ref = f32[3,4,192,1024]{3,2,1,0:T(8,128)} custom-call(s32[1]{0:T(128)} %bitcast.7.place_ref, f32[3,4,48,1024]{3,2,1,0:T(8,128)} %collective-permute-done.7.part_ref, f32[3,4,192,1024]{3,2,1,0:T(8,128)} %add_wall.2.acc_ref), custom_call_target="tpu_custom_call", output_to_operand_aliasing={{}: (2, {})} | custom-call | flops 589824 | bytes 7077888 | tf_op jit(solution)/shard_map/add_border/pallas_call | solution.py:240
  283.2 10.6 %collective-permute-done.6.part_ref = f32[3,2,192,512]{3,2,1,0:T(8,128)} collective-permute-done((f32[3,2,192,512]{3,2,1,0:T(8,128)}, f32[3,2,192,512]{3,2,1,0:T(8,128)}, u32[]{:S(2)}, u32[]{:S(2)}) %collective-permute-start.6) | collective-permute-done | bytes 2359328 | tf_op jit(solution)/shard_map/ppermute | solution.py:290
  293.8 3.5 %add_wall.3.acc_ref = f32[3,4,192,1024]{3,2,1,0:T(8,128)} custom-call(s32[1]{0:T(128)} %bitcast.6.place_ref, f32[3,2,192,512]{3,2,1,0:T(8,128)} %collective-permute-done.6.part_ref, f32[3,4,192,1024]{3,2,1,0:T(8,128)} %add_border.2.acc_ref), custom_call_target="tpu_custom_call", output_to_operand_aliasing={{}: (2, {})} | custom-call | flops 589824 | bytes 7077888 | tf_op jit(solution)/shard_map/add_wall/pallas_call | solution.py:240
  297.3 5.5 %collective-permute-done.5.part_ref = f32[3,4,48,1024]{3,2,1,0:T(8,128)} collective-permute-done((f32[3,4,48,1024]{3,2,1,0:T(8,128)}, f32[3,4,48,1024]{3,2,1,0:T(8,128)}, u32[]{:S(2)}, u32[]{:S(2)}) %collective-permute-start.5) | collective-permute-done | bytes 2359328 | tf_op jit(solution)/shard_map/ppermute | solution.py:333
  302.8 5.4 %add_border.3 = f32[3,4,192,1024]{3,2,1,0:T(8,128)} custom-call(s32[1]{0:T(128)} %bitcast.place_ref, f32[3,4,48,1024]{3,2,1,0:T(8,128)} %collective-permute-done.5.part_ref, f32[3,4,192,1024]{3,2,1,0:T(8,128)} %add_wall.3.acc_ref), custom_call_target="tpu_custom_call", output_to_operand_aliasing={{}: (2, {})} | custom-call | flops 589824 | bytes 7077888 | tf_op jit(solution)/shard_map/add_border/pallas_call | solution.py:240
  (22 shorter events, 4.8 us)
Async XLA Ops:
  0.0 5.5 %copy-start = (f32[3,4,192,1024]{3,2,1,0:T(8,128)S(1)}, f32[3,4,192,1024]{3,2,1,0:T(8,128)}, u32[]{:S(2)}) copy-start(f32[3,4,192,1024]{3,2,1,0:T(8,128)} %comp_ref.7) | copy-start | bytes 28311556
  11.3 66.0 %collective-permute-start.4 = (f32[5,4,192,1024]{3,2,1,0:T(8,128)}, f32[5,4,192,1024]{3,2,1,0:T(8,128)}, u32[]{:S(2)}, u32[]{:S(2)}) collective-permute-start(f32[5,4,192,1024]{3,2,1,0:T(8,128)} %pad_maximum_fusion), channel_id=1, source_target_pairs={{0,2},{2,0},{4,6},{6,4},{8,10},{10,8},{12,14},{14,12},{16,18},{18,... | collective-permute-start | bytes 47185928 | tf_op jit(solution)/shard_map/ppermute | solution.py:311
  20.1 88.3 %collective-permute-start.3 = (f32[5,2,192,512]{3,2,1,0:T(8,128)}, f32[5,2,192,512]{3,2,1,0:T(8,128)}, u32[]{:S(2)}, u32[]{:S(2)}) collective-permute-start(f32[5,2,192,512]{3,2,1,0:T(8,128)} %pad_maximum_fusion.4), channel_id=1, source_target_pairs={{0,1},{1,0},{2,3},{3,2},{4,5},{5,4},{6,7},{7,6},{8,9},{9,8},{10,11... | collective-permute-start | bytes 11796488 | tf_op jit(solution)/shard_map/ppermute | solution.py:290
  27.6 3.6 %copy-start.2 = (f32[2,2,192,512]{3,2,1,0:T(8,128)S(1)}, f32[2,2,192,512]{3,2,1,0:T(8,128)}, u32[]{:S(2)}) copy-start(f32[2,2,192,512]{3,2,1,0:T(8,128)} %get-tuple-element.24) | copy-start | bytes 4718596
  29.8 155.3 %collective-permute-start.2 = (f32[5,4,48,1024]{3,2,1,0:T(8,128)}, f32[5,4,48,1024]{3,2,1,0:T(8,128)}, u32[]{:S(2)}, u32[]{:S(2)}) collective-permute-start(f32[5,4,48,1024]{3,2,1,0:T(8,128)} %pad_maximum_fusion.3), channel_id=1, source_target_pairs={{0,30},{2,4},{4,2},{6,8},{8,6},{10,12},{12,10},{14,16},{16,14},{18... | collective-permute-start | bytes 11796488 | tf_op jit(solution)/shard_map/ppermute | solution.py:310
  33.9 160.8 %collective-permute-start.1 = (f32[5,2,192,512]{3,2,1,0:T(8,128)}, f32[5,2,192,512]{3,2,1,0:T(8,128)}, u32[]{:S(2)}, u32[]{:S(2)}) collective-permute-start(f32[5,2,192,512]{3,2,1,0:T(8,128)} %pad_maximum_fusion.2), channel_id=1, source_target_pairs={{0,1},{1,0},{2,3},{3,2},{4,5},{5,4},{6,7},{7,6},{8,9},{9,8},{10,11... | collective-permute-start | bytes 11796488 | tf_op jit(solution)/shard_map/ppermute | solution.py:290
  36.3 216.3 %collective-permute-start = (f32[5,4,48,1024]{3,2,1,0:T(8,128)}, f32[5,4,48,1024]{3,2,1,0:T(8,128)}, u32[]{:S(2)}, u32[]{:S(2)}) collective-permute-start(f32[5,4,48,1024]{3,2,1,0:T(8,128)} %pad_maximum_fusion.1), channel_id=1, source_target_pairs={{0,30},{2,4},{4,2},{6,8},{8,6},{10,12},{12,10},{14,16},{16,14},{18... | collective-permute-start | bytes 11796488 | tf_op jit(solution)/shard_map/ppermute | solution.py:310
  36.9 3.7 %copy-start.1 = (f32[3,4,192,1024]{3,2,1,0:T(8,128)S(1)}, f32[3,4,192,1024]{3,2,1,0:T(8,128)}, u32[]{:S(2)}) copy-start(f32[3,4,192,1024]{3,2,1,0:T(8,128)} %comp_ref.7) | copy-start | bytes 28311556
  118.3 143.8 %collective-permute-start.8 = (f32[3,2,192,512]{3,2,1,0:T(8,128)}, f32[3,2,192,512]{3,2,1,0:T(8,128)S(1)}, u32[]{:S(2)}, u32[]{:S(2)}) collective-permute-start(f32[3,2,192,512]{3,2,1,0:T(8,128)} %get-tuple-element.19), channel_id=1, source_target_pairs={{0,1},{1,0},{2,3},{3,2},{4,5},{5,4},{6,7},{7,6},{8,9},{9,8},{10,11... | collective-permute-start | bytes 7077896 | tf_op jit(solution)/shard_map/ppermute | solution.py:290
  193.6 84.2 %collective-permute-start.7 = (f32[3,4,48,1024]{3,2,1,0:T(8,128)}, f32[3,4,48,1024]{3,2,1,0:T(8,128)}, u32[]{:S(2)}, u32[]{:S(2)}) collective-permute-start(f32[3,4,48,1024]{3,2,1,0:T(8,128)} %get-tuple-element.18), channel_id=1, source_target_pairs={{0,30},{2,4},{4,2},{6,8},{8,6},{10,12},{12,10},{14,16},{16,14},{18... | collective-permute-start | bytes 7077896 | tf_op jit(solution)/shard_map/ppermute | solution.py:333
  204.8 89.0 %collective-permute-start.6 = (f32[3,2,192,512]{3,2,1,0:T(8,128)}, f32[3,2,192,512]{3,2,1,0:T(8,128)}, u32[]{:S(2)}, u32[]{:S(2)}) collective-permute-start(f32[3,2,192,512]{3,2,1,0:T(8,128)} %get-tuple-element.17), channel_id=1, source_target_pairs={{0,1},{1,0},{2,3},{3,2},{4,5},{5,4},{6,7},{7,6},{8,9},{9,8},{10,11... | collective-permute-start | bytes 7077896 | tf_op jit(solution)/shard_map/ppermute | solution.py:290
  261.0 41.8 %collective-permute-start.5 = (f32[3,4,48,1024]{3,2,1,0:T(8,128)}, f32[3,4,48,1024]{3,2,1,0:T(8,128)}, u32[]{:S(2)}, u32[]{:S(2)}) collective-permute-start(f32[3,4,48,1024]{3,2,1,0:T(8,128)} %get-tuple-element.16), channel_id=1, source_target_pairs={{0,30},{2,4},{4,2},{6,8},{8,6},{10,12},{12,10},{14,16},{16,14},{18... | collective-permute-start | bytes 7077896 | tf_op jit(solution)/shard_map/ppermute | solution.py:333

commit v2 on v1

--- a/solution.py
+++ b/solution.py
@@ -14,8 +14,9 @@
 relax_rate = 1.0 / 0.04
 courant = 0.5
 row_block = 8
-chunks = 2
-vmem_bytes = 40 * 1024 * 1024
+wall_weights = (1, 1)
+border_weights = (1, 1)
+vmem_bytes = 56 * 1024 * 1024
 
 
 def cheb_matrix(count, points):
@@ -30,6 +31,9 @@
     safe = jnp.where(same, 1.0, apart)
     offdiag = jnp.where(same, 0.0, weights[:, None] / weights[None, :] * signs / safe)
     return offdiag - jnp.diag(jnp.sum(offdiag, axis=1))
+
+
+small = pl.CostEstimate(flops=1024, bytes_accessed=1024, transcendentals=0)
 
 
 def params():
@@ -95,11 +99,48 @@
         out_specs=block,
         out_shape=jax.ShapeDtypeStruct(comp.shape, jnp.float32),
         compiler_params=params(),
-        cost_estimate=pl.CostEstimate(
-            flops=150 * comp.size, bytes_accessed=12 * comp.size, transcendentals=0
-        ),
+        cost_estimate=small,
         name="local_part",
     )(step, comp, vel)
+
+
+def pack_kernel(place_ref, comp_ref, vel_ref, out_ref):
+    out_ref[0:3] = comp_ref[...]
+    out_ref[3:5] = vel_ref[...]
+
+
+def pack(place, block, grid, source_at, sent_at, comp, vel, name):
+    planes, rows, lanes = block
+    shape = (5, grid[0] * planes, grid[1] * rows, grid[2] * lanes)
+    grid_spec = pltpu.PrefetchScalarGridSpec(
+        num_scalar_prefetch=1,
+        grid=grid,
+        in_specs=[pl.BlockSpec((3, *block), source_at), pl.BlockSpec((2, *block), source_at)],
+        out_specs=pl.BlockSpec((5, *block), sent_at),
+    )
+    return pl.pallas_call(
+        pack_kernel,
+        grid_spec=grid_spec,
+        out_shape=jax.ShapeDtypeStruct(shape, jnp.float32),
+        compiler_params=params(),
+        cost_estimate=small,
+        name=name,
+    )(place, comp, vel)
+
+
+def pack_wall(first, planes, columns, place, comp, vel):
+    rows = comp.shape[2]
+    tile = min(columns, 256)
+    tiles = columns // tile
+    source_at = lambda p, r, i, s: (0, first + p, 0, s[0] * tiles + i)
+    return pack(place, (1, rows, tile), (planes, 1, tiles), source_at, lambda p, r, i, s: (0, p, 0, i), comp, vel, "pack_wall")
+
+
+def pack_border(row, size, half, place, comp, vel):
+    planes, rows, lanes = comp.shape[1:]
+    tall = math.gcd(2 * row_block, math.gcd(half, math.gcd(row, size)))
+    source_at = lambda p, r, i, s: (0, 0, s[0] * (half // tall) + row // tall + r, 0)
+    return pack(place, (planes, tall, lanes), (1, size // tall, 1), source_at, lambda p, r, i, s: (0, 0, r, 0), comp, vel, "pack_border")
 
 
 def wall_kernel(groups, rows, *refs):
@@ -157,17 +198,14 @@
         out_shape=shapes,
         input_output_aliases={3 + groups: 0},
         compiler_params=params(),
-        cost_estimate=pl.CostEstimate(
-            flops=30 * count * count * columns * planes,
-            bytes_accessed=44 * count * columns * planes,
-            transcendentals=0,
-        ),
+        cost_estimate=small,
         name="wall_part",
     )(place, comp, vel, *received, matrix, acc)
     return out[0], out[1:]
 
 
-def border_kernel(coeffs, returns, lanes, flag_ref, step_ref, comp_ref, vel_ref, received_ref, acc_ref, out_ref, *back_ref):
+def border_kernel(coeffs, returns, lanes, flag_ref, step_ref, comp_ref, vel_ref, *refs):
+    received, acc_ref, out_ref, back_ref = (refs[:1], *refs[1:]) if returns else (refs[:2], *refs[2:], None)
     tile = min(lanes, 256)
 
     def run(after):
@@ -175,7 +213,8 @@
         for at in range(0, lanes, tile):
             here = slice(at, at + tile)
             own = [[(comp_ref[f, i, :, here] if f < 3 else vel_ref[f - 3, i, :, here]) for i in range(width)] for f in range(5)]
-            other = [[received_ref[f, i, :, here] for i in range(width)] for f in range(5)]
+            fields = [(received[0], f) for f in range(5)] if returns else [(received[f // 3], f % 3) for f in range(5)]
+            other = [[r[f, i, :, here] for i in range(width)] for r, f in fields]
             to_mine, to_theirs = (from_after, from_before) if after else (from_before, from_after)
             for i in range(width):
                 mine = [to_mine(other[f], i, coeffs) for f in range(5)]
@@ -186,14 +225,14 @@
                     theirs = [to_theirs(own[f], i, coeffs) for f in range(5)]
                     returned = x_terms(other[3][i], other[0][i], other[1][i], theirs)
                     for f in range(3):
-                        back_ref[0][f, i, :, here] = step * returned[f]
+                        back_ref[f, i, :, here] = step * returned[f]
 
     pl.when(flag_ref[0] == 1)(lambda: run(True))
     pl.when(flag_ref[0] == 0)(lambda: run(False))
 
 
 def border_part(returns, flags, coeffs, step, comp, vel, received, acc):
-    planes, size, lanes = received.shape[1:]
+    planes, size, lanes = received[0].shape[1:]
     here = lambda r, s: (0, 0, s[1] + r, 0)
     block = pl.BlockSpec((3, planes, row_block, lanes), here)
     sent = lambda r, s: (0, 0, r, 0)
@@ -204,7 +243,7 @@
             pl.BlockSpec((row_block, 128), lambda r, s: (s[1] + r, 0)),
             block,
             pl.BlockSpec((2, planes, row_block, lanes), here),
-            pl.BlockSpec((5, planes, row_block, lanes), sent),
+            *(pl.BlockSpec((min(x.shape[0], 5 - at), planes, row_block, lanes), sent) for at, x in zip((0, 3), received)),
             block,
         ],
         out_specs=[block] + [pl.BlockSpec((3, planes, row_block, lanes), sent)] * returns,
@@ -214,15 +253,11 @@
         grid_spec=grid_spec,
         out_shape=[jax.ShapeDtypeStruct(acc.shape, jnp.float32)]
         + [jax.ShapeDtypeStruct((3, planes, size, lanes), jnp.float32)] * returns,
-        input_output_aliases={5: 0},
-        compiler_params=params(),
-        cost_estimate=pl.CostEstimate(
-            flops=64 * 3 * planes * size * lanes,
-            bytes_accessed=4 * 19 * planes * size * lanes,
-            transcendentals=0,
-        ),
+        input_output_aliases={4 + len(received): 0},
+        compiler_params=params(),
+        cost_estimate=small,
         name="border_part",
-    )(flags, step, comp, vel, received, acc)
+    )(flags, step, comp, vel, *received, acc)
     return out
 
 
@@ -243,7 +278,7 @@
         out_shape=jax.ShapeDtypeStruct(acc.shape, jnp.float32),
         input_output_aliases={2: 0},
         compiler_params=params(),
-        cost_estimate=pl.CostEstimate(flops=part.size, bytes_accessed=12 * part.size, transcendentals=0),
+        cost_estimate=small,
         name=name,
     )(place, part, acc)
 
@@ -256,19 +291,18 @@
     )
 
 
-def add_border(place, part, acc):
+def add_border(row, half, place, part, acc):
     fields, planes, size, lanes = part.shape
-    block = (fields, planes, row_block, lanes)
-    return add_part(
-        place, part, acc, block, (size // row_block,), lambda r, s: (0, 0, r, 0), lambda r, s: (0, 0, s[0] + r, 0), "add_border"
-    )
-
-
-def shares(total, unit, parts):
+    tall = math.gcd(2 * row_block, math.gcd(half, math.gcd(row, size)))
+    block = (fields, planes, tall, lanes)
+    acc_at = lambda r, s: (0, 0, s[0] * (half // tall) + row // tall + r, 0)
+    return add_part(place, part, acc, block, (size // tall,), lambda r, s: (0, 0, r, 0), acc_at, "add_border")
+
+
+def shares(total, unit, weights):
     units = total // unit
-    sizes = [unit * (units // parts + (k < units % parts)) for k in range(parts)]
-    starts = [sum(sizes[:k]) for k in range(parts)]
-    return [(at, size) for at, size in zip(starts, sizes) if size]
+    ends = [unit * round(units * sum(weights[: k + 1]) / sum(weights)) for k in range(len(weights))]
+    return list(zip([0] + ends[:-1], [b - a for a, b in zip([0] + ends[:-1], ends)]))
 
 
 def shards(conformation, velocity):
@@ -281,35 +315,25 @@
     spacing = math.pi / (count - 1)
     coeffs = tuple(c / spacing for c in stencil_coeffs)
     half = rows // 2
-    wall_cuts = shares(planes, 1, chunks)
-    border_cuts = shares(half, row_block, chunks)
+    wall_cuts = shares(planes, 1, wall_weights)
+    border_cuts = shares(half, row_block, border_weights)
     near = [(i, i ^ 1) for i in range(slabs)]
     far = [(i, (i + 1 if i % 2 else i - 1) % slabs) for i in range(slabs)]
 
     def along_yz(x, by):
         return lax.ppermute(x, "yz", [(i, (i + by) % groups) for i in range(groups)])
 
-    def cut(plane, n_planes, row, n_rows, lane, n_lanes):
-        at = (0, plane, row, lane)
-        return jnp.concatenate(
-            [
-                lax.dynamic_slice(conformation, at, (3, n_planes, n_rows, n_lanes)),
-                lax.dynamic_slice(velocity, at, (2, n_planes, n_rows, n_lanes)),
-            ],
-            axis=0,
-        )
-
+    beside = [lax.ppermute(x, "gx", near) for x in (conformation, velocity)]
     walls, borders = [], []
     for (plane, n_planes), (row, n_rows) in zip(wall_cuts, border_cuts):
         pieces = [None] * groups
         for g in range(1, groups):
-            piece = cut(plane, n_planes, 0, rows, (me + g) % groups * columns, columns)
+            place = ((me + g) % groups).astype(jnp.int32).reshape(1)
+            piece = pack_wall(plane, n_planes, columns, place, conformation, velocity)
             pieces[groups - g] = along_yz(piece, g)
         walls.append(pieces[1:])
-        piece = cut(0, planes, odd * half + row, n_rows, 0, lanes)
+        piece = pack_border(row, n_rows, half, odd.reshape(1), conformation, velocity)
         borders.append(lax.ppermute(piece, "gx", far))
-    beside = lax.ppermute(cut(0, planes, 0, rows, 0, lanes), "gx", near)
-
     index = jnp.arange(count, dtype=jnp.int32)
     points = index % rows * groups + (index // rows + me) % groups
     theta = math.pi * points.astype(jnp.float32) / (count - 1)
@@ -329,13 +353,13 @@
         acc, back = wall_part(plane, place, conformation, velocity, walls[k], matrix, acc)
         wall_back.append([along_yz(b, g) for g, b in enumerate(back, 1)])
         far_flags = jnp.stack([odd, ((1 - odd) * half + row) // row_block])
-        acc, back = border_part(True, far_flags, coeffs, step, conformation, velocity, borders[k], acc)
+        acc, back = border_part(True, far_flags, coeffs, step, conformation, velocity, [borders[k]], acc)
         border_back.append(lax.ppermute(back, "gx", far))
     for k, ((plane, _), (row, _)) in enumerate(zip(wall_cuts, border_cuts)):
         for g, part in enumerate(wall_back[k], 1):
             source = ((me - g) % groups).astype(jnp.int32).reshape(1)
             acc = add_wall(plane, source, part, acc)
-        acc = add_border(((odd * half + row) // row_block).reshape(1), border_back[k], acc)
+        acc = add_border(row, half, odd.reshape(1), border_back[k], acc)
     return acc
 
 

time: 310 us -> 292 us (0.942)
  Pallas kernels: 103 us -> 126 us
  local copies, waits for them, and re-layouts: 20.5 us -> 2.18 us
  other arithmetic: 25.3 us -> 12.8 us
  waiting for transfers between devices: 151 us -> 139 us
    pallas_call x0 -> x4, Pallas kernels: none -> 19 us  [pack(): pl.pallas_call(pack_kernel, grid_spec=grid_spec, out_shape=jax.ShapeDtype...]
    concatenate x5 -> x0, other arithmetic: 15.1 us -> none  [cut(): jnp.concatenate([lax.dynamic_slice(conformation, at, (3, n_planes, n_rows...]
    dynamic_slice x5 -> x0, local copies, waits for them, and re-layouts: 14.8 us -> none  [the longest x3 9.04 us: cut(): lax.dynamic_slice(velocity, at, (2, n_planes, n_rows, n_lanes))]
    ppermute x4, waiting for transfers between devices: 19.2 us -> 14.5 us  [along_yz(): lax.ppermute(x, 'yz', [(i, (i + by) % groups) for i in range(groups)])]
    unnamed x6 -> x2, local copies, waits for them, and re-layouts: 5.64 us -> 1.43 us
    ppermute x2, waiting for transfers between devices: 18.4 us -> 14.2 us  [shards(): border_back.append(lax.ppermute(back, 'gx', far))]
    pallas_call x3, Pallas kernels: 39.6 us -> 42.7 us  [border_part(): pl.pallas_call(functools.partial(border_kernel, coeffs, returns, lanes),...]
  transfers between devices with their start and end apart: 9 -> 10, of which waited for: 6 -> 6; matrix products, arithmetic and copies ran while one was open for 10% -> 5% of each run, Pallas kernels for 32% -> 42%
where the time goes in v2:
time: 292 us; the launch traced here: 290 us
  waiting for transfers between devices  139 us (48%)
  Pallas kernels  126 us (43%)
  other arithmetic  12.8 us (4%)
  starting transfers between devices  9.38 us (3%)
    ppermute x2, waiting for transfers between devices, shards(): borders.append(lax.ppermute(piece, 'gx', far))  111 us
    pallas_call x3, Pallas kernels, border_part(): pl.pallas_call(functools.partial(border_kernel, coeffs, returns, lanes),...  42.7 us
    pallas_call x1, Pallas kernels, local_part(): pl.pallas_call(functools.partial(local_kernel, coeffs, lanes), grid=(rows...  28.2 us
    pallas_call x2, Pallas kernels, wall_part(): pl.pallas_call(functools.partial(wall_kernel, groups, rows), grid_spec=gr...  20.2 us
    pallas_call x4, Pallas kernels, pack(): pl.pallas_call(pack_kernel, grid_spec=grid_spec, out_shape=jax.ShapeDtype...  19 us
    pallas_call x4, Pallas kernels, add_part(): pl.pallas_call(add_kernel, grid_spec=grid_spec, out_shape=jax.ShapeDtypeS...  15.9 us
    ppermute x4, waiting for transfers between devices, along_yz(): lax.ppermute(x, 'yz', [(i, (i + by) % groups) for i in range(groups)])  14.5 us
    ppermute x2, waiting for transfers between devices, shards(): border_back.append(lax.ppermute(back, 'gx', far))  14.2 us
  transfers between devices with their start and end apart: 10, of which 6 were waited for; matrix products, arithmetic and copies ran while one was open for 5% of the time, Pallas kernels for 42%

profile of v2, /device:TPU:1, one launch (start us, length us, event | category | flops | bytes accessed | tf_op | source)
XLA Modules:
  0.0 289.8 jit_solution(4977086981956079844)
XLA Ops:
  0.5 4.6 %pack_wall.3 = f32[5,2,192,512]{3,2,1,0:T(8,128)} custom-call(s32[1]{0:T(128)} %bitcast.3.place_ref, f32[3,4,192,1024]{3,2,1,0:T(8,128)} %comp_ref.15, f32[3,4,192,1024]{3,2,1,0:T(8,128)} %vel_ref.15), custom_call_target="tpu_custom_call" | custom-call | flops 1024 | bytes 1024 | tf_op jit(solution)/shard_map/pack_wall/pallas_call | solution.py:121
  5.1 2.2 collective-permute-start.3
  7.4 4.9 %pack_border.3 = f32[5,4,48,1024]{3,2,1,0:T(8,128)} custom-call(s32[1]{0:T(128)} %bitcast.place_ref, f32[3,4,192,1024]{3,2,1,0:T(8,128)} %comp_ref.15, f32[3,4,192,1024]{3,2,1,0:T(8,128)} %vel_ref.15), custom_call_target="tpu_custom_call" | custom-call | flops 1024 | bytes 1024 | tf_op jit(solution)/shard_map/pack_border/pallas_call | solution.py:121
  12.2 1.9 collective-permute-start.2
  14.1 4.6 %pack_wall.2 = f32[5,2,192,512]{3,2,1,0:T(8,128)} custom-call(s32[1]{0:T(128)} %bitcast.3.place_ref, f32[3,4,192,1024]{3,2,1,0:T(8,128)} %comp_ref.15, f32[3,4,192,1024]{3,2,1,0:T(8,128)} %vel_ref.15), custom_call_target="tpu_custom_call" | custom-call | flops 1024 | bytes 1024 | tf_op jit(solution)/shard_map/pack_wall/pallas_call | solution.py:121
  19.0 4.9 %pack_border.2 = f32[5,4,48,1024]{3,2,1,0:T(8,128)} custom-call(s32[1]{0:T(128)} %bitcast.place_ref, f32[3,4,192,1024]{3,2,1,0:T(8,128)} %comp_ref.15, f32[3,4,192,1024]{3,2,1,0:T(8,128)} %vel_ref.15), custom_call_target="tpu_custom_call" | custom-call | flops 1024 | bytes 1024 | tf_op jit(solution)/shard_map/pack_border/pallas_call | solution.py:121
  24.3 0.7 broadcast_in_dim.48.step_ref
  25.0 28.2 %local_part.1.refs_2_ = f32[3,4,192,1024]{3,2,1,0:T(8,128)} custom-call(f32[192,128]{1,0:T(8,128)} %broadcast_in_dim.48.step_ref, f32[3,4,192,1024]{3,2,1,0:T(8,128)} %comp_ref.15, f32[3,4,192,1024]{3,2,1,0:T(8,128)} %vel_ref.15), custom_call_target="tpu_custom_call" | custom-call | flops 1024 | bytes 1024 | tf_op jit(solution)/shard_map/local_part/pallas_call | solution.py:95
  53.2 0.7 pad_add_fusion.1.flag_ref
  54.4 0.6 pad_add_fusion.2.flag_ref
  55.1 4.8 %fusion.11 = f32[384]{0:T(512)S(1)} fusion(f32[384]{0:T(512)S(1)} %get-tuple-element.24, s32[384]{0:T(512)S(1)} %fusion.14), kind=kLoop, calls=%fused_computation.25 | loop fusion | flops 4275840 | bytes 4608 | tf_op jit(solution)/shard_map/reduce_sum | solution.py:33
  59.9 5.0 %reduce-precision_convert_fusion = (bf16[384,384]{1,0:T(8,128)(2,1)S(1)}, bf16[384,384]{1,0:T(8,128)(2,1)S(1)}) fusion(f32[384]{0:T(512)S(1)} %fusion.11, f32[384]{0:T(512)S(1)} %get-tuple-element.23, f32[384]{0:T(512)S(1)} %get-tuple-element.24, s32[384]{0:T(512)S(1)} %fusion.14), kind=kLoop, calls=%fused_computation.8 | loop fusion | flops 5455872 | bytes 595968 | tf_op jit(solution)/shard_map/convert
  64.9 1.0 pad_maximum_fusion.refs_4_
  65.9 25.3 %border_part.3.refs_5_ = f32[3,4,192,1024]{3,2,1,0:T(8,128)} custom-call(s32[2]{0:T(128)} %pad_add_fusion.2.flag_ref, f32[192,128]{1,0:T(8,128)} %broadcast_in_dim.48.step_ref, f32[3,4,192,1024]{3,2,1,0:T(8,128)} %comp_ref.15, f32[3,4,192,1024]{3,2,1,0:T(8,128)} %vel_ref.15, ...), custom_call_target="tpu_custom_call", output_to_operand_aliasing={{}: (6, {})} | custom-call | flops 1024 | bytes 1024 | tf_op jit(solution)/shard_map/border_part/pallas_call | solution.py:251
  91.2 1.3 collective-permute-done.3.refs_3_
  92.5 10.1 %wall_part.2 = (f32[3,4,192,1024]{3,2,1,0:T(8,128)}, f32[3,2,192,512]{3,2,1,0:T(8,128)}) custom-call(s32[1]{0:T(128)} %bitcast.2.refs_0_, f32[3,4,192,1024]{3,2,1,0:T(8,128)} %comp_ref.15, f32[3,4,192,1024]{3,2,1,0:T(8,128)} %vel_ref.15, f32[5,2,192,512]{3,2,1,0:T(8,128)} %collective-permute-done.3.refs_3_, ...), custom_call_target="tpu_custom_call", output_to_operand_aliasing={{0}: (5, {})} | custom-call | flops 1024 | bytes 1024 | tf_op jit(solution)/shard_map/wall_part/pallas_call | solution.py:195
  102.6 1.1 collective-permute-start.9
  103.8 63.9 %collective-permute-done.2.refs_0_ = f32[5,4,48,1024]{3,2,1,0:T(8,128)} collective-permute-done((f32[5,4,48,1024]{3,2,1,0:T(8,128)}, f32[5,4,48,1024]{3,2,1,0:T(8,128)}, u32[]{:S(2)}, u32[]{:S(2)}) %collective-permute-start.2) | collective-permute-done | bytes 3932192 | tf_op jit(solution)/shard_map/ppermute | solution.py:336
  167.7 8.7 %border_part.4 = (f32[3,4,192,1024]{3,2,1,0:T(8,128)}, f32[3,4,48,1024]{3,2,1,0:T(8,128)}) custom-call(s32[2]{0:T(128)} %pad_add_fusion.1.flag_ref, f32[192,128]{1,0:T(8,128)} %broadcast_in_dim.48.step_ref, f32[3,4,192,1024]{3,2,1,0:T(8,128)} %comp_ref.15, f32[3,4,192,1024]{3,2,1,0:T(8,128)} %vel_ref.15, ...), custom_call_target="tpu_custom_call", output_to_operand_aliasing={{0}: (5, {})} | custom-call | flops 1024 | bytes 1024 | tf_op jit(solution)/shard_map/border_part/pallas_call | solution.py:251
  176.4 1.4 collective-permute-start.8
  177.8 10.1 %wall_part.3 = (f32[3,4,192,1024]{3,2,1,0:T(8,128)}, f32[3,2,192,512]{3,2,1,0:T(8,128)}) custom-call(s32[1]{0:T(128)} %bitcast.2.refs_0_, f32[3,4,192,1024]{3,2,1,0:T(8,128)} %comp_ref.15, f32[3,4,192,1024]{3,2,1,0:T(8,128)} %vel_ref.15, f32[5,2,192,512]{3,2,1,0:T(8,128)} %collective-permute-done.1.refs_3_, ...), custom_call_target="tpu_custom_call", output_to_operand_aliasing={{0}: (5, {})} | custom-call | flops 1024 | bytes 1024 | tf_op jit(solution)/shard_map/wall_part/pallas_call | solution.py:195
  188.2 46.9 %collective-permute-done.refs_0_ = f32[5,4,48,1024]{3,2,1,0:T(8,128)} collective-permute-done((f32[5,4,48,1024]{3,2,1,0:T(8,128)}, f32[5,4,48,1024]{3,2,1,0:T(8,128)}, u32[]{:S(2)}, u32[]{:S(2)}) %collective-permute-start) | collective-permute-done | bytes 3932192 | tf_op jit(solution)/shard_map/ppermute | solution.py:336
  235.1 8.7 %border_part.5 = (f32[3,4,192,1024]{3,2,1,0:T(8,128)}, f32[3,4,48,1024]{3,2,1,0:T(8,128)}) custom-call(s32[2]{0:T(128)} %pad_add_fusion.flag_ref, f32[192,128]{1,0:T(8,128)} %broadcast_in_dim.48.step_ref, f32[3,4,192,1024]{3,2,1,0:T(8,128)} %comp_ref.15, f32[3,4,192,1024]{3,2,1,0:T(8,128)} %vel_ref.15, ...), custom_call_target="tpu_custom_call", output_to_operand_aliasing={{0}: (5, {})} | custom-call | flops 1024 | bytes 1024 | tf_op jit(solution)/shard_map/border_part/pallas_call | solution.py:251
  243.8 1.4 collective-permute-start.6
  245.2 1.4 copy-done
  246.6 3.5 %add_wall.2.acc_ref = f32[3,4,192,1024]{3,2,1,0:T(8,128)} custom-call(s32[1]{0:T(128)} %bitcast.6.place_ref, f32[3,2,192,512]{3,2,1,0:T(8,128)} %copy-done, f32[3,4,192,1024]{3,2,1,0:T(8,128)} %get-tuple-element.20.acc_ref), custom_call_target="tpu_custom_call", output_to_operand_aliasing={{}: (2, {})} | custom-call | flops 1024 | bytes 1024 | tf_op jit(solution)/shard_map/add_wall/pallas_call | solution.py:275
  250.1 10.2 %collective-permute-done.8.part_ref = f32[3,4,48,1024]{3,2,1,0:T(8,128)} collective-permute-done((f32[3,4,48,1024]{3,2,1,0:T(8,128)}, f32[3,4,48,1024]{3,2,1,0:T(8,128)}, u32[]{:S(2)}, u32[]{:S(2)}) %collective-permute-start.8) | collective-permute-done | bytes 2359328 | tf_op jit(solution)/shard_map/ppermute | solution.py:357
  260.4 4.5 %add_border.2.acc_ref = f32[3,4,192,1024]{3,2,1,0:T(8,128)} custom-call(s32[1]{0:T(128)} %bitcast.place_ref, f32[3,4,48,1024]{3,2,1,0:T(8,128)} %collective-permute-done.8.part_ref, f32[3,4,192,1024]{3,2,1,0:T(8,128)} %add_wall.2.acc_ref), custom_call_target="tpu_custom_call", output_to_operand_aliasing={{}: (2, {})} | custom-call | flops 1024 | bytes 1024 | tf_op jit(solution)/shard_map/add_border/pallas_call | solution.py:275
  264.8 13.1 %collective-permute-done.7.part_ref = f32[3,2,192,512]{3,2,1,0:T(8,128)} collective-permute-done((f32[3,2,192,512]{3,2,1,0:T(8,128)}, f32[3,2,192,512]{3,2,1,0:T(8,128)}, u32[]{:S(2)}, u32[]{:S(2)}) %collective-permute-start.7) | collective-permute-done | bytes 2359328 | tf_op jit(solution)/shard_map/ppermute | solution.py:324
  277.9 3.5 %add_wall.3.acc_ref = f32[3,4,192,1024]{3,2,1,0:T(8,128)} custom-call(s32[1]{0:T(128)} %bitcast.6.place_ref, f32[3,2,192,512]{3,2,1,0:T(8,128)} %collective-permute-done.7.part_ref, f32[3,4,192,1024]{3,2,1,0:T(8,128)} %add_border.2.acc_ref), custom_call_target="tpu_custom_call", output_to_operand_aliasing={{}: (2, {})} | custom-call | flops 1024 | bytes 1024 | tf_op jit(solution)/shard_map/add_wall/pallas_call | solution.py:275
  281.4 3.9 %collective-permute-done.6.part_ref = f32[3,4,48,1024]{3,2,1,0:T(8,128)} collective-permute-done((f32[3,4,48,1024]{3,2,1,0:T(8,128)}, f32[3,4,48,1024]{3,2,1,0:T(8,128)}, u32[]{:S(2)}, u32[]{:S(2)}) %collective-permute-start.6) | collective-permute-done | bytes 2359328 | tf_op jit(solution)/shard_map/ppermute | solution.py:357
  285.3 4.5 %add_border.3 = f32[3,4,192,1024]{3,2,1,0:T(8,128)} custom-call(s32[1]{0:T(128)} %bitcast.place_ref, f32[3,4,48,1024]{3,2,1,0:T(8,128)} %collective-permute-done.6.part_ref, f32[3,4,192,1024]{3,2,1,0:T(8,128)} %add_wall.3.acc_ref), custom_call_target="tpu_custom_call", output_to_operand_aliasing={{}: (2, {})} | custom-call | flops 1024 | bytes 1024 | tf_op jit(solution)/shard_map/add_border/pallas_call | solution.py:275
  (14 shorter events, 2.0 us)
Async XLA Ops:
  0.0 23.9 %collective-permute-start.4 = (f32[3,4,192,1024]{3,2,1,0:T(8,128)}, f32[3,4,192,1024]{3,2,1,0:T(8,128)}, u32[]{:S(2)}, u32[]{:S(2)}) collective-permute-start(f32[3,4,192,1024]{3,2,1,0:T(8,128)} %comp_ref.15), channel_id=1, source_target_pairs={{0,2},{2,0},{4,6},{6,4},{8,10},{10,8},{12,14},{14,12},{16,18},{18,... | collective-permute-start | bytes 28311560 | tf_op jit(solution)/shard_map/ppermute | solution.py:326
  0.1 65.8 %collective-permute-start.5 = (f32[3,4,192,1024]{3,2,1,0:T(8,128)}, f32[3,4,192,1024]{3,2,1,0:T(8,128)}, u32[]{:S(2)}, u32[]{:S(2)}) collective-permute-start(f32[3,4,192,1024]{3,2,1,0:T(8,128)} %vel_ref.15), channel_id=1, source_target_pairs={{0,2},{2,0},{4,6},{6,4},{8,10},{10,8},{12,14},{14,12},{16,18},{18,... | collective-permute-start | bytes 28311560 | tf_op jit(solution)/shard_map/ppermute | solution.py:326
  5.1 87.4 %collective-permute-start.3 = (f32[5,2,192,512]{3,2,1,0:T(8,128)}, f32[5,2,192,512]{3,2,1,0:T(8,128)}, u32[]{:S(2)}, u32[]{:S(2)}) collective-permute-start(f32[5,2,192,512]{3,2,1,0:T(8,128)} %pack_wall.3), channel_id=1, source_target_pairs={{0,1},{1,0},{2,3},{3,2},{4,5},{5,4},{6,7},{7,6},{8,9},{9,8},{10,11... | collective-permute-start | bytes 11796488 | tf_op jit(solution)/shard_map/ppermute | solution.py:324
  12.2 155.4 %collective-permute-start.2 = (f32[5,4,48,1024]{3,2,1,0:T(8,128)}, f32[5,4,48,1024]{3,2,1,0:T(8,128)}, u32[]{:S(2)}, u32[]{:S(2)}) collective-permute-start(f32[5,4,48,1024]{3,2,1,0:T(8,128)} %pack_border.3), channel_id=1, source_target_pairs={{0,30},{2,4},{4,2},{6,8},{8,6},{10,12},{12,10},{14,16},{16,14},{18... | collective-permute-start | bytes 11796488 | tf_op jit(solution)/shard_map/ppermute | solution.py:336
  18.8 159.0 %collective-permute-start.1 = (f32[5,2,192,512]{3,2,1,0:T(8,128)}, f32[5,2,192,512]{3,2,1,0:T(8,128)}, u32[]{:S(2)}, u32[]{:S(2)}) collective-permute-start(f32[5,2,192,512]{3,2,1,0:T(8,128)} %pack_wall.2), channel_id=1, source_target_pairs={{0,1},{1,0},{2,3},{3,2},{4,5},{5,4},{6,7},{7,6},{8,9},{9,8},{10,11... | collective-permute-start | bytes 11796488 | tf_op jit(solution)/shard_map/ppermute | solution.py:324
  23.9 211.2 %collective-permute-start = (f32[5,4,48,1024]{3,2,1,0:T(8,128)}, f32[5,4,48,1024]{3,2,1,0:T(8,128)}, u32[]{:S(2)}, u32[]{:S(2)}) collective-permute-start(f32[5,4,48,1024]{3,2,1,0:T(8,128)} %pack_border.2), channel_id=1, source_target_pairs={{0,30},{2,4},{4,2},{6,8},{8,6},{10,12},{12,10},{14,16},{16,14},{18... | collective-permute-start | bytes 11796488 | tf_op jit(solution)/shard_map/ppermute | solution.py:336
  102.6 142.6 %collective-permute-start.9 = (f32[3,2,192,512]{3,2,1,0:T(8,128)}, f32[3,2,192,512]{3,2,1,0:T(8,128)S(1)}, u32[]{:S(2)}, u32[]{:S(2)}) collective-permute-start(f32[3,2,192,512]{3,2,1,0:T(8,128)} %get-tuple-element.19), channel_id=1, source_target_pairs={{0,1},{1,0},{2,3},{3,2},{4,5},{5,4},{6,7},{7,6},{8,9},{9,8},{10,11... | collective-permute-start | bytes 7077896 | tf_op jit(solution)/shard_map/ppermute | solution.py:324
  176.4 84.0 %collective-permute-start.8 = (f32[3,4,48,1024]{3,2,1,0:T(8,128)}, f32[3,4,48,1024]{3,2,1,0:T(8,128)}, u32[]{:S(2)}, u32[]{:S(2)}) collective-permute-start(f32[3,4,48,1024]{3,2,1,0:T(8,128)} %get-tuple-element.18), channel_id=1, source_target_pairs={{0,30},{2,4},{4,2},{6,8},{8,6},{10,12},{12,10},{14,16},{16,14},{18... | collective-permute-start | bytes 7077896 | tf_op jit(solution)/shard_map/ppermute | solution.py:357
  187.9 90.0 %collective-permute-start.7 = (f32[3,2,192,512]{3,2,1,0:T(8,128)}, f32[3,2,192,512]{3,2,1,0:T(8,128)}, u32[]{:S(2)}, u32[]{:S(2)}) collective-permute-start(f32[3,2,192,512]{3,2,1,0:T(8,128)} %get-tuple-element.17), channel_id=1, source_target_pairs={{0,1},{1,0},{2,3},{3,2},{4,5},{5,4},{6,7},{7,6},{8,9},{9,8},{10,11... | collective-permute-start | bytes 7077896 | tf_op jit(solution)/shard_map/ppermute | solution.py:324
  243.8 41.6 %collective-permute-start.6 = (f32[3,4,48,1024]{3,2,1,0:T(8,128)}, f32[3,4,48,1024]{3,2,1,0:T(8,128)}, u32[]{:S(2)}, u32[]{:S(2)}) collective-permute-start(f32[3,4,48,1024]{3,2,1,0:T(8,128)} %get-tuple-element.16), channel_id=1, source_target_pairs={{0,30},{2,4},{4,2},{6,8},{8,6},{10,12},{12,10},{14,16},{16,14},{18... | collective-permute-start | bytes 7077896 | tf_op jit(solution)/shard_map/ppermute | solution.py:357
  245.2 1.4 copy-start

commit v3 on v2

--- a/solution.py
+++ b/solution.py
@@ -14,8 +14,7 @@
 relax_rate = 1.0 / 0.04
 courant = 0.5
 row_block = 8
-wall_weights = (1, 1)
-border_weights = (1, 1)
+share_weights = ((1,), (2, 1))
 vmem_bytes = 56 * 1024 * 1024
 
 
@@ -34,6 +33,7 @@
 
 
 small = pl.CostEstimate(flops=1024, bytes_accessed=1024, transcendentals=0)
+heavy = pl.CostEstimate(flops=100000000000, bytes_accessed=1024, transcendentals=0)
 
 
 def params():
@@ -89,58 +89,41 @@
             out_ref[f, i] = comp[f] + step * (terms[f] - w * along_z[f] - relax)
 
 
-def local_part(coeffs, step, comp, vel):
-    fields, planes, rows, lanes = comp.shape
-    block = pl.BlockSpec((3, planes, row_block, lanes), lambda r: (0, 0, r, 0))
+def pack_kernel(boxes, place_ref, comp_ref, vel_ref, *refs):
+    outs, held, sems = refs[: len(boxes)], refs[len(boxes) : -1], refs[-1]
+    loads, stores = [], []
+    for j, (plane, n_planes, row, row_unit, n_rows, lane_unit, n_lanes) in enumerate(boxes):
+        rows = pl.ds(pl.multiple_of(place_ref[j] * row_unit + row, row_block), n_rows)
+        lanes = pl.ds(pl.multiple_of(place_ref[j] * lane_unit, 128), n_lanes)
+        for source, first, fields in ((comp_ref, 0, 3), (vel_ref, 3, 2)):
+            for f in range(fields):
+                for p in range(n_planes):
+                    k, to = len(loads), (first + f, p)
+                    loads.append(pltpu.make_async_copy(source.at[f, plane + p, rows, lanes], held[j].at[to], sems.at[0, k]))
+                    stores.append(pltpu.make_async_copy(held[j].at[to], outs[j].at[to], sems.at[1, k]))
+    for load in loads:
+        load.start()
+    for load, store in zip(loads, stores):
+        load.wait()
+        store.start()
+    for store in stores:
+        store.wait()
+
+
+def pack(places, boxes, comp, vel):
+    here = pl.BlockSpec(memory_space=pltpu.HBM)
+    shapes = [(5, planes, rows, lanes) for _, planes, _, _, rows, _, lanes in boxes]
     return pl.pallas_call(
-        functools.partial(local_kernel, coeffs, lanes),
-        grid=(rows // row_block,),
-        in_specs=[pl.BlockSpec((row_block, 128), lambda r: (r, 0)), block, block],
-        out_specs=block,
-        out_shape=jax.ShapeDtypeStruct(comp.shape, jnp.float32),
+        functools.partial(pack_kernel, boxes),
+        in_specs=[pl.BlockSpec(memory_space=pltpu.SMEM), here, here],
+        out_specs=[here] * len(boxes),
+        out_shape=[jax.ShapeDtypeStruct(shape, jnp.float32) for shape in shapes],
+        scratch_shapes=[pltpu.VMEM(shape, jnp.float32) for shape in shapes]
+        + [pltpu.SemaphoreType.DMA((2, sum(5 * shape[1] for shape in shapes)))],
         compiler_params=params(),
         cost_estimate=small,
-        name="local_part",
-    )(step, comp, vel)
-
-
-def pack_kernel(place_ref, comp_ref, vel_ref, out_ref):
-    out_ref[0:3] = comp_ref[...]
-    out_ref[3:5] = vel_ref[...]
-
-
-def pack(place, block, grid, source_at, sent_at, comp, vel, name):
-    planes, rows, lanes = block
-    shape = (5, grid[0] * planes, grid[1] * rows, grid[2] * lanes)
-    grid_spec = pltpu.PrefetchScalarGridSpec(
-        num_scalar_prefetch=1,
-        grid=grid,
-        in_specs=[pl.BlockSpec((3, *block), source_at), pl.BlockSpec((2, *block), source_at)],
-        out_specs=pl.BlockSpec((5, *block), sent_at),
-    )
-    return pl.pallas_call(
-        pack_kernel,
-        grid_spec=grid_spec,
-        out_shape=jax.ShapeDtypeStruct(shape, jnp.float32),
-        compiler_params=params(),
-        cost_estimate=small,
-        name=name,
-    )(place, comp, vel)
-
-
-def pack_wall(first, planes, columns, place, comp, vel):
-    rows = comp.shape[2]
-    tile = min(columns, 256)
-    tiles = columns // tile
-    source_at = lambda p, r, i, s: (0, first + p, 0, s[0] * tiles + i)
-    return pack(place, (1, rows, tile), (planes, 1, tiles), source_at, lambda p, r, i, s: (0, p, 0, i), comp, vel, "pack_wall")
-
-
-def pack_border(row, size, half, place, comp, vel):
-    planes, rows, lanes = comp.shape[1:]
-    tall = math.gcd(2 * row_block, math.gcd(half, math.gcd(row, size)))
-    source_at = lambda p, r, i, s: (0, 0, s[0] * (half // tall) + row // tall + r, 0)
-    return pack(place, (planes, tall, lanes), (1, size // tall, 1), source_at, lambda p, r, i, s: (0, 0, r, 0), comp, vel, "pack_border")
+        name="pack",
+    )(places, comp, vel)
 
 
 def wall_kernel(groups, rows, *refs):
@@ -171,21 +154,21 @@
             back[g - 1][f, 0] = terms[f][g * rows : (g + 1) * rows]
 
 
-def wall_part(first, place, comp, vel, received, matrix, acc):
+def wall_part(first, skip, planes, place, comp, vel, received, matrix, acc):
     groups = len(received) + 1
     rows, lanes = comp.shape[2:]
-    planes = received[0].shape[1]
     columns = lanes // groups
     tile = min(columns, 256)
     tiles = columns // tile
     own = lambda p, i, s: (0, first + p, 0, s[0] * tiles + i)
     own_block = pl.BlockSpec((3, 1, rows, tile), own)
+    held = lambda p, i, s: (0, skip + p, 0, i)
     sent = lambda p, i, s: (0, p, 0, i)
     grid_spec = pltpu.PrefetchScalarGridSpec(
         num_scalar_prefetch=1,
         grid=(planes, tiles),
         in_specs=[own_block, pl.BlockSpec((2, 1, rows, tile), own)]
-        + [pl.BlockSpec((5, 1, rows, tile), sent)] * (groups - 1)
+        + [pl.BlockSpec((5, 1, rows, tile), held)] * (groups - 1)
         + [pl.BlockSpec(matrix.shape, lambda p, i, s: (0, 0)), own_block],
         out_specs=[own_block] + [pl.BlockSpec((3, 1, rows, tile), sent)] * (groups - 1),
     )
@@ -198,7 +181,7 @@
         out_shape=shapes,
         input_output_aliases={3 + groups: 0},
         compiler_params=params(),
-        cost_estimate=small,
+        cost_estimate=heavy,
         name="wall_part",
     )(place, comp, vel, *received, matrix, acc)
     return out[0], out[1:]
@@ -231,10 +214,11 @@
     pl.when(flag_ref[0] == 0)(lambda: run(False))
 
 
-def border_part(returns, flags, coeffs, step, comp, vel, received, acc):
-    planes, size, lanes = received[0].shape[1:]
+def border_part(returns, skip, size, flags, coeffs, step, comp, vel, received, acc):
+    planes, lanes = comp.shape[1], comp.shape[3]
     here = lambda r, s: (0, 0, s[1] + r, 0)
     block = pl.BlockSpec((3, planes, row_block, lanes), here)
+    held = lambda r, s: (0, 0, skip // row_block + r, 0)
     sent = lambda r, s: (0, 0, r, 0)
     grid_spec = pltpu.PrefetchScalarGridSpec(
         num_scalar_prefetch=1,
@@ -243,7 +227,7 @@
             pl.BlockSpec((row_block, 128), lambda r, s: (s[1] + r, 0)),
             block,
             pl.BlockSpec((2, planes, row_block, lanes), here),
-            *(pl.BlockSpec((min(x.shape[0], 5 - at), planes, row_block, lanes), sent) for at, x in zip((0, 3), received)),
+            *(pl.BlockSpec((min(x.shape[0], 5 - at), planes, row_block, lanes), held) for at, x in zip((0, 3), received)),
             block,
         ],
         out_specs=[block] + [pl.BlockSpec((3, planes, row_block, lanes), sent)] * returns,
@@ -255,54 +239,89 @@
         + [jax.ShapeDtypeStruct((3, planes, size, lanes), jnp.float32)] * returns,
         input_output_aliases={4 + len(received): 0},
         compiler_params=params(),
-        cost_estimate=small,
+        cost_estimate=heavy if returns else small,
         name="border_part",
     )(flags, step, comp, vel, *received, acc)
     return out
 
 
-def add_kernel(place_ref, part_ref, acc_ref, out_ref):
-    out_ref[...] = acc_ref[...] + part_ref[...]
-
-
-def add_part(place, part, acc, block, grid, part_at, acc_at, name):
+def first_kernel(coeffs, lanes, flag_ref, step_ref, comp_ref, vel_ref, comp_near, vel_near, out_ref):
+    local_kernel(coeffs, lanes, step_ref, comp_ref, vel_ref, out_ref)
+    border_kernel(coeffs, False, lanes, flag_ref, step_ref, comp_ref, vel_ref, comp_near, vel_near, out_ref, out_ref)
+
+
+def first_part(flags, coeffs, step, comp, vel, comp_near, vel_near):
+    fields, planes, rows, lanes = comp.shape
+    at = lambda r, s: (0, 0, r, 0)
+    block = pl.BlockSpec((fields, planes, row_block, lanes), at)
+    two = pl.BlockSpec((2, planes, row_block, lanes), at)
     grid_spec = pltpu.PrefetchScalarGridSpec(
         num_scalar_prefetch=1,
-        grid=grid,
-        in_specs=[pl.BlockSpec(block, part_at), pl.BlockSpec(block, acc_at)],
-        out_specs=pl.BlockSpec(block, acc_at),
+        grid=(rows // row_block,),
+        in_specs=[pl.BlockSpec((row_block, 128), lambda r, s: (r, 0)), block, block, block, two],
+        out_specs=block,
     )
     return pl.pallas_call(
-        add_kernel,
+        functools.partial(first_kernel, coeffs, lanes),
         grid_spec=grid_spec,
+        out_shape=jax.ShapeDtypeStruct(comp.shape, jnp.float32),
+        compiler_params=params(),
+        cost_estimate=small,
+        name="first_part",
+    )(flags, step, comp, vel, comp_near, vel_near)
+
+
+def add_kernel(first, row, row_unit, lane_unit, place_ref, part_ref, acc_ref, out_ref, parts, sums, sems):
+    fields, planes, size, lanes = part_ref.shape
+    rows = pl.ds(pl.multiple_of(place_ref[0] * row_unit + row, row_block), size)
+    columns = pl.ds(pl.multiple_of(place_ref[0] * lane_unit, 128), lanes)
+    pieces = [(f, p) for f in range(fields) for p in range(planes)]
+    loads, stores = [], []
+    for k, (f, p) in enumerate(pieces):
+        loads.append(
+            (
+                pltpu.make_async_copy(part_ref.at[f, p], parts.at[f, p], sems.at[0, k]),
+                pltpu.make_async_copy(acc_ref.at[f, first + p, rows, columns], sums.at[f, p], sems.at[1, k]),
+            )
+        )
+        stores.append(pltpu.make_async_copy(parts.at[f, p], out_ref.at[f, first + p, rows, columns], sems.at[2, k]))
+    for pair in loads:
+        for load in pair:
+            load.start()
+    for (f, p), pair, store in zip(pieces, loads, stores):
+        for load in pair:
+            load.wait()
+        parts[f, p] = parts[f, p] + sums[f, p]
+        store.start()
+    for store in stores:
+        store.wait()
+
+
+def add_part(first, row, row_unit, lane_unit, place, part, acc):
+    here = pl.BlockSpec(memory_space=pltpu.HBM)
+    return pl.pallas_call(
+        functools.partial(add_kernel, first, row, row_unit, lane_unit),
+        in_specs=[pl.BlockSpec(memory_space=pltpu.SMEM), pl.BlockSpec(memory_space=pl.ANY), here],
+        out_specs=here,
         out_shape=jax.ShapeDtypeStruct(acc.shape, jnp.float32),
         input_output_aliases={2: 0},
+        scratch_shapes=[pltpu.VMEM(part.shape, jnp.float32)] * 2
+        + [pltpu.SemaphoreType.DMA((3, part.shape[0] * part.shape[1]))],
         compiler_params=params(),
         cost_estimate=small,
-        name=name,
+        name="add_part",
     )(place, part, acc)
 
 
-def add_wall(first, place, part, acc):
-    fields, planes, rows, columns = part.shape
-    block = (fields, 1, rows, columns)
-    return add_part(
-        place, part, acc, block, (planes,), lambda p, s: (0, p, 0, 0), lambda p, s: (0, first + p, 0, s[0]), "add_wall"
-    )
-
-
-def add_border(row, half, place, part, acc):
-    fields, planes, size, lanes = part.shape
-    tall = math.gcd(2 * row_block, math.gcd(half, math.gcd(row, size)))
-    block = (fields, planes, tall, lanes)
-    acc_at = lambda r, s: (0, 0, s[0] * (half // tall) + row // tall + r, 0)
-    return add_part(place, part, acc, block, (size // tall,), lambda r, s: (0, 0, r, 0), acc_at, "add_border")
-
-
-def shares(total, unit, weights):
-    units = total // unit
-    ends = [unit * round(units * sum(weights[: k + 1]) / sum(weights)) for k in range(len(weights))]
-    return list(zip([0] + ends[:-1], [b - a for a, b in zip([0] + ends[:-1], ends)]))
+def shares(total, unit):
+    flat = [w for share in share_weights for w in share]
+    ends = [unit * round(total // unit * sum(flat[:k]) / sum(flat)) for k in range(len(flat) + 1)]
+    cuts, k = [], 0
+    for share in share_weights:
+        own = [(a, b - a) for a, b in zip(ends[k:], ends[k + 1 : k + 1 + len(share)]) if b > a]
+        cuts.append((ends[k], ends[k + len(share)] - ends[k], own))
+        k += len(share)
+    return [cut for cut in cuts if cut[1]]
 
 
 def shards(conformation, velocity):
@@ -315,8 +334,8 @@
     spacing = math.pi / (count - 1)
     coeffs = tuple(c / spacing for c in stencil_coeffs)
     half = rows // 2
-    wall_cuts = shares(planes, 1, wall_weights)
-    border_cuts = shares(half, row_block, border_weights)
+    wall_cuts = shares(planes, 1)
+    border_cuts = shares(half, row_block)
     near = [(i, i ^ 1) for i in range(slabs)]
     far = [(i, (i + 1 if i % 2 else i - 1) % slabs) for i in range(slabs)]
 
@@ -325,15 +344,22 @@
 
     beside = [lax.ppermute(x, "gx", near) for x in (conformation, velocity)]
     walls, borders = [], []
-    for (plane, n_planes), (row, n_rows) in zip(wall_cuts, border_cuts):
-        pieces = [None] * groups
-        for g in range(1, groups):
-            place = ((me + g) % groups).astype(jnp.int32).reshape(1)
-            piece = pack_wall(plane, n_planes, columns, place, conformation, velocity)
-            pieces[groups - g] = along_yz(piece, g)
-        walls.append(pieces[1:])
-        piece = pack_border(row, n_rows, half, odd.reshape(1), conformation, velocity)
-        borders.append(lax.ppermute(piece, "gx", far))
+    for k in range(len(share_weights)):
+        places, boxes = [], []
+        for plane, n_planes, _ in wall_cuts[k : k + 1]:
+            places += [(me + g) % groups for g in range(1, groups)]
+            boxes += [(plane, n_planes, 0, 0, rows, columns, columns)] * (groups - 1)
+        for row, n_rows, _ in border_cuts[k : k + 1]:
+            places.append(odd)
+            boxes.append((0, planes, row, half, n_rows, 0, lanes))
+        packed = [
+            pack(place.astype(jnp.int32).reshape(1), [box], conformation, velocity)[0] for place, box in zip(places, boxes)
+        ]
+        if k < len(wall_cuts):
+            walls.append([along_yz(packed[g - 1], g) for g in range(1, groups)][::-1])
+        if k < len(border_cuts):
+            borders.append(lax.ppermute(packed[-1], "gx", far))
+
     index = jnp.arange(count, dtype=jnp.int32)
     points = index % rows * groups + (index // rows + me) % groups
     theta = math.pi * points.astype(jnp.float32) / (count - 1)
@@ -344,22 +370,30 @@
     matrix = jnp.concatenate([high, high, low], axis=1).astype(jnp.bfloat16)
     step = jnp.broadcast_to(step_size[:rows, None], (rows, 128))
 
-    acc = local_part(coeffs, step, conformation, velocity)
-    near_flags = jnp.stack([1 - odd, jnp.zeros_like(odd)])
-    (acc,) = border_part(False, near_flags, coeffs, step, conformation, velocity, beside, acc)
+    acc = first_part((1 - odd).reshape(1), coeffs, step, conformation, velocity, *beside)
     place = me.astype(jnp.int32).reshape(1)
-    wall_back, border_back = [], []
-    for k, ((plane, _), (row, _)) in enumerate(zip(wall_cuts, border_cuts)):
-        acc, back = wall_part(plane, place, conformation, velocity, walls[k], matrix, acc)
-        wall_back.append([along_yz(b, g) for g, b in enumerate(back, 1)])
-        far_flags = jnp.stack([odd, ((1 - odd) * half + row) // row_block])
-        acc, back = border_part(True, far_flags, coeffs, step, conformation, velocity, [borders[k]], acc)
-        border_back.append(lax.ppermute(back, "gx", far))
-    for k, ((plane, _), (row, _)) in enumerate(zip(wall_cuts, border_cuts)):
-        for g, part in enumerate(wall_back[k], 1):
-            source = ((me - g) % groups).astype(jnp.int32).reshape(1)
-            acc = add_wall(plane, source, part, acc)
-        acc = add_border(row, half, odd.reshape(1), border_back[k], acc)
+    returned = []
+    for k in range(len(share_weights)):
+        wall_own = wall_cuts[k][2] if k < len(wall_cuts) else []
+        border_own = border_cuts[k][2] if k < len(border_cuts) else []
+        for j in range(max(len(wall_own), len(border_own))):
+            if j < len(wall_own):
+                at, size = wall_own[j]
+                acc, back = wall_part(
+                    at, at - wall_cuts[k][0], size, place, conformation, velocity, walls[k], matrix, acc
+                )
+                for g, b in enumerate(back, 1):
+                    source = ((me - g) % groups).astype(jnp.int32).reshape(1)
+                    returned.append((at, 0, 0, columns, source, along_yz(b, g)))
+            if j < len(border_own):
+                at, size = border_own[j]
+                far_flags = jnp.stack([odd, ((1 - odd) * half + at) // row_block])
+                acc, back = border_part(
+                    True, at - border_cuts[k][0], size, far_flags, coeffs, step, conformation, velocity, [borders[k]], acc
+                )
+                returned.append((0, at, half, 0, odd.reshape(1), lax.ppermute(back, "gx", far)))
+    for first, row, row_unit, lane_unit, source, part in returned:
+        acc = add_part(first, row, row_unit, lane_unit, source, part, acc)
     return acc
 
 

time: 292 us -> 286 us (0.979)
  Pallas kernels: 126 us -> 109 us
  waiting for transfers between devices: 139 us -> 147 us
    ppermute x4 -> x5, waiting for transfers between devices: 14.5 us -> 45.5 us  [along_yz(): lax.ppermute(x, 'yz', [(i, (i + by) % groups) for i in range(groups)])]
    ppermute x4 -> x5, waiting for transfers between devices: 125 us -> 102 us  [the longest x2 60.6 us: shards(): borders.append(lax.ppermute(packed[-1], 'gx', far))]
    pallas_call x3, Pallas kernels: 42.7 us -> 20.1 us  [border_part(): pl.pallas_call(functools.partial(border_kernel, coeffs, returns, lanes),...]
    pallas_call x9 -> x11, Pallas kernels: 63.1 us -> 66.6 us  [the longest x1 33.2 us: first_part(): pl.pallas_call(functools.partial(first_kernel, coeffs, lanes), grid_spec=...]
    pallas_call x2 -> x3, Pallas kernels: 20.2 us -> 22.6 us  [wall_part(): pl.pallas_call(functools.partial(wall_kernel, groups, rows), grid_spec=gr...]
    another operation x4 -> x3, other arithmetic: 6.87 us -> 6.25 us
  transfers between devices with their start and end apart: 10 -> 12, of which waited for: 6 -> 8; matrix products, arithmetic and copies ran while one was open for 5% -> 5% of each run, Pallas kernels for 42% -> 37%
where the time goes in v3:
time: 286 us; the launch traced here: 285 us
  waiting for transfers between devices  147 us (51%)
  Pallas kernels  109 us (38%)
  other arithmetic  12.2 us (4%)
  starting transfers between devices  11.5 us (4%)
  local copies, waits for them, and re-layouts  4.09 us (1%)
    ppermute x2, waiting for transfers between devices, shards(): borders.append(lax.ppermute(packed[-1], 'gx', far))  60.6 us
    ppermute x5, waiting for transfers between devices, along_yz(): lax.ppermute(x, 'yz', [(i, (i + by) % groups) for i in range(groups)])  45.5 us
    ppermute x3, waiting for transfers between devices, shards(): lax.ppermute(back, 'gx', far)  41.3 us
    pallas_call x1, Pallas kernels, first_part(): pl.pallas_call(functools.partial(first_kernel, coeffs, lanes), grid_spec=...  33.2 us
    pallas_call x3, Pallas kernels, wall_part(): pl.pallas_call(functools.partial(wall_kernel, groups, rows), grid_spec=gr...  22.6 us
    pallas_call x3, Pallas kernels, border_part(): pl.pallas_call(functools.partial(border_kernel, coeffs, returns, lanes),...  20.1 us
    pallas_call x6, Pallas kernels, add_part(): pl.pallas_call(functools.partial(add_kernel, first, row, row_unit, lane_u...  17.8 us
    pallas_call x4, Pallas kernels, pack(): pl.pallas_call(functools.partial(pack_kernel, boxes), in_specs=[pl.BlockS...  15.6 us
  transfers between devices with their start and end apart: 12, of which 8 were waited for; matrix products, arithmetic and copies ran while one was open for 5% of the time, Pallas kernels for 37%

profile of v3, /device:TPU:1, one launch (start us, length us, event | category | flops | bytes accessed | tf_op | source)
XLA Modules:
  0.0 284.6 jit_solution(16173164505627356537)
XLA Ops:
  0.5 2.4 pack.7
  2.9 2.3 collective-permute-start.3
  5.2 2.6 pack.6
  7.8 1.9 collective-permute-start.2
  9.8 5.2 %pack.5 = f32[5,3,192,512]{3,2,1,0:T(8,128)} custom-call(s32[1]{0:T(128)} %bitcast.3.place_ref, f32[3,4,192,1024]{3,2,1,0:T(8,128)} %comp_ref.15, f32[3,4,192,1024]{3,2,1,0:T(8,128)} %vel_ref.15), custom_call_target="tpu_custom_call" | custom-call | flops 1024 | bytes 1024 | tf_op jit(solution)/shard_map/pack/pallas_call | solution.py:116
  15.3 5.3 %pack.4 = f32[5,4,72,1024]{3,2,1,0:T(8,128)} custom-call(s32[1]{0:T(128)} %bitcast.place_ref, f32[3,4,192,1024]{3,2,1,0:T(8,128)} %comp_ref.15, f32[3,4,192,1024]{3,2,1,0:T(8,128)} %vel_ref.15), custom_call_target="tpu_custom_call" | custom-call | flops 1024 | bytes 1024 | tf_op jit(solution)/shard_map/pack/pallas_call | solution.py:116
  22.1 4.8 %fusion.11 = f32[384]{0:T(512)S(1)} fusion(f32[384]{0:T(512)S(1)} %get-tuple-element.34, s32[384]{0:T(512)S(1)} %fusion.14), kind=kLoop, calls=%fused_computation.25 | loop fusion | flops 4275840 | bytes 4608 | tf_op jit(solution)/shard_map/reduce_sum | solution.py:32
  26.9 5.0 %reduce-precision_convert_fusion = (bf16[384,384]{1,0:T(8,128)(2,1)S(1)}, bf16[384,384]{1,0:T(8,128)(2,1)S(1)}) fusion(f32[384]{0:T(512)S(1)} %fusion.11, f32[384]{0:T(512)S(1)} %get-tuple-element.33, f32[384]{0:T(512)S(1)} %get-tuple-element.34, s32[384]{0:T(512)S(1)} %fusion.14), kind=kLoop, calls=%fused_computation.8 | loop fusion | flops 5455872 | bytes 595968 | tf_op jit(solution)/shard_map/convert
  34.0 33.2 %first_part.1.refs_5_ = f32[3,4,192,1024]{3,2,1,0:T(8,128)} custom-call(s32[1]{0:T(128)} %bitcast.6.flag_ref, f32[192,128]{1,0:T(8,128)} %broadcast_in_dim.48.step_ref, f32[3,4,192,1024]{3,2,1,0:T(8,128)} %comp_ref.15, f32[3,4,192,1024]{3,2,1,0:T(8,128)} %vel_ref.15, f32[3,4,192,1024]{3,2,1,0:T(8,128)} %collective-permute-done.4.comp_near, ...), custom_call_target="tpu_custom_call" | custom-call | flops 1024 | bytes 1024 | tf_op jit(solution)/shard_map/first_part/pallas_call | solution.py:264
  67.2 1.3 copy-done.2
  68.5 6.2 %wall_part.3 = (f32[3,4,192,1024]{3,2,1,0:T(8,128)}, f32[3,1,192,512]{3,2,1,0:T(8,128)}) custom-call(s32[1]{0:T(128)} %bitcast.2.refs_0_, f32[3,4,192,1024]{3,2,1,0:T(8,128)} %comp_ref.15, f32[3,4,192,1024]{3,2,1,0:T(8,128)} %vel_ref.15, f32[5,1,192,512]{3,2,1,0:T(8,128)} %copy-done.2, ...), custom_call_target="tpu_custom_call", output_to_operand_aliasing={{0}: (5, {})} | custom-call | flops 99999997952 | bytes 1024 | tf_op jit(solution)/shard_map/wall_part/pallas_call | solution.py:178
  75.9 53.7 %collective-permute-done.2.refs_0_ = f32[5,4,24,1024]{3,2,1,0:T(8,128)} collective-permute-done((f32[5,4,24,1024]{3,2,1,0:T(8,128)}, f32[5,4,24,1024]{3,2,1,0:T(8,128)}, u32[]{:S(2)}, u32[]{:S(2)}) %collective-permute-start.2) | collective-permute-done | bytes 1966112 | tf_op jit(solution)/shard_map/ppermute | solution.py:361
  129.6 5.7 %border_part.3 = (f32[3,4,192,1024]{3,2,1,0:T(8,128)}, f32[3,4,24,1024]{3,2,1,0:T(8,128)}) custom-call(s32[2]{0:T(128)} %pad_add_fusion.2.flag_ref, f32[192,128]{1,0:T(8,128)} %broadcast_in_dim.48.step_ref, f32[3,4,192,1024]{3,2,1,0:T(8,128)} %comp_ref.15, f32[3,4,192,1024]{3,2,1,0:T(8,128)} %vel_ref.15, ...), custom_call_target="tpu_custom_call", output_to_operand_aliasing={{0}: (5, {})} | custom-call | flops 99999997952 | bytes 1024 | tf_op jit(solution)/shard_map/border_part/pallas_call | solution.py:235
  135.3 1.4 collective-permute-start.10
  136.8 37.9 %collective-permute-done.1.refs_3_ = f32[5,3,192,512]{3,2,1,0:T(8,128)} collective-permute-done((f32[5,3,192,512]{3,2,1,0:T(8,128)}, f32[5,3,192,512]{3,2,1,0:T(8,128)}, u32[]{:S(2)}, u32[]{:S(2)}) %collective-permute-start.1) | collective-permute-done | bytes 5898272 | tf_op jit(solution)/shard_map/ppermute | solution.py:343
  174.7 10.1 %wall_part.4 = (f32[3,4,192,1024]{3,2,1,0:T(8,128)}, f32[3,2,192,512]{3,2,1,0:T(8,128)}) custom-call(s32[1]{0:T(128)} %bitcast.2.refs_0_, f32[3,4,192,1024]{3,2,1,0:T(8,128)} %comp_ref.15, f32[3,4,192,1024]{3,2,1,0:T(8,128)} %vel_ref.15, f32[5,3,192,512]{3,2,1,0:T(8,128)} %collective-permute-done.1.refs_3_, ...), custom_call_target="tpu_custom_call", output_to_operand_aliasing={{0}: (5, {})} | custom-call | flops 99999997952 | bytes 1024 | tf_op jit(solution)/shard_map/wall_part/pallas_call | solution.py:178
  185.9 6.9 %collective-permute-done.refs_0_ = f32[5,4,72,1024]{3,2,1,0:T(8,128)} collective-permute-done((f32[5,4,72,1024]{3,2,1,0:T(8,128)}, f32[5,4,72,1024]{3,2,1,0:T(8,128)}, u32[]{:S(2)}, u32[]{:S(2)}) %collective-permute-start) | collective-permute-done | bytes 5898272 | tf_op jit(solution)/shard_map/ppermute | solution.py:361
  192.8 8.7 %border_part.4 = (f32[3,4,192,1024]{3,2,1,0:T(8,128)}, f32[3,4,48,1024]{3,2,1,0:T(8,128)}) custom-call(s32[2]{0:T(128)} %get-tuple-element.32.flag_ref, f32[192,128]{1,0:T(8,128)} %broadcast_in_dim.48.step_ref, f32[3,4,192,1024]{3,2,1,0:T(8,128)} %comp_ref.15, f32[3,4,192,1024]{3,2,1,0:T(8,128)} %vel_ref.15, ...), custom_call_target="tpu_custom_call", output_to_operand_aliasing={{0}: (5, {})} | custom-call | flops 99999997952 | bytes 1024 | tf_op jit(solution)/shard_map/border_part/pallas_call | solution.py:235
  201.5 1.4 collective-permute-start.8
  202.9 6.2 %wall_part.5 = (f32[3,4,192,1024]{3,2,1,0:T(8,128)}, f32[3,1,192,512]{3,2,1,0:T(8,128)}) custom-call(s32[1]{0:T(128)} %bitcast.2.refs_0_, f32[3,4,192,1024]{3,2,1,0:T(8,128)} %comp_ref.15, f32[3,4,192,1024]{3,2,1,0:T(8,128)} %vel_ref.15, f32[5,3,192,512]{3,2,1,0:T(8,128)} %collective-permute-done.1.refs_3_, ...), custom_call_target="tpu_custom_call", output_to_operand_aliasing={{0}: (5, {})} | custom-call | flops 99999997952 | bytes 1024 | tf_op jit(solution)/shard_map/wall_part/pallas_call | solution.py:178
  209.4 5.7 %border_part.5 = (f32[3,4,192,1024]{3,2,1,0:T(8,128)}, f32[3,4,24,1024]{3,2,1,0:T(8,128)}) custom-call(s32[2]{0:T(128)} %get-tuple-element.31.flag_ref, f32[192,128]{1,0:T(8,128)} %broadcast_in_dim.48.step_ref, f32[3,4,192,1024]{3,2,1,0:T(8,128)} %comp_ref.15, f32[3,4,192,1024]{3,2,1,0:T(8,128)} %vel_ref.15, ...), custom_call_target="tpu_custom_call", output_to_operand_aliasing={{0}: (5, {})} | custom-call | flops 99999997952 | bytes 1024 | tf_op jit(solution)/shard_map/border_part/pallas_call | solution.py:235
  215.8 2.4 add_part.6.acc_ref
  218.2 25.2 %collective-permute-done.10.part_ref = f32[3,4,24,1024]{3,2,1,0:T(8,128)} collective-permute-done((f32[3,4,24,1024]{3,2,1,0:T(8,128)}, f32[3,4,24,1024]{3,2,1,0:T(8,128)}, u32[]{:S(2)}, u32[]{:S(2)}) %collective-permute-start.10) | collective-permute-done | bytes 1179680 | tf_op jit(solution)/shard_map/ppermute | solution.py:394
  243.4 2.7 add_part.7.acc_ref
  246.0 4.5 %collective-permute-done.9.part_ref = f32[3,2,192,512]{3,2,1,0:T(8,128)} collective-permute-done((f32[3,2,192,512]{3,2,1,0:T(8,128)}, f32[3,2,192,512]{3,2,1,0:T(8,128)}, u32[]{:S(2)}, u32[]{:S(2)}) %collective-permute-start.9) | collective-permute-done | bytes 2359328 | tf_op jit(solution)/shard_map/ppermute | solution.py:343
  250.5 3.7 %add_part.8.acc_ref = f32[3,4,192,1024]{3,2,1,0:T(8,128)} custom-call(s32[1]{0:T(128)} %bitcast.7.place_ref, f32[3,2,192,512]{3,2,1,0:T(8,128)} %collective-permute-done.9.part_ref, f32[3,4,192,1024]{3,2,1,0:T(8,128)} %add_part.7.acc_ref), custom_call_target="tpu_custom_call", output_to_operand_aliasing={{}: (2, {})} | custom-call | flops 1024 | bytes 1024 | tf_op jit(solution)/shard_map/add_part/pallas_call | solution.py:302
  254.2 14.4 %collective-permute-done.8.part_ref = f32[3,4,48,1024]{3,2,1,0:T(8,128)} collective-permute-done((f32[3,4,48,1024]{3,2,1,0:T(8,128)}, f32[3,4,48,1024]{3,2,1,0:T(8,128)}, u32[]{:S(2)}, u32[]{:S(2)}) %collective-permute-start.8) | collective-permute-done | bytes 2359328 | tf_op jit(solution)/shard_map/ppermute | solution.py:394
  268.6 4.0 %add_part.9.acc_ref = f32[3,4,192,1024]{3,2,1,0:T(8,128)} custom-call(s32[1]{0:T(128)} %bitcast.place_ref, f32[3,4,48,1024]{3,2,1,0:T(8,128)} %collective-permute-done.8.part_ref, f32[3,4,192,1024]{3,2,1,0:T(8,128)} %add_part.8.acc_ref), custom_call_target="tpu_custom_call", output_to_operand_aliasing={{}: (2, {})} | custom-call | flops 1024 | bytes 1024 | tf_op jit(solution)/shard_map/add_part/pallas_call | solution.py:302
  272.5 3.1 %collective-permute-done.7.part_ref = f32[3,1,192,512]{3,2,1,0:T(8,128)S(1)} collective-permute-done((f32[3,1,192,512]{3,2,1,0:T(8,128)}, f32[3,1,192,512]{3,2,1,0:T(8,128)S(1)}, u32[]{:S(2)}, u32[]{:S(2)}) %collective-permute-start.7) | collective-permute-done | bytes 1179680 | tf_op jit(solution)/shard_map/ppermute | solution.py:343
  276.7 2.4 add_part.10.acc_ref
  279.2 1.7 collective-permute-done.6.part_ref
  281.9 2.7 add_part.11
  (24 shorter events, 9.5 us)
Async XLA Ops:
  0.0 32.9 %collective-permute-start.4 = (f32[3,4,192,1024]{3,2,1,0:T(8,128)}, f32[3,4,192,1024]{3,2,1,0:T(8,128)}, u32[]{:S(2)}, u32[]{:S(2)}) collective-permute-start(f32[3,4,192,1024]{3,2,1,0:T(8,128)} %comp_ref.15), channel_id=1, source_target_pairs={{0,2},{2,0},{4,6},{6,4},{8,10},{10,8},{12,14},{14,12},{16,18},{18,... | collective-permute-start | bytes 28311560 | tf_op jit(solution)/shard_map/ppermute | solution.py:345
  0.1 33.2 %collective-permute-start.5 = (f32[3,4,192,1024]{3,2,1,0:T(8,128)}, f32[3,4,192,1024]{3,2,1,0:T(8,128)}, u32[]{:S(2)}, u32[]{:S(2)}) collective-permute-start(f32[3,4,192,1024]{3,2,1,0:T(8,128)} %vel_ref.15), channel_id=1, source_target_pairs={{0,2},{2,0},{4,6},{6,4},{8,10},{10,8},{12,14},{14,12},{16,18},{18,... | collective-permute-start | bytes 28311560 | tf_op jit(solution)/shard_map/ppermute | solution.py:345
  2.9 64.3 %collective-permute-start.3 = (f32[5,1,192,512]{3,2,1,0:T(8,128)}, f32[5,1,192,512]{3,2,1,0:T(8,128)S(1)}, u32[]{:S(2)}, u32[]{:S(2)}) collective-permute-start(f32[5,1,192,512]{3,2,1,0:T(8,128)} %pack.7), channel_id=1, source_target_pairs={{0,1},{1,0},{2,3},{3,2},{4,5},{5,4},{6,7},{7,6},{8,9},{9,8},{10,11... | collective-permute-start | bytes 5898248 | tf_op jit(solution)/shard_map/ppermute | solution.py:343
  7.8 121.8 %collective-permute-start.2 = (f32[5,4,24,1024]{3,2,1,0:T(8,128)}, f32[5,4,24,1024]{3,2,1,0:T(8,128)}, u32[]{:S(2)}, u32[]{:S(2)}) collective-permute-start(f32[5,4,24,1024]{3,2,1,0:T(8,128)} %pack.6), channel_id=1, source_target_pairs={{0,30},{2,4},{4,2},{6,8},{8,6},{10,12},{12,10},{14,16},{16,14},{18... | collective-permute-start | bytes 5898248 | tf_op jit(solution)/shard_map/ppermute | solution.py:361
  15.0 159.6 %collective-permute-start.1 = (f32[5,3,192,512]{3,2,1,0:T(8,128)}, f32[5,3,192,512]{3,2,1,0:T(8,128)}, u32[]{:S(2)}, u32[]{:S(2)}) collective-permute-start(f32[5,3,192,512]{3,2,1,0:T(8,128)} %pack.5), channel_id=1, source_target_pairs={{0,1},{1,0},{2,3},{3,2},{4,5},{5,4},{6,7},{7,6},{8,9},{9,8},{10,11... | collective-permute-start | bytes 17694728 | tf_op jit(solution)/shard_map/ppermute | solution.py:343
  32.9 159.9 %collective-permute-start = (f32[5,4,72,1024]{3,2,1,0:T(8,128)}, f32[5,4,72,1024]{3,2,1,0:T(8,128)}, u32[]{:S(2)}, u32[]{:S(2)}) collective-permute-start(f32[5,4,72,1024]{3,2,1,0:T(8,128)} %pack.4), channel_id=1, source_target_pairs={{0,30},{2,4},{4,2},{6,8},{8,6},{10,12},{12,10},{14,16},{16,14},{18... | collective-permute-start | bytes 17694728 | tf_op jit(solution)/shard_map/ppermute | solution.py:361
  67.2 1.3 copy-start.2
  74.7 140.4 %collective-permute-start.11 = (f32[3,1,192,512]{3,2,1,0:T(8,128)}, f32[3,1,192,512]{3,2,1,0:T(8,128)}, u32[]{:S(2)}, u32[]{:S(2)}) collective-permute-start(f32[3,1,192,512]{3,2,1,0:T(8,128)} %get-tuple-element.27), channel_id=1, source_target_pairs={{0,1},{1,0},{2,3},{3,2},{4,5},{5,4},{6,7},{7,6},{8,9},{9,8},{10,11... | collective-permute-start | bytes 3538952 | tf_op jit(solution)/shard_map/ppermute | solution.py:343
  135.3 108.0 %collective-permute-start.10 = (f32[3,4,24,1024]{3,2,1,0:T(8,128)}, f32[3,4,24,1024]{3,2,1,0:T(8,128)}, u32[]{:S(2)}, u32[]{:S(2)}) collective-permute-start(f32[3,4,24,1024]{3,2,1,0:T(8,128)} %get-tuple-element.26), channel_id=1, source_target_pairs={{0,30},{2,4},{4,2},{6,8},{8,6},{10,12},{12,10},{14,16},{16,14},{18... | collective-permute-start | bytes 3538952 | tf_op jit(solution)/shard_map/ppermute | solution.py:394
  184.8 65.7 %collective-permute-start.9 = (f32[3,2,192,512]{3,2,1,0:T(8,128)}, f32[3,2,192,512]{3,2,1,0:T(8,128)}, u32[]{:S(2)}, u32[]{:S(2)}) collective-permute-start(f32[3,2,192,512]{3,2,1,0:T(8,128)} %get-tuple-element.25), channel_id=1, source_target_pairs={{0,1},{1,0},{2,3},{3,2},{4,5},{5,4},{6,7},{7,6},{8,9},{9,8},{10,11... | collective-permute-start | bytes 7077896 | tf_op jit(solution)/shard_map/ppermute | solution.py:343
  201.5 67.1 %collective-permute-start.8 = (f32[3,4,48,1024]{3,2,1,0:T(8,128)}, f32[3,4,48,1024]{3,2,1,0:T(8,128)}, u32[]{:S(2)}, u32[]{:S(2)}) collective-permute-start(f32[3,4,48,1024]{3,2,1,0:T(8,128)} %get-tuple-element.24), channel_id=1, source_target_pairs={{0,30},{2,4},{4,2},{6,8},{8,6},{10,12},{12,10},{14,16},{16,14},{18... | collective-permute-start | bytes 7077896 | tf_op jit(solution)/shard_map/ppermute | solution.py:394
  209.2 66.5 %collective-permute-start.7 = (f32[3,1,192,512]{3,2,1,0:T(8,128)}, f32[3,1,192,512]{3,2,1,0:T(8,128)S(1)}, u32[]{:S(2)}, u32[]{:S(2)}) collective-permute-start(f32[3,1,192,512]{3,2,1,0:T(8,128)} %get-tuple-element.23), channel_id=1, source_target_pairs={{0,1},{1,0},{2,3},{3,2},{4,5},{5,4},{6,7},{7,6},{8,9},{9,8},{10,11... | collective-permute-start | bytes 3538952 | tf_op jit(solution)/shard_map/ppermute | solution.py:343
  215.1 65.8 %collective-permute-start.6 = (f32[3,4,24,1024]{3,2,1,0:T(8,128)}, f32[3,4,24,1024]{3,2,1,0:T(8,128)S(1)}, u32[]{:S(2)}, u32[]{:S(2)}) collective-permute-start(f32[3,4,24,1024]{3,2,1,0:T(8,128)} %get-tuple-element.22), channel_id=1, source_target_pairs={{0,30},{2,4},{4,2},{6,8},{8,6},{10,12},{12,10},{14,16},{16,14},{18... | collective-permute-start | bytes 3538952 | tf_op jit(solution)/shard_map/ppermute | solution.py:394
  275.7 1.0 copy-start
  280.9 1.0 copy-start.1

commit v4 on v3

--- a/solution.py
+++ b/solution.py
@@ -14,7 +14,7 @@
 relax_rate = 1.0 / 0.04
 courant = 0.5
 row_block = 8
-share_weights = ((1,), (2, 1))
+share_weights = ((3,), (7, 2))
 vmem_bytes = 56 * 1024 * 1024
 
 
@@ -307,7 +307,7 @@
         input_output_aliases={2: 0},
         scratch_shapes=[pltpu.VMEM(part.shape, jnp.float32)] * 2
         + [pltpu.SemaphoreType.DMA((3, part.shape[0] * part.shape[1]))],
-        compiler_params=params(),
+        compiler_params=pltpu.CompilerParams(vmem_limit_bytes=24 * 1024 * 1024),
         cost_estimate=small,
         name="add_part",
     )(place, part, acc)

time: 286 us -> 285 us (level)
    ppermute x3, waiting for transfers between devices: 41.3 us -> 45 us  [shards(): lax.ppermute(back, 'gx', far)]
    ppermute x5, waiting for transfers between devices: 45.5 us -> 42.4 us  [along_yz(): lax.ppermute(x, 'yz', [(i, (i + by) % groups) for i in range(groups)])]
  transfers between devices with their start and end apart: 12 -> 12, of which waited for: 8 -> 7; matrix products, arithmetic and copies ran while one was open for 5% -> 5% of each run, Pallas kernels for 37% -> 38%
where the time goes in v4:
time: 285 us; the launch traced here: 284 us
  waiting for transfers between devices  148 us (52%)
  Pallas kernels  110 us (39%)
  other arithmetic  12.1 us (4%)
  starting transfers between devices  11.5 us (4%)
    ppermute x2, waiting for transfers between devices, shards(): borders.append(lax.ppermute(packed[-1], 'gx', far))  60.7 us
    ppermute x3, waiting for transfers between devices, shards(): lax.ppermute(back, 'gx', far)  45 us
    ppermute x5, waiting for transfers between devices, along_yz(): lax.ppermute(x, 'yz', [(i, (i + by) % groups) for i in range(groups)])  42.4 us
    pallas_call x1, Pallas kernels, first_part(): pl.pallas_call(functools.partial(first_kernel, coeffs, lanes), grid_spec=...  33.2 us
    pallas_call x3, Pallas kernels, wall_part(): pl.pallas_call(functools.partial(wall_kernel, groups, rows), grid_spec=gr...  22.6 us
    pallas_call x3, Pallas kernels, border_part(): pl.pallas_call(functools.partial(border_kernel, coeffs, returns, lanes),...  20.1 us
    pallas_call x6, Pallas kernels, add_part(): pl.pallas_call(functools.partial(add_kernel, first, row, row_unit, lane_u...  18.5 us
    pallas_call x4, Pallas kernels, pack(): pl.pallas_call(functools.partial(pack_kernel, boxes), in_specs=[pl.BlockS...  15.5 us
  transfers between devices with their start and end apart: 12, of which 7 were waited for; matrix products, arithmetic and copies ran while one was open for 5% of the time, Pallas kernels for 38%

profile of v4, /device:TPU:1, one launch (start us, length us, event | category | flops | bytes accessed | tf_op | source)
XLA Modules:
  0.0 283.7 jit_solution(14838640439359990435)
XLA Ops:
  0.5 2.4 pack.7
  2.9 2.3 collective-permute-start.3
  5.2 2.6 pack.6
  7.8 1.9 collective-permute-start.2
  9.8 5.2 %pack.5 = f32[5,3,192,512]{3,2,1,0:T(8,128)} custom-call(s32[1]{0:T(128)} %bitcast.3.place_ref, f32[3,4,192,1024]{3,2,1,0:T(8,128)} %comp_ref.15, f32[3,4,192,1024]{3,2,1,0:T(8,128)} %vel_ref.15), custom_call_target="tpu_custom_call" | custom-call | flops 1024 | bytes 1024 | tf_op jit(solution)/shard_map/pack/pallas_call | solution.py:116
  15.3 5.3 %pack.4 = f32[5,4,72,1024]{3,2,1,0:T(8,128)} custom-call(s32[1]{0:T(128)} %bitcast.place_ref, f32[3,4,192,1024]{3,2,1,0:T(8,128)} %comp_ref.15, f32[3,4,192,1024]{3,2,1,0:T(8,128)} %vel_ref.15), custom_call_target="tpu_custom_call" | custom-call | flops 1024 | bytes 1024 | tf_op jit(solution)/shard_map/pack/pallas_call | solution.py:116
  22.0 4.8 %fusion.11 = f32[384]{0:T(512)S(1)} fusion(f32[384]{0:T(512)S(1)} %get-tuple-element.34, s32[384]{0:T(512)S(1)} %fusion.14), kind=kLoop, calls=%fused_computation.25 | loop fusion | flops 4275840 | bytes 4608 | tf_op jit(solution)/shard_map/reduce_sum | solution.py:32
  26.9 5.0 %reduce-precision_convert_fusion = (bf16[384,384]{1,0:T(8,128)(2,1)S(1)}, bf16[384,384]{1,0:T(8,128)(2,1)S(1)}) fusion(f32[384]{0:T(512)S(1)} %fusion.11, f32[384]{0:T(512)S(1)} %get-tuple-element.33, f32[384]{0:T(512)S(1)} %get-tuple-element.34, s32[384]{0:T(512)S(1)} %fusion.14), kind=kLoop, calls=%fused_computation.8 | loop fusion | flops 5455872 | bytes 595968 | tf_op jit(solution)/shard_map/convert
  33.9 33.2 %first_part.1.refs_5_ = f32[3,4,192,1024]{3,2,1,0:T(8,128)} custom-call(s32[1]{0:T(128)} %bitcast.6.flag_ref, f32[192,128]{1,0:T(8,128)} %broadcast_in_dim.48.step_ref, f32[3,4,192,1024]{3,2,1,0:T(8,128)} %comp_ref.15, f32[3,4,192,1024]{3,2,1,0:T(8,128)} %vel_ref.15, f32[3,4,192,1024]{3,2,1,0:T(8,128)} %collective-permute-done.4.comp_near, ...), custom_call_target="tpu_custom_call" | custom-call | flops 1024 | bytes 1024 | tf_op jit(solution)/shard_map/first_part/pallas_call | solution.py:264
  67.1 1.3 copy-done
  68.4 6.2 %wall_part.3 = (f32[3,4,192,1024]{3,2,1,0:T(8,128)}, f32[3,1,192,512]{3,2,1,0:T(8,128)}) custom-call(s32[1]{0:T(128)} %bitcast.2.refs_0_, f32[3,4,192,1024]{3,2,1,0:T(8,128)} %comp_ref.15, f32[3,4,192,1024]{3,2,1,0:T(8,128)} %vel_ref.15, f32[5,1,192,512]{3,2,1,0:T(8,128)} %copy-done, ...), custom_call_target="tpu_custom_call", output_to_operand_aliasing={{0}: (5, {})} | custom-call | flops 99999997952 | bytes 1024 | tf_op jit(solution)/shard_map/wall_part/pallas_call | solution.py:178
  74.6 1.2 collective-permute-start.11
  75.9 53.8 %collective-permute-done.2.refs_0_ = f32[5,4,24,1024]{3,2,1,0:T(8,128)} collective-permute-done((f32[5,4,24,1024]{3,2,1,0:T(8,128)}, f32[5,4,24,1024]{3,2,1,0:T(8,128)}, u32[]{:S(2)}, u32[]{:S(2)}) %collective-permute-start.2) | collective-permute-done | bytes 1966112 | tf_op jit(solution)/shard_map/ppermute | solution.py:361
  129.6 5.7 %border_part.3 = (f32[3,4,192,1024]{3,2,1,0:T(8,128)}, f32[3,4,24,1024]{3,2,1,0:T(8,128)}) custom-call(s32[2]{0:T(128)} %pad_add_fusion.2.flag_ref, f32[192,128]{1,0:T(8,128)} %broadcast_in_dim.48.step_ref, f32[3,4,192,1024]{3,2,1,0:T(8,128)} %comp_ref.15, f32[3,4,192,1024]{3,2,1,0:T(8,128)} %vel_ref.15, ...), custom_call_target="tpu_custom_call", output_to_operand_aliasing={{0}: (5, {})} | custom-call | flops 99999997952 | bytes 1024 | tf_op jit(solution)/shard_map/border_part/pallas_call | solution.py:235
  135.3 1.4 collective-permute-start.10
  136.8 37.9 %collective-permute-done.1.refs_3_ = f32[5,3,192,512]{3,2,1,0:T(8,128)} collective-permute-done((f32[5,3,192,512]{3,2,1,0:T(8,128)}, f32[5,3,192,512]{3,2,1,0:T(8,128)}, u32[]{:S(2)}, u32[]{:S(2)}) %collective-permute-start.1) | collective-permute-done | bytes 5898272 | tf_op jit(solution)/shard_map/ppermute | solution.py:343
  174.7 10.1 %wall_part.4 = (f32[3,4,192,1024]{3,2,1,0:T(8,128)}, f32[3,2,192,512]{3,2,1,0:T(8,128)}) custom-call(s32[1]{0:T(128)} %bitcast.2.refs_0_, f32[3,4,192,1024]{3,2,1,0:T(8,128)} %comp_ref.15, f32[3,4,192,1024]{3,2,1,0:T(8,128)} %vel_ref.15, f32[5,3,192,512]{3,2,1,0:T(8,128)} %collective-permute-done.1.refs_3_, ...), custom_call_target="tpu_custom_call", output_to_operand_aliasing={{0}: (5, {})} | custom-call | flops 99999997952 | bytes 1024 | tf_op jit(solution)/shard_map/wall_part/pallas_call | solution.py:178
  185.9 6.9 %collective-permute-done.refs_0_ = f32[5,4,72,1024]{3,2,1,0:T(8,128)} collective-permute-done((f32[5,4,72,1024]{3,2,1,0:T(8,128)}, f32[5,4,72,1024]{3,2,1,0:T(8,128)}, u32[]{:S(2)}, u32[]{:S(2)}) %collective-permute-start) | collective-permute-done | bytes 5898272 | tf_op jit(solution)/shard_map/ppermute | solution.py:361
  192.8 10.5 %border_part.4 = (f32[3,4,192,1024]{3,2,1,0:T(8,128)}, f32[3,4,56,1024]{3,2,1,0:T(8,128)}) custom-call(s32[2]{0:T(128)} %get-tuple-element.32.flag_ref, f32[192,128]{1,0:T(8,128)} %broadcast_in_dim.48.step_ref, f32[3,4,192,1024]{3,2,1,0:T(8,128)} %comp_ref.15, f32[3,4,192,1024]{3,2,1,0:T(8,128)} %vel_ref.15, ...), custom_call_target="tpu_custom_call", output_to_operand_aliasing={{0}: (5, {})} | custom-call | flops 99999997952 | bytes 1024 | tf_op jit(solution)/shard_map/border_part/pallas_call | solution.py:235
  203.3 1.4 collective-permute-start.8
  204.7 6.2 %wall_part.5 = (f32[3,4,192,1024]{3,2,1,0:T(8,128)}, f32[3,1,192,512]{3,2,1,0:T(8,128)}) custom-call(s32[1]{0:T(128)} %bitcast.2.refs_0_, f32[3,4,192,1024]{3,2,1,0:T(8,128)} %comp_ref.15, f32[3,4,192,1024]{3,2,1,0:T(8,128)} %vel_ref.15, f32[5,3,192,512]{3,2,1,0:T(8,128)} %collective-permute-done.1.refs_3_, ...), custom_call_target="tpu_custom_call", output_to_operand_aliasing={{0}: (5, {})} | custom-call | flops 99999997952 | bytes 1024 | tf_op jit(solution)/shard_map/wall_part/pallas_call | solution.py:178
  211.2 3.9 %border_part.5 = (f32[3,4,192,1024]{3,2,1,0:T(8,128)}, f32[3,4,16,1024]{3,2,1,0:T(8,128)}) custom-call(s32[2]{0:T(128)} %get-tuple-element.31.flag_ref, f32[192,128]{1,0:T(8,128)} %broadcast_in_dim.48.step_ref, f32[3,4,192,1024]{3,2,1,0:T(8,128)} %comp_ref.15, f32[3,4,192,1024]{3,2,1,0:T(8,128)} %vel_ref.15, ...), custom_call_target="tpu_custom_call", output_to_operand_aliasing={{0}: (5, {})} | custom-call | flops 99999997952 | bytes 1024 | tf_op jit(solution)/shard_map/border_part/pallas_call | solution.py:235
  215.7 2.4 add_part.6.acc_ref
  218.2 25.2 %collective-permute-done.10.part_ref = f32[3,4,24,1024]{3,2,1,0:T(8,128)} collective-permute-done((f32[3,4,24,1024]{3,2,1,0:T(8,128)}, f32[3,4,24,1024]{3,2,1,0:T(8,128)}, u32[]{:S(2)}, u32[]{:S(2)}) %collective-permute-start.10) | collective-permute-done | bytes 1179680 | tf_op jit(solution)/shard_map/ppermute | solution.py:394
  243.4 2.7 add_part.7.acc_ref
  246.0 4.5 %collective-permute-done.9.part_ref = f32[3,2,192,512]{3,2,1,0:T(8,128)} collective-permute-done((f32[3,2,192,512]{3,2,1,0:T(8,128)}, f32[3,2,192,512]{3,2,1,0:T(8,128)}, u32[]{:S(2)}, u32[]{:S(2)}) %collective-permute-start.9) | collective-permute-done | bytes 2359328 | tf_op jit(solution)/shard_map/ppermute | solution.py:343
  250.5 3.7 %add_part.8.acc_ref = f32[3,4,192,1024]{3,2,1,0:T(8,128)} custom-call(s32[1]{0:T(128)} %bitcast.7.place_ref, f32[3,2,192,512]{3,2,1,0:T(8,128)} %collective-permute-done.9.part_ref, f32[3,4,192,1024]{3,2,1,0:T(8,128)} %add_part.7.acc_ref), custom_call_target="tpu_custom_call", output_to_operand_aliasing={{}: (2, {})} | custom-call | flops 1024 | bytes 1024 | tf_op jit(solution)/shard_map/add_part/pallas_call | solution.py:302
  254.2 18.6 %collective-permute-done.8.part_ref = f32[3,4,56,1024]{3,2,1,0:T(8,128)} collective-permute-done((f32[3,4,56,1024]{3,2,1,0:T(8,128)}, f32[3,4,56,1024]{3,2,1,0:T(8,128)}, u32[]{:S(2)}, u32[]{:S(2)}) %collective-permute-start.8) | collective-permute-done | bytes 2752544 | tf_op jit(solution)/shard_map/ppermute | solution.py:394
  272.8 4.4 %add_part.9.acc_ref = f32[3,4,192,1024]{3,2,1,0:T(8,128)} custom-call(s32[1]{0:T(128)} %bitcast.place_ref, f32[3,4,56,1024]{3,2,1,0:T(8,128)} %collective-permute-done.8.part_ref, f32[3,4,192,1024]{3,2,1,0:T(8,128)} %add_part.8.acc_ref), custom_call_target="tpu_custom_call", output_to_operand_aliasing={{}: (2, {})} | custom-call | flops 1024 | bytes 1024 | tf_op jit(solution)/shard_map/add_part/pallas_call | solution.py:302
  277.1 2.5 add_part.10.acc_ref
  279.6 1.3 collective-permute-done.6.part_ref
  280.9 2.9 %add_part.11 = f32[3,4,192,1024]{3,2,1,0:T(8,128)} custom-call(s32[1]{0:T(128)} %bitcast.place_ref, f32[3,4,16,1024]{3,2,1,0:T(8,128)S(1)} %collective-permute-done.6.part_ref, f32[3,4,192,1024]{3,2,1,0:T(8,128)} %add_part.10.acc_ref), custom_call_target="tpu_custom_call", output_to_operand_aliasing={{}: (2, {})} | custom-call | flops 1024 | bytes 1024 | tf_op jit(solution)/shard_map/add_part/pallas_call | solution.py:302
  (20 shorter events, 6.2 us)
Async XLA Ops:
  0.0 32.9 %collective-permute-start.4 = (f32[3,4,192,1024]{3,2,1,0:T(8,128)}, f32[3,4,192,1024]{3,2,1,0:T(8,128)}, u32[]{:S(2)}, u32[]{:S(2)}) collective-permute-start(f32[3,4,192,1024]{3,2,1,0:T(8,128)} %comp_ref.15), channel_id=1, source_target_pairs={{0,2},{2,0},{4,6},{6,4},{8,10},{10,8},{12,14},{14,12},{16,18},{18,... | collective-permute-start | bytes 28311560 | tf_op jit(solution)/shard_map/ppermute | solution.py:345
  0.1 33.1 %collective-permute-start.5 = (f32[3,4,192,1024]{3,2,1,0:T(8,128)}, f32[3,4,192,1024]{3,2,1,0:T(8,128)}, u32[]{:S(2)}, u32[]{:S(2)}) collective-permute-start(f32[3,4,192,1024]{3,2,1,0:T(8,128)} %vel_ref.15), channel_id=1, source_target_pairs={{0,2},{2,0},{4,6},{6,4},{8,10},{10,8},{12,14},{14,12},{16,18},{18,... | collective-permute-start | bytes 28311560 | tf_op jit(solution)/shard_map/ppermute | solution.py:345
  2.9 64.2 %collective-permute-start.3 = (f32[5,1,192,512]{3,2,1,0:T(8,128)}, f32[5,1,192,512]{3,2,1,0:T(8,128)S(1)}, u32[]{:S(2)}, u32[]{:S(2)}) collective-permute-start(f32[5,1,192,512]{3,2,1,0:T(8,128)} %pack.7), channel_id=1, source_target_pairs={{0,1},{1,0},{2,3},{3,2},{4,5},{5,4},{6,7},{7,6},{8,9},{9,8},{10,11... | collective-permute-start | bytes 5898248 | tf_op jit(solution)/shard_map/ppermute | solution.py:343
  7.8 121.8 %collective-permute-start.2 = (f32[5,4,24,1024]{3,2,1,0:T(8,128)}, f32[5,4,24,1024]{3,2,1,0:T(8,128)}, u32[]{:S(2)}, u32[]{:S(2)}) collective-permute-start(f32[5,4,24,1024]{3,2,1,0:T(8,128)} %pack.6), channel_id=1, source_target_pairs={{0,30},{2,4},{4,2},{6,8},{8,6},{10,12},{12,10},{14,16},{16,14},{18... | collective-permute-start | bytes 5898248 | tf_op jit(solution)/shard_map/ppermute | solution.py:361
  15.0 159.6 %collective-permute-start.1 = (f32[5,3,192,512]{3,2,1,0:T(8,128)}, f32[5,3,192,512]{3,2,1,0:T(8,128)}, u32[]{:S(2)}, u32[]{:S(2)}) collective-permute-start(f32[5,3,192,512]{3,2,1,0:T(8,128)} %pack.5), channel_id=1, source_target_pairs={{0,1},{1,0},{2,3},{3,2},{4,5},{5,4},{6,7},{7,6},{8,9},{9,8},{10,11... | collective-permute-start | bytes 17694728 | tf_op jit(solution)/shard_map/ppermute | solution.py:343
  32.9 159.9 %collective-permute-start = (f32[5,4,72,1024]{3,2,1,0:T(8,128)}, f32[5,4,72,1024]{3,2,1,0:T(8,128)}, u32[]{:S(2)}, u32[]{:S(2)}) collective-permute-start(f32[5,4,72,1024]{3,2,1,0:T(8,128)} %pack.4), channel_id=1, source_target_pairs={{0,30},{2,4},{4,2},{6,8},{8,6},{10,12},{12,10},{14,16},{16,14},{18... | collective-permute-start | bytes 17694728 | tf_op jit(solution)/shard_map/ppermute | solution.py:361
  67.1 1.3 copy-start
  74.6 140.5 %collective-permute-start.11 = (f32[3,1,192,512]{3,2,1,0:T(8,128)}, f32[3,1,192,512]{3,2,1,0:T(8,128)}, u32[]{:S(2)}, u32[]{:S(2)}) collective-permute-start(f32[3,1,192,512]{3,2,1,0:T(8,128)} %get-tuple-element.27), channel_id=1, source_target_pairs={{0,1},{1,0},{2,3},{3,2},{4,5},{5,4},{6,7},{7,6},{8,9},{9,8},{10,11... | collective-permute-start | bytes 3538952 | tf_op jit(solution)/shard_map/ppermute | solution.py:343
  135.3 108.0 %collective-permute-start.10 = (f32[3,4,24,1024]{3,2,1,0:T(8,128)}, f32[3,4,24,1024]{3,2,1,0:T(8,128)}, u32[]{:S(2)}, u32[]{:S(2)}) collective-permute-start(f32[3,4,24,1024]{3,2,1,0:T(8,128)} %get-tuple-element.26), channel_id=1, source_target_pairs={{0,30},{2,4},{4,2},{6,8},{8,6},{10,12},{12,10},{14,16},{16,14},{18... | collective-permute-start | bytes 3538952 | tf_op jit(solution)/shard_map/ppermute | solution.py:394
  184.8 65.7 %collective-permute-start.9 = (f32[3,2,192,512]{3,2,1,0:T(8,128)}, f32[3,2,192,512]{3,2,1,0:T(8,128)}, u32[]{:S(2)}, u32[]{:S(2)}) collective-permute-start(f32[3,2,192,512]{3,2,1,0:T(8,128)} %get-tuple-element.25), channel_id=1, source_target_pairs={{0,1},{1,0},{2,3},{3,2},{4,5},{5,4},{6,7},{7,6},{8,9},{9,8},{10,11... | collective-permute-start | bytes 7077896 | tf_op jit(solution)/shard_map/ppermute | solution.py:343
  203.3 69.4 %collective-permute-start.8 = (f32[3,4,56,1024]{3,2,1,0:T(8,128)}, f32[3,4,56,1024]{3,2,1,0:T(8,128)}, u32[]{:S(2)}, u32[]{:S(2)}) collective-permute-start(f32[3,4,56,1024]{3,2,1,0:T(8,128)} %get-tuple-element.24), channel_id=1, source_target_pairs={{0,30},{2,4},{4,2},{6,8},{8,6},{10,12},{12,10},{14,16},{16,14},{18... | collective-permute-start | bytes 8257544 | tf_op jit(solution)/shard_map/ppermute | solution.py:394
  211.0 66.2 %collective-permute-start.7 = (f32[3,1,192,512]{3,2,1,0:T(8,128)}, f32[3,1,192,512]{3,2,1,0:T(8,128)S(1)}, u32[]{:S(2)}, u32[]{:S(2)}) collective-permute-start(f32[3,1,192,512]{3,2,1,0:T(8,128)} %get-tuple-element.23), channel_id=1, source_target_pairs={{0,1},{1,0},{2,3},{3,2},{4,5},{5,4},{6,7},{7,6},{8,9},{9,8},{10,11... | collective-permute-start | bytes 3538952 | tf_op jit(solution)/shard_map/ppermute | solution.py:343
  215.1 65.8 %collective-permute-start.6 = (f32[3,4,16,1024]{3,2,1,0:T(8,128)}, f32[3,4,16,1024]{3,2,1,0:T(8,128)S(1)}, u32[]{:S(2)}, u32[]{:S(2)}) collective-permute-start(f32[3,4,16,1024]{3,2,1,0:T(8,128)} %get-tuple-element.22), channel_id=1, source_target_pairs={{0,30},{2,4},{4,2},{6,8},{8,6},{10,12},{12,10},{14,16},{16,14},{18... | collective-permute-start | bytes 2359304 | tf_op jit(solution)/shard_map/ppermute | solution.py:394

commit v5 on v4

--- a/solution.py
+++ b/solution.py
@@ -89,8 +89,8 @@
             out_ref[f, i] = comp[f] + step * (terms[f] - w * along_z[f] - relax)
 
 
-def pack_kernel(boxes, place_ref, comp_ref, vel_ref, *refs):
-    outs, held, sems = refs[: len(boxes)], refs[len(boxes) : -1], refs[-1]
+def pack_kernel(boxes, direct, place_ref, comp_ref, vel_ref, *refs):
+    outs, held, sems = refs[: len(boxes)], refs[: len(boxes)] if direct else refs[len(boxes) : -1], refs[-1]
     loads, stores = [], []
     for j, (plane, n_planes, row, row_unit, n_rows, lane_unit, n_lanes) in enumerate(boxes):
         rows = pl.ds(pl.multiple_of(place_ref[j] * row_unit + row, row_block), n_rows)
@@ -100,25 +100,27 @@
                 for p in range(n_planes):
                     k, to = len(loads), (first + f, p)
                     loads.append(pltpu.make_async_copy(source.at[f, plane + p, rows, lanes], held[j].at[to], sems.at[0, k]))
-                    stores.append(pltpu.make_async_copy(held[j].at[to], outs[j].at[to], sems.at[1, k]))
+                    if not direct:
+                        stores.append(pltpu.make_async_copy(held[j].at[to], outs[j].at[to], sems.at[1, k]))
     for load in loads:
         load.start()
-    for load, store in zip(loads, stores):
+    for k, load in enumerate(loads):
         load.wait()
-        store.start()
+        if not direct:
+            stores[k].start()
     for store in stores:
         store.wait()
 
 
-def pack(places, boxes, comp, vel):
+def pack(places, boxes, direct, comp, vel):
     here = pl.BlockSpec(memory_space=pltpu.HBM)
     shapes = [(5, planes, rows, lanes) for _, planes, _, _, rows, _, lanes in boxes]
     return pl.pallas_call(
-        functools.partial(pack_kernel, boxes),
+        functools.partial(pack_kernel, boxes, direct),
         in_specs=[pl.BlockSpec(memory_space=pltpu.SMEM), here, here],
-        out_specs=[here] * len(boxes),
-        out_shape=[jax.ShapeDtypeStruct(shape, jnp.float32) for shape in shapes],
-        scratch_shapes=[pltpu.VMEM(shape, jnp.float32) for shape in shapes]
+        out_specs=[pl.BlockSpec(memory_space=pltpu.VMEM) if direct else here] * len(boxes),
+        out_shape=[pltpu.VMEM(shape, jnp.float32) if direct else jax.ShapeDtypeStruct(shape, jnp.float32) for shape in shapes],
+        scratch_shapes=[pltpu.VMEM(shape, jnp.float32) for shape in shapes if not direct]
         + [pltpu.SemaphoreType.DMA((2, sum(5 * shape[1] for shape in shapes)))],
         compiler_params=params(),
         cost_estimate=small,
@@ -353,7 +355,7 @@
             places.append(odd)
             boxes.append((0, planes, row, half, n_rows, 0, lanes))
         packed = [
-            pack(place.astype(jnp.int32).reshape(1), [box], conformation, velocity)[0] for place, box in zip(places, boxes)
+            pack(place.astype(jnp.int32).reshape(1), [box], k == 0 and box[-2] > 0, conformation, velocity)[0] for place, box in zip(places, boxes)
         ]
         if k < len(wall_cuts):
             walls.append([along_yz(packed[g - 1], g) for g in range(1, groups)][::-1])

time: 285 us -> 284 us (level)
  no operation moved by 1% of the time
where the time goes in v5:
time: 284 us; the launch traced here: 283 us
  waiting for transfers between devices  149 us (52%)
  Pallas kernels  109 us (38%)
  other arithmetic  12.1 us (4%)
  starting transfers between devices  11.5 us (4%)
    ppermute x2, waiting for transfers between devices, shards(): borders.append(lax.ppermute(packed[-1], 'gx', far))  62.1 us
    ppermute x3, waiting for transfers between devices, shards(): lax.ppermute(back, 'gx', far)  45.1 us
    ppermute x5, waiting for transfers between devices, along_yz(): lax.ppermute(x, 'yz', [(i, (i + by) % groups) for i in range(groups)])  41.9 us
    pallas_call x1, Pallas kernels, first_part(): pl.pallas_call(functools.partial(first_kernel, coeffs, lanes), grid_spec=...  33.2 us
    pallas_call x3, Pallas kernels, wall_part(): pl.pallas_call(functools.partial(wall_kernel, groups, rows), grid_spec=gr...  22.6 us
    pallas_call x3, Pallas kernels, border_part(): pl.pallas_call(functools.partial(border_kernel, coeffs, returns, lanes),...  20.3 us
    pallas_call x6, Pallas kernels, add_part(): pl.pallas_call(functools.partial(add_kernel, first, row, row_unit, lane_u...  18.5 us
    pallas_call x4, Pallas kernels, pack(): pl.pallas_call(functools.partial(pack_kernel, boxes, direct), in_specs=[p...  14.7 us
  transfers between devices with their start and end apart: 12, of which 7 were waited for; matrix products, arithmetic and copies ran while one was open for 5% of the time, Pallas kernels for 38%

profile of v5, /device:TPU:1, one launch (start us, length us, event | category | flops | bytes accessed | tf_op | source)
XLA Modules:
  0.0 282.9 jit_solution(736629825838622385)
XLA Ops:
  0.5 1.6 pack.7
  2.1 2.3 collective-permute-start.3
  4.4 2.6 pack.6
  7.0 1.9 collective-permute-start.2
  9.0 5.2 %pack.5 = f32[5,3,192,512]{3,2,1,0:T(8,128)} custom-call(s32[1]{0:T(128)} %bitcast.3.place_ref, f32[3,4,192,1024]{3,2,1,0:T(8,128)} %comp_ref.15, f32[3,4,192,1024]{3,2,1,0:T(8,128)} %vel_ref.15), custom_call_target="tpu_custom_call" | custom-call | flops 1024 | bytes 1024 | tf_op jit(solution)/shard_map/pack/pallas_call | solution.py:118
  14.5 5.3 %pack.4 = f32[5,4,72,1024]{3,2,1,0:T(8,128)} custom-call(s32[1]{0:T(128)} %bitcast.place_ref, f32[3,4,192,1024]{3,2,1,0:T(8,128)} %comp_ref.15, f32[3,4,192,1024]{3,2,1,0:T(8,128)} %vel_ref.15), custom_call_target="tpu_custom_call" | custom-call | flops 1024 | bytes 1024 | tf_op jit(solution)/shard_map/pack/pallas_call | solution.py:118
  21.3 4.8 %fusion.11 = f32[384]{0:T(512)S(1)} fusion(f32[384]{0:T(512)S(1)} %get-tuple-element.34, s32[384]{0:T(512)S(1)} %fusion.14), kind=kLoop, calls=%fused_computation.25 | loop fusion | flops 4275840 | bytes 4608 | tf_op jit(solution)/shard_map/reduce_sum | solution.py:32
  26.1 5.0 %reduce-precision_convert_fusion = (bf16[384,384]{1,0:T(8,128)(2,1)S(1)}, bf16[384,384]{1,0:T(8,128)(2,1)S(1)}) fusion(f32[384]{0:T(512)S(1)} %fusion.11, f32[384]{0:T(512)S(1)} %get-tuple-element.33, f32[384]{0:T(512)S(1)} %get-tuple-element.34, s32[384]{0:T(512)S(1)} %fusion.14), kind=kLoop, calls=%fused_computation.8 | loop fusion | flops 5455872 | bytes 595968 | tf_op jit(solution)/shard_map/convert
  33.1 33.2 %first_part.1.refs_5_ = f32[3,4,192,1024]{3,2,1,0:T(8,128)} custom-call(s32[1]{0:T(128)} %bitcast.6.flag_ref, f32[192,128]{1,0:T(8,128)} %broadcast_in_dim.48.step_ref, f32[3,4,192,1024]{3,2,1,0:T(8,128)} %comp_ref.15, f32[3,4,192,1024]{3,2,1,0:T(8,128)} %vel_ref.15, f32[3,4,192,1024]{3,2,1,0:T(8,128)} %collective-permute-done.4.comp_near, ...), custom_call_target="tpu_custom_call" | custom-call | flops 1024 | bytes 1024 | tf_op jit(solution)/shard_map/first_part/pallas_call | solution.py:266
  66.3 6.3 %wall_part.3 = (f32[3,4,192,1024]{3,2,1,0:T(8,128)}, f32[3,1,192,512]{3,2,1,0:T(8,128)}) custom-call(s32[1]{0:T(128)} %bitcast.2.refs_0_, f32[3,4,192,1024]{3,2,1,0:T(8,128)} %comp_ref.15, f32[3,4,192,1024]{3,2,1,0:T(8,128)} %vel_ref.15, f32[5,1,192,512]{3,2,1,0:T(8,128)} %collective-permute-done.3.refs_3_, ...), custom_call_target="tpu_custom_call", output_to_operand_aliasing={{0}: (5, {})} | custom-call | flops 99999997952 | bytes 1024 | tf_op jit(solution)/shard_map/wall_part/pallas_call | solution.py:180
  72.6 1.2 collective-permute-start.11
  73.9 54.9 %collective-permute-done.2.refs_0_ = f32[5,4,24,1024]{3,2,1,0:T(8,128)} collective-permute-done((f32[5,4,24,1024]{3,2,1,0:T(8,128)}, f32[5,4,24,1024]{3,2,1,0:T(8,128)}, u32[]{:S(2)}, u32[]{:S(2)}) %collective-permute-start.2) | collective-permute-done | bytes 1966112 | tf_op jit(solution)/shard_map/ppermute | solution.py:363
  128.8 5.8 %border_part.3 = (f32[3,4,192,1024]{3,2,1,0:T(8,128)}, f32[3,4,24,1024]{3,2,1,0:T(8,128)}) custom-call(s32[2]{0:T(128)} %pad_add_fusion.2.flag_ref, f32[192,128]{1,0:T(8,128)} %broadcast_in_dim.48.step_ref, f32[3,4,192,1024]{3,2,1,0:T(8,128)} %comp_ref.15, f32[3,4,192,1024]{3,2,1,0:T(8,128)} %vel_ref.15, ...), custom_call_target="tpu_custom_call", output_to_operand_aliasing={{0}: (5, {})} | custom-call | flops 99999997952 | bytes 1024 | tf_op jit(solution)/shard_map/border_part/pallas_call | solution.py:237
  134.6 1.4 collective-permute-start.10
  136.0 37.6 %collective-permute-done.1.refs_3_ = f32[5,3,192,512]{3,2,1,0:T(8,128)} collective-permute-done((f32[5,3,192,512]{3,2,1,0:T(8,128)}, f32[5,3,192,512]{3,2,1,0:T(8,128)}, u32[]{:S(2)}, u32[]{:S(2)}) %collective-permute-start.1) | collective-permute-done | bytes 5898272 | tf_op jit(solution)/shard_map/ppermute | solution.py:345
  173.6 10.1 %wall_part.4 = (f32[3,4,192,1024]{3,2,1,0:T(8,128)}, f32[3,2,192,512]{3,2,1,0:T(8,128)}) custom-call(s32[1]{0:T(128)} %bitcast.2.refs_0_, f32[3,4,192,1024]{3,2,1,0:T(8,128)} %comp_ref.15, f32[3,4,192,1024]{3,2,1,0:T(8,128)} %vel_ref.15, f32[5,3,192,512]{3,2,1,0:T(8,128)} %collective-permute-done.1.refs_3_, ...), custom_call_target="tpu_custom_call", output_to_operand_aliasing={{0}: (5, {})} | custom-call | flops 99999997952 | bytes 1024 | tf_op jit(solution)/shard_map/wall_part/pallas_call | solution.py:180
  183.7 1.1 collective-permute-start.9
  184.9 7.1 %collective-permute-done.refs_0_ = f32[5,4,72,1024]{3,2,1,0:T(8,128)} collective-permute-done((f32[5,4,72,1024]{3,2,1,0:T(8,128)}, f32[5,4,72,1024]{3,2,1,0:T(8,128)}, u32[]{:S(2)}, u32[]{:S(2)}) %collective-permute-start) | collective-permute-done | bytes 5898272 | tf_op jit(solution)/shard_map/ppermute | solution.py:363
  192.0 10.5 %border_part.4 = (f32[3,4,192,1024]{3,2,1,0:T(8,128)}, f32[3,4,56,1024]{3,2,1,0:T(8,128)}) custom-call(s32[2]{0:T(128)} %get-tuple-element.32.flag_ref, f32[192,128]{1,0:T(8,128)} %broadcast_in_dim.48.step_ref, f32[3,4,192,1024]{3,2,1,0:T(8,128)} %comp_ref.15, f32[3,4,192,1024]{3,2,1,0:T(8,128)} %vel_ref.15, ...), custom_call_target="tpu_custom_call", output_to_operand_aliasing={{0}: (5, {})} | custom-call | flops 99999997952 | bytes 1024 | tf_op jit(solution)/shard_map/border_part/pallas_call | solution.py:237
  202.5 1.4 collective-permute-start.8
  203.9 6.2 %wall_part.5 = (f32[3,4,192,1024]{3,2,1,0:T(8,128)}, f32[3,1,192,512]{3,2,1,0:T(8,128)}) custom-call(s32[1]{0:T(128)} %bitcast.2.refs_0_, f32[3,4,192,1024]{3,2,1,0:T(8,128)} %comp_ref.15, f32[3,4,192,1024]{3,2,1,0:T(8,128)} %vel_ref.15, f32[5,3,192,512]{3,2,1,0:T(8,128)} %collective-permute-done.1.refs_3_, ...), custom_call_target="tpu_custom_call", output_to_operand_aliasing={{0}: (5, {})} | custom-call | flops 99999997952 | bytes 1024 | tf_op jit(solution)/shard_map/wall_part/pallas_call | solution.py:180
  210.4 4.0 %border_part.5 = (f32[3,4,192,1024]{3,2,1,0:T(8,128)}, f32[3,4,16,1024]{3,2,1,0:T(8,128)}) custom-call(s32[2]{0:T(128)} %get-tuple-element.31.flag_ref, f32[192,128]{1,0:T(8,128)} %broadcast_in_dim.48.step_ref, f32[3,4,192,1024]{3,2,1,0:T(8,128)} %comp_ref.15, f32[3,4,192,1024]{3,2,1,0:T(8,128)} %vel_ref.15, ...), custom_call_target="tpu_custom_call", output_to_operand_aliasing={{0}: (5, {})} | custom-call | flops 99999997952 | bytes 1024 | tf_op jit(solution)/shard_map/border_part/pallas_call | solution.py:237
  215.0 2.4 add_part.6.acc_ref
  217.5 25.1 %collective-permute-done.10.part_ref = f32[3,4,24,1024]{3,2,1,0:T(8,128)} collective-permute-done((f32[3,4,24,1024]{3,2,1,0:T(8,128)}, f32[3,4,24,1024]{3,2,1,0:T(8,128)}, u32[]{:S(2)}, u32[]{:S(2)}) %collective-permute-start.10) | collective-permute-done | bytes 1179680 | tf_op jit(solution)/shard_map/ppermute | solution.py:396
  242.5 2.7 add_part.7.acc_ref
  245.2 4.2 %collective-permute-done.9.part_ref = f32[3,2,192,512]{3,2,1,0:T(8,128)} collective-permute-done((f32[3,2,192,512]{3,2,1,0:T(8,128)}, f32[3,2,192,512]{3,2,1,0:T(8,128)}, u32[]{:S(2)}, u32[]{:S(2)}) %collective-permute-start.9) | collective-permute-done | bytes 2359328 | tf_op jit(solution)/shard_map/ppermute | solution.py:345
  249.5 3.7 %add_part.8.acc_ref = f32[3,4,192,1024]{3,2,1,0:T(8,128)} custom-call(s32[1]{0:T(128)} %bitcast.7.place_ref, f32[3,2,192,512]{3,2,1,0:T(8,128)} %collective-permute-done.9.part_ref, f32[3,4,192,1024]{3,2,1,0:T(8,128)} %add_part.7.acc_ref), custom_call_target="tpu_custom_call", output_to_operand_aliasing={{}: (2, {})} | custom-call | flops 1024 | bytes 1024 | tf_op jit(solution)/shard_map/add_part/pallas_call | solution.py:304
  253.1 18.8 %collective-permute-done.8.part_ref = f32[3,4,56,1024]{3,2,1,0:T(8,128)} collective-permute-done((f32[3,4,56,1024]{3,2,1,0:T(8,128)}, f32[3,4,56,1024]{3,2,1,0:T(8,128)}, u32[]{:S(2)}, u32[]{:S(2)}) %collective-permute-start.8) | collective-permute-done | bytes 2752544 | tf_op jit(solution)/shard_map/ppermute | solution.py:396
  271.9 4.4 %add_part.9.acc_ref = f32[3,4,192,1024]{3,2,1,0:T(8,128)} custom-call(s32[1]{0:T(128)} %bitcast.place_ref, f32[3,4,56,1024]{3,2,1,0:T(8,128)} %collective-permute-done.8.part_ref, f32[3,4,192,1024]{3,2,1,0:T(8,128)} %add_part.8.acc_ref), custom_call_target="tpu_custom_call", output_to_operand_aliasing={{}: (2, {})} | custom-call | flops 1024 | bytes 1024 | tf_op jit(solution)/shard_map/add_part/pallas_call | solution.py:304
  276.3 2.5 add_part.10.acc_ref
  278.8 1.3 collective-permute-done.6.part_ref
  280.1 2.9 %add_part.11 = f32[3,4,192,1024]{3,2,1,0:T(8,128)} custom-call(s32[1]{0:T(128)} %bitcast.place_ref, f32[3,4,16,1024]{3,2,1,0:T(8,128)S(1)} %collective-permute-done.6.part_ref, f32[3,4,192,1024]{3,2,1,0:T(8,128)} %add_part.10.acc_ref), custom_call_target="tpu_custom_call", output_to_operand_aliasing={{}: (2, {})} | custom-call | flops 1024 | bytes 1024 | tf_op jit(solution)/shard_map/add_part/pallas_call | solution.py:304
  (18 shorter events, 5.1 us)
Async XLA Ops:
  0.0 32.1 %collective-permute-start.4 = (f32[3,4,192,1024]{3,2,1,0:T(8,128)}, f32[3,4,192,1024]{3,2,1,0:T(8,128)}, u32[]{:S(2)}, u32[]{:S(2)}) collective-permute-start(f32[3,4,192,1024]{3,2,1,0:T(8,128)} %comp_ref.15), channel_id=1, source_target_pairs={{0,2},{2,0},{4,6},{6,4},{8,10},{10,8},{12,14},{14,12},{16,18},{18,... | collective-permute-start | bytes 28311560 | tf_op jit(solution)/shard_map/ppermute | solution.py:347
  0.1 32.3 %collective-permute-start.5 = (f32[3,4,192,1024]{3,2,1,0:T(8,128)}, f32[3,4,192,1024]{3,2,1,0:T(8,128)}, u32[]{:S(2)}, u32[]{:S(2)}) collective-permute-start(f32[3,4,192,1024]{3,2,1,0:T(8,128)} %vel_ref.15), channel_id=1, source_target_pairs={{0,2},{2,0},{4,6},{6,4},{8,10},{10,8},{12,14},{14,12},{16,18},{18,... | collective-permute-start | bytes 28311560 | tf_op jit(solution)/shard_map/ppermute | solution.py:347
  2.1 64.3 %collective-permute-start.3 = (f32[5,1,192,512]{3,2,1,0:T(8,128)S(1)}, f32[5,1,192,512]{3,2,1,0:T(8,128)}, u32[]{:S(2)}, u32[]{:S(2)}) collective-permute-start(f32[5,1,192,512]{3,2,1,0:T(8,128)S(1)} %pack.7), channel_id=1, source_target_pairs={{0,1},{1,0},{2,3},{3,2},{4,5},{5,4},{6,7},{7,6},{8,9},{9,8},{10,11... | collective-permute-start | bytes 5898248 | tf_op jit(solution)/shard_map/ppermute | solution.py:345
  7.0 121.8 %collective-permute-start.2 = (f32[5,4,24,1024]{3,2,1,0:T(8,128)}, f32[5,4,24,1024]{3,2,1,0:T(8,128)}, u32[]{:S(2)}, u32[]{:S(2)}) collective-permute-start(f32[5,4,24,1024]{3,2,1,0:T(8,128)} %pack.6), channel_id=1, source_target_pairs={{0,30},{2,4},{4,2},{6,8},{8,6},{10,12},{12,10},{14,16},{16,14},{18... | collective-permute-start | bytes 5898248 | tf_op jit(solution)/shard_map/ppermute | solution.py:363
  14.2 159.4 %collective-permute-start.1 = (f32[5,3,192,512]{3,2,1,0:T(8,128)}, f32[5,3,192,512]{3,2,1,0:T(8,128)}, u32[]{:S(2)}, u32[]{:S(2)}) collective-permute-start(f32[5,3,192,512]{3,2,1,0:T(8,128)} %pack.5), channel_id=1, source_target_pairs={{0,1},{1,0},{2,3},{3,2},{4,5},{5,4},{6,7},{7,6},{8,9},{9,8},{10,11... | collective-permute-start | bytes 17694728 | tf_op jit(solution)/shard_map/ppermute | solution.py:345
  32.1 159.9 %collective-permute-start = (f32[5,4,72,1024]{3,2,1,0:T(8,128)}, f32[5,4,72,1024]{3,2,1,0:T(8,128)}, u32[]{:S(2)}, u32[]{:S(2)}) collective-permute-start(f32[5,4,72,1024]{3,2,1,0:T(8,128)} %pack.4), channel_id=1, source_target_pairs={{0,30},{2,4},{4,2},{6,8},{8,6},{10,12},{12,10},{14,16},{16,14},{18... | collective-permute-start | bytes 17694728 | tf_op jit(solution)/shard_map/ppermute | solution.py:363
  72.6 141.8 %collective-permute-start.11 = (f32[3,1,192,512]{3,2,1,0:T(8,128)}, f32[3,1,192,512]{3,2,1,0:T(8,128)}, u32[]{:S(2)}, u32[]{:S(2)}) collective-permute-start(f32[3,1,192,512]{3,2,1,0:T(8,128)} %get-tuple-element.27), channel_id=1, source_target_pairs={{0,1},{1,0},{2,3},{3,2},{4,5},{5,4},{6,7},{7,6},{8,9},{9,8},{10,11... | collective-permute-start | bytes 3538952 | tf_op jit(solution)/shard_map/ppermute | solution.py:345
  134.6 108.0 %collective-permute-start.10 = (f32[3,4,24,1024]{3,2,1,0:T(8,128)}, f32[3,4,24,1024]{3,2,1,0:T(8,128)}, u32[]{:S(2)}, u32[]{:S(2)}) collective-permute-start(f32[3,4,24,1024]{3,2,1,0:T(8,128)} %get-tuple-element.26), channel_id=1, source_target_pairs={{0,30},{2,4},{4,2},{6,8},{8,6},{10,12},{12,10},{14,16},{16,14},{18... | collective-permute-start | bytes 3538952 | tf_op jit(solution)/shard_map/ppermute | solution.py:396
  183.7 65.7 %collective-permute-start.9 = (f32[3,2,192,512]{3,2,1,0:T(8,128)}, f32[3,2,192,512]{3,2,1,0:T(8,128)}, u32[]{:S(2)}, u32[]{:S(2)}) collective-permute-start(f32[3,2,192,512]{3,2,1,0:T(8,128)} %get-tuple-element.25), channel_id=1, source_target_pairs={{0,1},{1,0},{2,3},{3,2},{4,5},{5,4},{6,7},{7,6},{8,9},{9,8},{10,11... | collective-permute-start | bytes 7077896 | tf_op jit(solution)/shard_map/ppermute | solution.py:345
  202.5 69.4 %collective-permute-start.8 = (f32[3,4,56,1024]{3,2,1,0:T(8,128)}, f32[3,4,56,1024]{3,2,1,0:T(8,128)}, u32[]{:S(2)}, u32[]{:S(2)}) collective-permute-start(f32[3,4,56,1024]{3,2,1,0:T(8,128)} %get-tuple-element.24), channel_id=1, source_target_pairs={{0,30},{2,4},{4,2},{6,8},{8,6},{10,12},{12,10},{14,16},{16,14},{18... | collective-permute-start | bytes 8257544 | tf_op jit(solution)/shard_map/ppermute | solution.py:396
  210.2 66.1 %collective-permute-start.7 = (f32[3,1,192,512]{3,2,1,0:T(8,128)}, f32[3,1,192,512]{3,2,1,0:T(8,128)S(1)}, u32[]{:S(2)}, u32[]{:S(2)}) collective-permute-start(f32[3,1,192,512]{3,2,1,0:T(8,128)} %get-tuple-element.23), channel_id=1, source_target_pairs={{0,1},{1,0},{2,3},{3,2},{4,5},{5,4},{6,7},{7,6},{8,9},{9,8},{10,11... | collective-permute-start | bytes 3538952 | tf_op jit(solution)/shard_map/ppermute | solution.py:345
  214.4 65.7 %collective-permute-start.6 = (f32[3,4,16,1024]{3,2,1,0:T(8,128)}, f32[3,4,16,1024]{3,2,1,0:T(8,128)S(1)}, u32[]{:S(2)}, u32[]{:S(2)}) collective-permute-start(f32[3,4,16,1024]{3,2,1,0:T(8,128)} %get-tuple-element.22), channel_id=1, source_target_pairs={{0,30},{2,4},{4,2},{6,8},{8,6},{10,12},{12,10},{14,16},{16,14},{18... | collective-permute-start | bytes 2359304 | tf_op jit(solution)/shard_map/ppermute | solution.py:396

commit v6 on v5

--- a/solution.py
+++ b/solution.py
@@ -97,11 +97,11 @@
         lanes = pl.ds(pl.multiple_of(place_ref[j] * lane_unit, 128), n_lanes)
         for source, first, fields in ((comp_ref, 0, 3), (vel_ref, 3, 2)):
             for f in range(fields):
-                for p in range(n_planes):
-                    k, to = len(loads), (first + f, p)
-                    loads.append(pltpu.make_async_copy(source.at[f, plane + p, rows, lanes], held[j].at[to], sems.at[0, k]))
-                    if not direct:
-                        stores.append(pltpu.make_async_copy(held[j].at[to], outs[j].at[to], sems.at[1, k]))
+                k, to = len(loads), first + f
+                planes = pl.ds(plane, n_planes)
+                loads.append(pltpu.make_async_copy(source.at[f, planes, rows, lanes], held[j].at[to], sems.at[0, k]))
+                if not direct:
+                    stores.append(pltpu.make_async_copy(held[j].at[to], outs[j].at[to], sems.at[1, k]))
     for load in loads:
         load.start()
     for k, load in enumerate(loads):
@@ -121,7 +121,7 @@
         out_specs=[pl.BlockSpec(memory_space=pltpu.VMEM) if direct else here] * len(boxes),
         out_shape=[pltpu.VMEM(shape, jnp.float32) if direct else jax.ShapeDtypeStruct(shape, jnp.float32) for shape in shapes],
         scratch_shapes=[pltpu.VMEM(shape, jnp.float32) for shape in shapes if not direct]
-        + [pltpu.SemaphoreType.DMA((2, sum(5 * shape[1] for shape in shapes)))],
+        + [pltpu.SemaphoreType.DMA((2, 5 * len(boxes)))],
         compiler_params=params(),
         cost_estimate=small,
         name="pack",
@@ -277,24 +277,24 @@
     fields, planes, size, lanes = part_ref.shape
     rows = pl.ds(pl.multiple_of(place_ref[0] * row_unit + row, row_block), size)
     columns = pl.ds(pl.multiple_of(place_ref[0] * lane_unit, 128), lanes)
-    pieces = [(f, p) for f in range(fields) for p in range(planes)]
+    box = (pl.ds(first, planes), rows, columns)
     loads, stores = [], []
-    for k, (f, p) in enumerate(pieces):
+    for f in range(fields):
         loads.append(
             (
-                pltpu.make_async_copy(part_ref.at[f, p], parts.at[f, p], sems.at[0, k]),
-                pltpu.make_async_copy(acc_ref.at[f, first + p, rows, columns], sums.at[f, p], sems.at[1, k]),
+                pltpu.make_async_copy(part_ref.at[f], parts.at[f], sems.at[0, f]),
+                pltpu.make_async_copy(acc_ref.at[(f, *box)], sums.at[f], sems.at[1, f]),
             )
         )
-        stores.append(pltpu.make_async_copy(parts.at[f, p], out_ref.at[f, first + p, rows, columns], sems.at[2, k]))
+        stores.append(pltpu.make_async_copy(parts.at[f], out_ref.at[(f, *box)], sems.at[2, f]))
     for pair in loads:
         for load in pair:
             load.start()
-    for (f, p), pair, store in zip(pieces, loads, stores):
-        for load in pair:
+    for f in range(fields):
+        for load in loads[f]:
             load.wait()
-        parts[f, p] = parts[f, p] + sums[f, p]
-        store.start()
+        parts[f] = parts[f] + sums[f]
+        stores[f].start()
     for store in stores:
         store.wait()
 
@@ -308,7 +308,7 @@
         out_shape=jax.ShapeDtypeStruct(acc.shape, jnp.float32),
         input_output_aliases={2: 0},
         scratch_shapes=[pltpu.VMEM(part.shape, jnp.float32)] * 2
-        + [pltpu.SemaphoreType.DMA((3, part.shape[0] * part.shape[1]))],
+        + [pltpu.SemaphoreType.DMA((3, part.shape[0]))],
         compiler_params=pltpu.CompilerParams(vmem_limit_bytes=24 * 1024 * 1024),
         cost_estimate=small,
         name="add_part",

time: 284 us -> 283 us (level)
  transfers between devices with their start and end apart: 12 -> 12, of which waited for: 7 -> 7; matrix products, arithmetic and copies ran while one was open for 5% -> 5% of each run, Pallas kernels for 38% -> 37%
where the time goes in v6:
time: 283 us; the launch traced here: 282 us
  waiting for transfers between devices  151 us (53%)
  Pallas kernels  107 us (38%)
  other arithmetic  12.1 us (4%)
  starting transfers between devices  11.5 us (4%)
    ppermute x2, waiting for transfers between devices, shards(): borders.append(lax.ppermute(packed[-1], 'gx', far))  62.3 us
    ppermute x3, waiting for transfers between devices, shards(): lax.ppermute(back, 'gx', far)  45.7 us
    ppermute x5, waiting for transfers between devices, along_yz(): lax.ppermute(x, 'yz', [(i, (i + by) % groups) for i in range(groups)])  42.6 us
    pallas_call x1, Pallas kernels, first_part(): pl.pallas_call(functools.partial(first_kernel, coeffs, lanes), grid_spec=...  33.2 us
    pallas_call x3, Pallas kernels, wall_part(): pl.pallas_call(functools.partial(wall_kernel, groups, rows), grid_spec=gr...  22.6 us
    pallas_call x3, Pallas kernels, border_part(): pl.pallas_call(functools.partial(border_kernel, coeffs, returns, lanes),...  20.3 us
    pallas_call x6, Pallas kernels, add_part(): pl.pallas_call(functools.partial(add_kernel, first, row, row_unit, lane_u...  16.6 us
    pallas_call x4, Pallas kernels, pack(): pl.pallas_call(functools.partial(pack_kernel, boxes, direct), in_specs=[p...  14 us
  transfers between devices with their start and end apart: 12, of which 7 were waited for; matrix products, arithmetic and copies ran while one was open for 5% of the time, Pallas kernels for 37%

profile of v6, /device:TPU:1, one launch (start us, length us, event | category | flops | bytes accessed | tf_op | source)
XLA Modules:
  0.0 281.8 jit_solution(11677428483755471849)
XLA Ops:
  0.5 1.6 pack.7
  2.1 2.3 collective-permute-start.3
  4.4 2.4 pack.6
  6.8 1.9 collective-permute-start.2
  8.7 5.0 %pack.5 = f32[5,3,192,512]{3,2,1,0:T(8,128)} custom-call(s32[1]{0:T(128)} %bitcast.3.place_ref, f32[3,4,192,1024]{3,2,1,0:T(8,128)} %comp_ref.15, f32[3,4,192,1024]{3,2,1,0:T(8,128)} %vel_ref.15), custom_call_target="tpu_custom_call" | custom-call | flops 1024 | bytes 1024 | tf_op jit(solution)/shard_map/pack/pallas_call | solution.py:118
  14.0 5.0 %pack.4 = f32[5,4,72,1024]{3,2,1,0:T(8,128)} custom-call(s32[1]{0:T(128)} %bitcast.place_ref, f32[3,4,192,1024]{3,2,1,0:T(8,128)} %comp_ref.15, f32[3,4,192,1024]{3,2,1,0:T(8,128)} %vel_ref.15), custom_call_target="tpu_custom_call" | custom-call | flops 1024 | bytes 1024 | tf_op jit(solution)/shard_map/pack/pallas_call | solution.py:118
  20.5 4.8 %fusion.11 = f32[384]{0:T(512)S(1)} fusion(f32[384]{0:T(512)S(1)} %get-tuple-element.34, s32[384]{0:T(512)S(1)} %fusion.14), kind=kLoop, calls=%fused_computation.25 | loop fusion | flops 4275840 | bytes 4608 | tf_op jit(solution)/shard_map/reduce_sum | solution.py:32
  25.3 5.0 %reduce-precision_convert_fusion = (bf16[384,384]{1,0:T(8,128)(2,1)S(1)}, bf16[384,384]{1,0:T(8,128)(2,1)S(1)}) fusion(f32[384]{0:T(512)S(1)} %fusion.11, f32[384]{0:T(512)S(1)} %get-tuple-element.33, f32[384]{0:T(512)S(1)} %get-tuple-element.34, s32[384]{0:T(512)S(1)} %fusion.14), kind=kLoop, calls=%fused_computation.8 | loop fusion | flops 5455872 | bytes 595968 | tf_op jit(solution)/shard_map/convert
  32.4 33.2 %first_part.1.refs_5_ = f32[3,4,192,1024]{3,2,1,0:T(8,128)} custom-call(s32[1]{0:T(128)} %bitcast.6.flag_ref, f32[192,128]{1,0:T(8,128)} %broadcast_in_dim.48.step_ref, f32[3,4,192,1024]{3,2,1,0:T(8,128)} %comp_ref.15, f32[3,4,192,1024]{3,2,1,0:T(8,128)} %vel_ref.15, f32[3,4,192,1024]{3,2,1,0:T(8,128)} %collective-permute-done.4.comp_near, ...), custom_call_target="tpu_custom_call" | custom-call | flops 1024 | bytes 1024 | tf_op jit(solution)/shard_map/first_part/pallas_call | solution.py:266
  65.6 6.3 %wall_part.3 = (f32[3,4,192,1024]{3,2,1,0:T(8,128)}, f32[3,1,192,512]{3,2,1,0:T(8,128)}) custom-call(s32[1]{0:T(128)} %bitcast.2.refs_0_, f32[3,4,192,1024]{3,2,1,0:T(8,128)} %comp_ref.15, f32[3,4,192,1024]{3,2,1,0:T(8,128)} %vel_ref.15, f32[5,1,192,512]{3,2,1,0:T(8,128)} %collective-permute-done.3.refs_3_, ...), custom_call_target="tpu_custom_call", output_to_operand_aliasing={{0}: (5, {})} | custom-call | flops 99999997952 | bytes 1024 | tf_op jit(solution)/shard_map/wall_part/pallas_call | solution.py:180
  71.8 1.2 collective-permute-start.11
  73.1 55.4 %collective-permute-done.2.refs_0_ = f32[5,4,24,1024]{3,2,1,0:T(8,128)} collective-permute-done((f32[5,4,24,1024]{3,2,1,0:T(8,128)}, f32[5,4,24,1024]{3,2,1,0:T(8,128)}, u32[]{:S(2)}, u32[]{:S(2)}) %collective-permute-start.2) | collective-permute-done | bytes 1966112 | tf_op jit(solution)/shard_map/ppermute | solution.py:363
  128.5 5.8 %border_part.3 = (f32[3,4,192,1024]{3,2,1,0:T(8,128)}, f32[3,4,24,1024]{3,2,1,0:T(8,128)}) custom-call(s32[2]{0:T(128)} %pad_add_fusion.2.flag_ref, f32[192,128]{1,0:T(8,128)} %broadcast_in_dim.48.step_ref, f32[3,4,192,1024]{3,2,1,0:T(8,128)} %comp_ref.15, f32[3,4,192,1024]{3,2,1,0:T(8,128)} %vel_ref.15, ...), custom_call_target="tpu_custom_call", output_to_operand_aliasing={{0}: (5, {})} | custom-call | flops 99999997952 | bytes 1024 | tf_op jit(solution)/shard_map/border_part/pallas_call | solution.py:237
  134.3 1.4 collective-permute-start.10
  135.7 37.9 %collective-permute-done.1.refs_3_ = f32[5,3,192,512]{3,2,1,0:T(8,128)} collective-permute-done((f32[5,3,192,512]{3,2,1,0:T(8,128)}, f32[5,3,192,512]{3,2,1,0:T(8,128)}, u32[]{:S(2)}, u32[]{:S(2)}) %collective-permute-start.1) | collective-permute-done | bytes 5898272 | tf_op jit(solution)/shard_map/ppermute | solution.py:345
  173.6 10.1 %wall_part.4 = (f32[3,4,192,1024]{3,2,1,0:T(8,128)}, f32[3,2,192,512]{3,2,1,0:T(8,128)}) custom-call(s32[1]{0:T(128)} %bitcast.2.refs_0_, f32[3,4,192,1024]{3,2,1,0:T(8,128)} %comp_ref.15, f32[3,4,192,1024]{3,2,1,0:T(8,128)} %vel_ref.15, f32[5,3,192,512]{3,2,1,0:T(8,128)} %collective-permute-done.1.refs_3_, ...), custom_call_target="tpu_custom_call", output_to_operand_aliasing={{0}: (5, {})} | custom-call | flops 99999997952 | bytes 1024 | tf_op jit(solution)/shard_map/wall_part/pallas_call | solution.py:180
  183.7 1.1 collective-permute-start.9
  184.9 6.9 %collective-permute-done.refs_0_ = f32[5,4,72,1024]{3,2,1,0:T(8,128)} collective-permute-done((f32[5,4,72,1024]{3,2,1,0:T(8,128)}, f32[5,4,72,1024]{3,2,1,0:T(8,128)}, u32[]{:S(2)}, u32[]{:S(2)}) %collective-permute-start) | collective-permute-done | bytes 5898272 | tf_op jit(solution)/shard_map/ppermute | solution.py:363
  191.7 10.5 %border_part.4 = (f32[3,4,192,1024]{3,2,1,0:T(8,128)}, f32[3,4,56,1024]{3,2,1,0:T(8,128)}) custom-call(s32[2]{0:T(128)} %get-tuple-element.32.flag_ref, f32[192,128]{1,0:T(8,128)} %broadcast_in_dim.48.step_ref, f32[3,4,192,1024]{3,2,1,0:T(8,128)} %comp_ref.15, f32[3,4,192,1024]{3,2,1,0:T(8,128)} %vel_ref.15, ...), custom_call_target="tpu_custom_call", output_to_operand_aliasing={{0}: (5, {})} | custom-call | flops 99999997952 | bytes 1024 | tf_op jit(solution)/shard_map/border_part/pallas_call | solution.py:237
  202.3 1.4 collective-permute-start.8
  203.7 6.2 %wall_part.5 = (f32[3,4,192,1024]{3,2,1,0:T(8,128)}, f32[3,1,192,512]{3,2,1,0:T(8,128)}) custom-call(s32[1]{0:T(128)} %bitcast.2.refs_0_, f32[3,4,192,1024]{3,2,1,0:T(8,128)} %comp_ref.15, f32[3,4,192,1024]{3,2,1,0:T(8,128)} %vel_ref.15, f32[5,3,192,512]{3,2,1,0:T(8,128)} %collective-permute-done.1.refs_3_, ...), custom_call_target="tpu_custom_call", output_to_operand_aliasing={{0}: (5, {})} | custom-call | flops 99999997952 | bytes 1024 | tf_op jit(solution)/shard_map/wall_part/pallas_call | solution.py:180
  210.1 4.0 %border_part.5 = (f32[3,4,192,1024]{3,2,1,0:T(8,128)}, f32[3,4,16,1024]{3,2,1,0:T(8,128)}) custom-call(s32[2]{0:T(128)} %get-tuple-element.31.flag_ref, f32[192,128]{1,0:T(8,128)} %broadcast_in_dim.48.step_ref, f32[3,4,192,1024]{3,2,1,0:T(8,128)} %comp_ref.15, f32[3,4,192,1024]{3,2,1,0:T(8,128)} %vel_ref.15, ...), custom_call_target="tpu_custom_call", output_to_operand_aliasing={{0}: (5, {})} | custom-call | flops 99999997952 | bytes 1024 | tf_op jit(solution)/shard_map/border_part/pallas_call | solution.py:237
  214.8 2.4 add_part.6.acc_ref
  217.2 25.1 %collective-permute-done.10.part_ref = f32[3,4,24,1024]{3,2,1,0:T(8,128)} collective-permute-done((f32[3,4,24,1024]{3,2,1,0:T(8,128)}, f32[3,4,24,1024]{3,2,1,0:T(8,128)}, u32[]{:S(2)}, u32[]{:S(2)}) %collective-permute-start.10) | collective-permute-done | bytes 1179680 | tf_op jit(solution)/shard_map/ppermute | solution.py:396
  242.3 2.4 add_part.7.acc_ref
  244.7 4.7 %collective-permute-done.9.part_ref = f32[3,2,192,512]{3,2,1,0:T(8,128)} collective-permute-done((f32[3,2,192,512]{3,2,1,0:T(8,128)}, f32[3,2,192,512]{3,2,1,0:T(8,128)}, u32[]{:S(2)}, u32[]{:S(2)}) %collective-permute-start.9) | collective-permute-done | bytes 2359328 | tf_op jit(solution)/shard_map/ppermute | solution.py:345
  249.5 3.4 %add_part.8.acc_ref = f32[3,4,192,1024]{3,2,1,0:T(8,128)} custom-call(s32[1]{0:T(128)} %bitcast.7.place_ref, f32[3,2,192,512]{3,2,1,0:T(8,128)} %collective-permute-done.9.part_ref, f32[3,4,192,1024]{3,2,1,0:T(8,128)} %add_part.7.acc_ref), custom_call_target="tpu_custom_call", output_to_operand_aliasing={{}: (2, {})} | custom-call | flops 1024 | bytes 1024 | tf_op jit(solution)/shard_map/add_part/pallas_call | solution.py:304
  252.8 18.9 %collective-permute-done.8.part_ref = f32[3,4,56,1024]{3,2,1,0:T(8,128)} collective-permute-done((f32[3,4,56,1024]{3,2,1,0:T(8,128)}, f32[3,4,56,1024]{3,2,1,0:T(8,128)}, u32[]{:S(2)}, u32[]{:S(2)}) %collective-permute-start.8) | collective-permute-done | bytes 2752544 | tf_op jit(solution)/shard_map/ppermute | solution.py:396
  271.7 3.9 %add_part.9.acc_ref = f32[3,4,192,1024]{3,2,1,0:T(8,128)} custom-call(s32[1]{0:T(128)} %bitcast.place_ref, f32[3,4,56,1024]{3,2,1,0:T(8,128)} %collective-permute-done.8.part_ref, f32[3,4,192,1024]{3,2,1,0:T(8,128)} %add_part.8.acc_ref), custom_call_target="tpu_custom_call", output_to_operand_aliasing={{}: (2, {})} | custom-call | flops 1024 | bytes 1024 | tf_op jit(solution)/shard_map/add_part/pallas_call | solution.py:304
  275.6 2.5 add_part.10.acc_ref
  278.1 1.8 collective-permute-done.6.part_ref
  279.8 1.9 add_part.11
  (18 shorter events, 5.1 us)
Async XLA Ops:
  0.0 31.3 %collective-permute-start.4 = (f32[3,4,192,1024]{3,2,1,0:T(8,128)}, f32[3,4,192,1024]{3,2,1,0:T(8,128)}, u32[]{:S(2)}, u32[]{:S(2)}) collective-permute-start(f32[3,4,192,1024]{3,2,1,0:T(8,128)} %comp_ref.15), channel_id=1, source_target_pairs={{0,2},{2,0},{4,6},{6,4},{8,10},{10,8},{12,14},{14,12},{16,18},{18,... | collective-permute-start | bytes 28311560 | tf_op jit(solution)/shard_map/ppermute | solution.py:347
  0.1 31.6 %collective-permute-start.5 = (f32[3,4,192,1024]{3,2,1,0:T(8,128)}, f32[3,4,192,1024]{3,2,1,0:T(8,128)}, u32[]{:S(2)}, u32[]{:S(2)}) collective-permute-start(f32[3,4,192,1024]{3,2,1,0:T(8,128)} %vel_ref.15), channel_id=1, source_target_pairs={{0,2},{2,0},{4,6},{6,4},{8,10},{10,8},{12,14},{14,12},{16,18},{18,... | collective-permute-start | bytes 28311560 | tf_op jit(solution)/shard_map/ppermute | solution.py:347
  2.1 63.5 %collective-permute-start.3 = (f32[5,1,192,512]{3,2,1,0:T(8,128)S(1)}, f32[5,1,192,512]{3,2,1,0:T(8,128)}, u32[]{:S(2)}, u32[]{:S(2)}) collective-permute-start(f32[5,1,192,512]{3,2,1,0:T(8,128)S(1)} %pack.7), channel_id=1, source_target_pairs={{0,1},{1,0},{2,3},{3,2},{4,5},{5,4},{6,7},{7,6},{8,9},{9,8},{10,11... | collective-permute-start | bytes 5898248 | tf_op jit(solution)/shard_map/ppermute | solution.py:345
  6.8 121.8 %collective-permute-start.2 = (f32[5,4,24,1024]{3,2,1,0:T(8,128)}, f32[5,4,24,1024]{3,2,1,0:T(8,128)}, u32[]{:S(2)}, u32[]{:S(2)}) collective-permute-start(f32[5,4,24,1024]{3,2,1,0:T(8,128)} %pack.6), channel_id=1, source_target_pairs={{0,30},{2,4},{4,2},{6,8},{8,6},{10,12},{12,10},{14,16},{16,14},{18... | collective-permute-start | bytes 5898248 | tf_op jit(solution)/shard_map/ppermute | solution.py:363
  13.7 159.9 %collective-permute-start.1 = (f32[5,3,192,512]{3,2,1,0:T(8,128)}, f32[5,3,192,512]{3,2,1,0:T(8,128)}, u32[]{:S(2)}, u32[]{:S(2)}) collective-permute-start(f32[5,3,192,512]{3,2,1,0:T(8,128)} %pack.5), channel_id=1, source_target_pairs={{0,1},{1,0},{2,3},{3,2},{4,5},{5,4},{6,7},{7,6},{8,9},{9,8},{10,11... | collective-permute-start | bytes 17694728 | tf_op jit(solution)/shard_map/ppermute | solution.py:345
  31.3 160.4 %collective-permute-start = (f32[5,4,72,1024]{3,2,1,0:T(8,128)}, f32[5,4,72,1024]{3,2,1,0:T(8,128)}, u32[]{:S(2)}, u32[]{:S(2)}) collective-permute-start(f32[5,4,72,1024]{3,2,1,0:T(8,128)} %pack.4), channel_id=1, source_target_pairs={{0,30},{2,4},{4,2},{6,8},{8,6},{10,12},{12,10},{14,16},{16,14},{18... | collective-permute-start | bytes 17694728 | tf_op jit(solution)/shard_map/ppermute | solution.py:363
  71.8 142.3 %collective-permute-start.11 = (f32[3,1,192,512]{3,2,1,0:T(8,128)}, f32[3,1,192,512]{3,2,1,0:T(8,128)}, u32[]{:S(2)}, u32[]{:S(2)}) collective-permute-start(f32[3,1,192,512]{3,2,1,0:T(8,128)} %get-tuple-element.27), channel_id=1, source_target_pairs={{0,1},{1,0},{2,3},{3,2},{4,5},{5,4},{6,7},{7,6},{8,9},{9,8},{10,11... | collective-permute-start | bytes 3538952 | tf_op jit(solution)/shard_map/ppermute | solution.py:345
  134.3 108.0 %collective-permute-start.10 = (f32[3,4,24,1024]{3,2,1,0:T(8,128)}, f32[3,4,24,1024]{3,2,1,0:T(8,128)}, u32[]{:S(2)}, u32[]{:S(2)}) collective-permute-start(f32[3,4,24,1024]{3,2,1,0:T(8,128)} %get-tuple-element.26), channel_id=1, source_target_pairs={{0,30},{2,4},{4,2},{6,8},{8,6},{10,12},{12,10},{14,16},{16,14},{18... | collective-permute-start | bytes 3538952 | tf_op jit(solution)/shard_map/ppermute | solution.py:396
  183.7 65.7 %collective-permute-start.9 = (f32[3,2,192,512]{3,2,1,0:T(8,128)}, f32[3,2,192,512]{3,2,1,0:T(8,128)}, u32[]{:S(2)}, u32[]{:S(2)}) collective-permute-start(f32[3,2,192,512]{3,2,1,0:T(8,128)} %get-tuple-element.25), channel_id=1, source_target_pairs={{0,1},{1,0},{2,3},{3,2},{4,5},{5,4},{6,7},{7,6},{8,9},{9,8},{10,11... | collective-permute-start | bytes 7077896 | tf_op jit(solution)/shard_map/ppermute | solution.py:345
  202.3 69.4 %collective-permute-start.8 = (f32[3,4,56,1024]{3,2,1,0:T(8,128)}, f32[3,4,56,1024]{3,2,1,0:T(8,128)}, u32[]{:S(2)}, u32[]{:S(2)}) collective-permute-start(f32[3,4,56,1024]{3,2,1,0:T(8,128)} %get-tuple-element.24), channel_id=1, source_target_pairs={{0,30},{2,4},{4,2},{6,8},{8,6},{10,12},{12,10},{14,16},{16,14},{18... | collective-permute-start | bytes 8257544 | tf_op jit(solution)/shard_map/ppermute | solution.py:396
  209.9 65.7 %collective-permute-start.7 = (f32[3,1,192,512]{3,2,1,0:T(8,128)}, f32[3,1,192,512]{3,2,1,0:T(8,128)S(1)}, u32[]{:S(2)}, u32[]{:S(2)}) collective-permute-start(f32[3,1,192,512]{3,2,1,0:T(8,128)} %get-tuple-element.23), channel_id=1, source_target_pairs={{0,1},{1,0},{2,3},{3,2},{4,5},{5,4},{6,7},{7,6},{8,9},{9,8},{10,11... | collective-permute-start | bytes 3538952 | tf_op jit(solution)/shard_map/ppermute | solution.py:345
  214.1 65.7 %collective-permute-start.6 = (f32[3,4,16,1024]{3,2,1,0:T(8,128)}, f32[3,4,16,1024]{3,2,1,0:T(8,128)S(1)}, u32[]{:S(2)}, u32[]{:S(2)}) collective-permute-start(f32[3,4,16,1024]{3,2,1,0:T(8,128)} %get-tuple-element.22), channel_id=1, source_target_pairs={{0,30},{2,4},{4,2},{6,8},{8,6},{10,12},{12,10},{14,16},{16,14},{18... | collective-permute-start | bytes 2359304 | tf_op jit(solution)/shard_map/ppermute | solution.py:396

commit v7 on v6

--- a/solution.py
+++ b/solution.py
@@ -14,7 +14,7 @@
 relax_rate = 1.0 / 0.04
 courant = 0.5
 row_block = 8
-share_weights = ((3,), (7, 2))
+share_weights = ((3,), (8, 1))
 vmem_bytes = 56 * 1024 * 1024
 
 

time: 283 us -> 287 us (1.014)
  waiting for transfers between devices: 151 us -> 158 us
  Pallas kernels: 107 us -> 102 us
    ppermute x5 -> x4, waiting for transfers between devices: 42.6 us -> 99.9 us  [along_yz(): lax.ppermute(x, 'yz', [(i, (i + by) % groups) for i in range(groups)])]
    ppermute x3, waiting for transfers between devices: 45.7 us -> 0.01 us  [shards(): lax.ppermute(back, 'gx', far)]
    ppermute x2, waiting for transfers between devices: 62.3 us -> 58.2 us  [shards(): borders.append(lax.ppermute(packed[-1], 'gx', far))]
    pallas_call x3 -> x2, Pallas kernels: 22.6 us -> 20 us  [wall_part(): pl.pallas_call(functools.partial(wall_kernel, groups, rows), grid_spec=gr...]
    pallas_call x6 -> x5, Pallas kernels: 16.6 us -> 15.1 us  [add_part(): pl.pallas_call(functools.partial(add_kernel, first, row, row_unit, lane_u...]
  transfers between devices with their start and end apart: 12 -> 11, of which waited for: 7 -> 4; matrix products, arithmetic and copies ran while one was open for 5% -> 5% of each run, Pallas kernels for 37% -> 35%
where the time goes in v7:
time: 287 us; the launch traced here: 285 us
  waiting for transfers between devices  158 us (55%)
  Pallas kernels  102 us (36%)
  other arithmetic  12.7 us (4%)
  starting transfers between devices  10.9 us (4%)
    ppermute x4, waiting for transfers between devices, along_yz(): lax.ppermute(x, 'yz', [(i, (i + by) % groups) for i in range(groups)])  99.9 us
    ppermute x2, waiting for transfers between devices, shards(): borders.append(lax.ppermute(packed[-1], 'gx', far))  58.2 us
    pallas_call x1, Pallas kernels, first_part(): pl.pallas_call(functools.partial(first_kernel, coeffs, lanes), grid_spec=...  33.2 us
    pallas_call x3, Pallas kernels, border_part(): pl.pallas_call(functools.partial(border_kernel, coeffs, returns, lanes),...  20.1 us
    pallas_call x2, Pallas kernels, wall_part(): pl.pallas_call(functools.partial(wall_kernel, groups, rows), grid_spec=gr...  20 us
    pallas_call x5, Pallas kernels, add_part(): pl.pallas_call(functools.partial(add_kernel, first, row, row_unit, lane_u...  15.1 us
    pallas_call x4, Pallas kernels, pack(): pl.pallas_call(functools.partial(pack_kernel, boxes, direct), in_specs=[p...  13.9 us
  transfers between devices with their start and end apart: 11, of which 4 were waited for; matrix products, arithmetic and copies ran while one was open for 5% of the time, Pallas kernels for 35%

profile of v7, /device:TPU:1, one launch (start us, length us, event | category | flops | bytes accessed | tf_op | source)
XLA Modules:
  0.0 284.9 jit_solution(7635023856931931027)
XLA Ops:
  0.5 1.6 pack.7
  2.1 2.3 collective-permute-start.3
  4.4 2.4 pack.6
  6.7 1.9 collective-permute-start.2
  8.7 5.0 %pack.5 = f32[5,3,192,512]{3,2,1,0:T(8,128)} custom-call(s32[1]{0:T(128)} %bitcast.4.place_ref, f32[3,4,192,1024]{3,2,1,0:T(8,128)} %comp_ref.15, f32[3,4,192,1024]{3,2,1,0:T(8,128)} %vel_ref.15), custom_call_target="tpu_custom_call" | custom-call | flops 1024 | bytes 1024 | tf_op jit(solution)/shard_map/pack/pallas_call | solution.py:118
  14.0 5.0 %pack.4 = f32[5,4,72,1024]{3,2,1,0:T(8,128)} custom-call(s32[1]{0:T(128)} %bitcast.place_ref, f32[3,4,192,1024]{3,2,1,0:T(8,128)} %comp_ref.15, f32[3,4,192,1024]{3,2,1,0:T(8,128)} %vel_ref.15), custom_call_target="tpu_custom_call" | custom-call | flops 1024 | bytes 1024 | tf_op jit(solution)/shard_map/pack/pallas_call | solution.py:118
  19.1 0.6 pad_add_fusion.2.flag_ref
  19.7 0.6 pad_add_fusion.1.flag_ref
  20.3 0.7 pad_add_fusion.flag_ref
  21.0 4.8 %fusion.11 = f32[384]{0:T(512)S(1)} fusion(f32[384]{0:T(512)S(1)} %get-tuple-element.28, s32[384]{0:T(512)S(1)} %fusion.14), kind=kLoop, calls=%fused_computation.25 | loop fusion | flops 4275840 | bytes 4608 | tf_op jit(solution)/shard_map/reduce_sum | solution.py:32
  25.8 5.0 %reduce-precision_convert_fusion = (bf16[384,384]{1,0:T(8,128)(2,1)S(1)}, bf16[384,384]{1,0:T(8,128)(2,1)S(1)}) fusion(f32[384]{0:T(512)S(1)} %fusion.11, f32[384]{0:T(512)S(1)} %get-tuple-element.27, f32[384]{0:T(512)S(1)} %get-tuple-element.28, s32[384]{0:T(512)S(1)} %fusion.14), kind=kLoop, calls=%fused_computation.8 | loop fusion | flops 5455872 | bytes 595968 | tf_op jit(solution)/shard_map/convert
  30.8 1.0 pad_maximum_fusion.refs_4_
  32.1 0.7 broadcast_in_dim.48.step_ref
  32.9 33.2 %first_part.1.refs_5_ = f32[3,4,192,1024]{3,2,1,0:T(8,128)} custom-call(s32[1]{0:T(128)} %bitcast.6.flag_ref, f32[192,128]{1,0:T(8,128)} %broadcast_in_dim.48.step_ref, f32[3,4,192,1024]{3,2,1,0:T(8,128)} %comp_ref.15, f32[3,4,192,1024]{3,2,1,0:T(8,128)} %vel_ref.15, f32[3,4,192,1024]{3,2,1,0:T(8,128)} %collective-permute-done.4.comp_near, ...), custom_call_target="tpu_custom_call" | custom-call | flops 1024 | bytes 1024 | tf_op jit(solution)/shard_map/first_part/pallas_call | solution.py:266
  66.1 6.2 %wall_part.2 = (f32[3,4,192,1024]{3,2,1,0:T(8,128)}, f32[3,1,192,512]{3,2,1,0:T(8,128)}) custom-call(s32[1]{0:T(128)} %bitcast.3.refs_0_, f32[3,4,192,1024]{3,2,1,0:T(8,128)} %comp_ref.15, f32[3,4,192,1024]{3,2,1,0:T(8,128)} %vel_ref.15, f32[5,1,192,512]{3,2,1,0:T(8,128)} %collective-permute-done.3.refs_3_, ...), custom_call_target="tpu_custom_call", output_to_operand_aliasing={{0}: (5, {})} | custom-call | flops 99999997952 | bytes 1024 | tf_op jit(solution)/shard_map/wall_part/pallas_call | solution.py:180
  72.3 1.3 collective-permute-start.10
  73.5 55.0 %collective-permute-done.2.refs_0_ = f32[5,4,24,1024]{3,2,1,0:T(8,128)} collective-permute-done((f32[5,4,24,1024]{3,2,1,0:T(8,128)}, f32[5,4,24,1024]{3,2,1,0:T(8,128)}, u32[]{:S(2)}, u32[]{:S(2)}) %collective-permute-start.2) | collective-permute-done | bytes 1966112 | tf_op jit(solution)/shard_map/ppermute | solution.py:363
  128.5 5.7 %border_part.3 = (f32[3,4,192,1024]{3,2,1,0:T(8,128)}, f32[3,4,24,1024]{3,2,1,0:T(8,128)}) custom-call(s32[2]{0:T(128)} %pad_add_fusion.2.flag_ref, f32[192,128]{1,0:T(8,128)} %broadcast_in_dim.48.step_ref, f32[3,4,192,1024]{3,2,1,0:T(8,128)} %comp_ref.15, f32[3,4,192,1024]{3,2,1,0:T(8,128)} %vel_ref.15, ...), custom_call_target="tpu_custom_call", output_to_operand_aliasing={{0}: (5, {})} | custom-call | flops 99999997952 | bytes 1024 | tf_op jit(solution)/shard_map/border_part/pallas_call | solution.py:237
  134.2 1.4 collective-permute-start.9
  135.7 38.0 %collective-permute-done.1.refs_3_ = f32[5,3,192,512]{3,2,1,0:T(8,128)} collective-permute-done((f32[5,3,192,512]{3,2,1,0:T(8,128)}, f32[5,3,192,512]{3,2,1,0:T(8,128)}, u32[]{:S(2)}, u32[]{:S(2)}) %collective-permute-start.1) | collective-permute-done | bytes 5898272 | tf_op jit(solution)/shard_map/ppermute | solution.py:345
  173.6 13.8 %wall_part.3 = (f32[3,4,192,1024]{3,2,1,0:T(8,128)}, f32[3,3,192,512]{3,2,1,0:T(8,128)}) custom-call(s32[1]{0:T(128)} %bitcast.3.refs_0_, f32[3,4,192,1024]{3,2,1,0:T(8,128)} %comp_ref.15, f32[3,4,192,1024]{3,2,1,0:T(8,128)} %vel_ref.15, f32[5,3,192,512]{3,2,1,0:T(8,128)} %collective-permute-done.1.refs_3_, ...), custom_call_target="tpu_custom_call", output_to_operand_aliasing={{0}: (5, {})} | custom-call | flops 99999997952 | bytes 1024 | tf_op jit(solution)/shard_map/wall_part/pallas_call | solution.py:180
  187.4 1.1 collective-permute-start.8
  188.5 3.2 %collective-permute-done.refs_0_ = f32[5,4,72,1024]{3,2,1,0:T(8,128)} collective-permute-done((f32[5,4,72,1024]{3,2,1,0:T(8,128)}, f32[5,4,72,1024]{3,2,1,0:T(8,128)}, u32[]{:S(2)}, u32[]{:S(2)}) %collective-permute-start) | collective-permute-done | bytes 5898272 | tf_op jit(solution)/shard_map/ppermute | solution.py:363
  191.7 11.0 %border_part.4 = (f32[3,4,192,1024]{3,2,1,0:T(8,128)}, f32[3,4,64,1024]{3,2,1,0:T(8,128)}) custom-call(s32[2]{0:T(128)} %pad_add_fusion.1.flag_ref, f32[192,128]{1,0:T(8,128)} %broadcast_in_dim.48.step_ref, f32[3,4,192,1024]{3,2,1,0:T(8,128)} %comp_ref.15, f32[3,4,192,1024]{3,2,1,0:T(8,128)} %vel_ref.15, ...), custom_call_target="tpu_custom_call", output_to_operand_aliasing={{0}: (5, {})} | custom-call | flops 99999997952 | bytes 1024 | tf_op jit(solution)/shard_map/border_part/pallas_call | solution.py:237
  202.8 1.4 collective-permute-start.7
  204.2 3.3 %border_part.5 = (f32[3,4,192,1024]{3,2,1,0:T(8,128)}, f32[3,4,8,1024]{3,2,1,0:T(8,128)}) custom-call(s32[2]{0:T(128)} %pad_add_fusion.flag_ref, f32[192,128]{1,0:T(8,128)} %broadcast_in_dim.48.step_ref, f32[3,4,192,1024]{3,2,1,0:T(8,128)} %comp_ref.15, f32[3,4,192,1024]{3,2,1,0:T(8,128)} %vel_ref.15, ...), custom_call_target="tpu_custom_call", output_to_operand_aliasing={{0}: (5, {})} | custom-call | flops 99999997952 | bytes 1024 | tf_op jit(solution)/shard_map/border_part/pallas_call | solution.py:237
  207.8 2.5 add_part.5.acc_ref
  210.3 2.5 add_part.6.acc_ref
  212.8 62.0 %collective-permute-done.8.part_ref = f32[3,3,192,512]{3,2,1,0:T(8,128)} collective-permute-done((f32[3,3,192,512]{3,2,1,0:T(8,128)}, f32[3,3,192,512]{3,2,1,0:T(8,128)}, u32[]{:S(2)}, u32[]{:S(2)}) %collective-permute-start.8) | collective-permute-done | bytes 3538976 | tf_op jit(solution)/shard_map/ppermute | solution.py:345
  274.7 4.8 %add_part.7.acc_ref = f32[3,4,192,1024]{3,2,1,0:T(8,128)} custom-call(s32[1]{0:T(128)} %bitcast.7.place_ref, f32[3,3,192,512]{3,2,1,0:T(8,128)} %collective-permute-done.8.part_ref, f32[3,4,192,1024]{3,2,1,0:T(8,128)} %add_part.6.acc_ref), custom_call_target="tpu_custom_call", output_to_operand_aliasing={{}: (2, {})} | custom-call | flops 1024 | bytes 1024 | tf_op jit(solution)/shard_map/add_part/pallas_call | solution.py:304
  279.6 3.1 %add_part.8.acc_ref = f32[3,4,192,1024]{3,2,1,0:T(8,128)} custom-call(s32[1]{0:T(128)} %bitcast.place_ref, f32[3,4,64,1024]{3,2,1,0:T(8,128)S(1)} %collective-permute-done.7.part_ref, f32[3,4,192,1024]{3,2,1,0:T(8,128)} %add_part.7.acc_ref), custom_call_target="tpu_custom_call", output_to_operand_aliasing={{}: (2, {})} | custom-call | flops 1024 | bytes 1024 | tf_op jit(solution)/shard_map/add_part/pallas_call | solution.py:304
  282.7 2.2 add_part.9
  (15 shorter events, 1.5 us)
Async XLA Ops:
  0.0 31.8 %collective-permute-start.4 = (f32[3,4,192,1024]{3,2,1,0:T(8,128)}, f32[3,4,192,1024]{3,2,1,0:T(8,128)}, u32[]{:S(2)}, u32[]{:S(2)}) collective-permute-start(f32[3,4,192,1024]{3,2,1,0:T(8,128)} %comp_ref.15), channel_id=1, source_target_pairs={{0,2},{2,0},{4,6},{6,4},{8,10},{10,8},{12,14},{14,12},{16,18},{18,... | collective-permute-start | bytes 28311560 | tf_op jit(solution)/shard_map/ppermute | solution.py:347
  0.1 32.1 %collective-permute-start.5 = (f32[3,4,192,1024]{3,2,1,0:T(8,128)}, f32[3,4,192,1024]{3,2,1,0:T(8,128)}, u32[]{:S(2)}, u32[]{:S(2)}) collective-permute-start(f32[3,4,192,1024]{3,2,1,0:T(8,128)} %vel_ref.15), channel_id=1, source_target_pairs={{0,2},{2,0},{4,6},{6,4},{8,10},{10,8},{12,14},{14,12},{16,18},{18,... | collective-permute-start | bytes 28311560 | tf_op jit(solution)/shard_map/ppermute | solution.py:347
  2.1 64.0 %collective-permute-start.3 = (f32[5,1,192,512]{3,2,1,0:T(8,128)S(1)}, f32[5,1,192,512]{3,2,1,0:T(8,128)}, u32[]{:S(2)}, u32[]{:S(2)}) collective-permute-start(f32[5,1,192,512]{3,2,1,0:T(8,128)S(1)} %pack.7), channel_id=1, source_target_pairs={{0,1},{1,0},{2,3},{3,2},{4,5},{5,4},{6,7},{7,6},{8,9},{9,8},{10,11... | collective-permute-start | bytes 5898248 | tf_op jit(solution)/shard_map/ppermute | solution.py:345
  6.7 121.8 %collective-permute-start.2 = (f32[5,4,24,1024]{3,2,1,0:T(8,128)}, f32[5,4,24,1024]{3,2,1,0:T(8,128)}, u32[]{:S(2)}, u32[]{:S(2)}) collective-permute-start(f32[5,4,24,1024]{3,2,1,0:T(8,128)} %pack.6), channel_id=1, source_target_pairs={{0,30},{2,4},{4,2},{6,8},{8,6},{10,12},{12,10},{14,16},{16,14},{18... | collective-permute-start | bytes 5898248 | tf_op jit(solution)/shard_map/ppermute | solution.py:363
  13.7 159.9 %collective-permute-start.1 = (f32[5,3,192,512]{3,2,1,0:T(8,128)}, f32[5,3,192,512]{3,2,1,0:T(8,128)}, u32[]{:S(2)}, u32[]{:S(2)}) collective-permute-start(f32[5,3,192,512]{3,2,1,0:T(8,128)} %pack.5), channel_id=1, source_target_pairs={{0,1},{1,0},{2,3},{3,2},{4,5},{5,4},{6,7},{7,6},{8,9},{9,8},{10,11... | collective-permute-start | bytes 17694728 | tf_op jit(solution)/shard_map/ppermute | solution.py:345
  31.8 159.9 %collective-permute-start = (f32[5,4,72,1024]{3,2,1,0:T(8,128)}, f32[5,4,72,1024]{3,2,1,0:T(8,128)}, u32[]{:S(2)}, u32[]{:S(2)}) collective-permute-start(f32[5,4,72,1024]{3,2,1,0:T(8,128)} %pack.4), channel_id=1, source_target_pairs={{0,30},{2,4},{4,2},{6,8},{8,6},{10,12},{12,10},{14,16},{16,14},{18... | collective-permute-start | bytes 17694728 | tf_op jit(solution)/shard_map/ppermute | solution.py:363
  72.3 135.5 %collective-permute-start.10 = (f32[3,1,192,512]{3,2,1,0:T(8,128)}, f32[3,1,192,512]{3,2,1,0:T(8,128)}, u32[]{:S(2)}, u32[]{:S(2)}) collective-permute-start(f32[3,1,192,512]{3,2,1,0:T(8,128)} %get-tuple-element.23), channel_id=1, source_target_pairs={{0,1},{1,0},{2,3},{3,2},{4,5},{5,4},{6,7},{7,6},{8,9},{9,8},{10,11... | collective-permute-start | bytes 3538952 | tf_op jit(solution)/shard_map/ppermute | solution.py:345
  134.2 76.1 %collective-permute-start.9 = (f32[3,4,24,1024]{3,2,1,0:T(8,128)}, f32[3,4,24,1024]{3,2,1,0:T(8,128)}, u32[]{:S(2)}, u32[]{:S(2)}) collective-permute-start(f32[3,4,24,1024]{3,2,1,0:T(8,128)} %get-tuple-element.22), channel_id=1, source_target_pairs={{0,30},{2,4},{4,2},{6,8},{8,6},{10,12},{12,10},{14,16},{16,14},{18... | collective-permute-start | bytes 3538952 | tf_op jit(solution)/shard_map/ppermute | solution.py:396
  187.4 87.3 %collective-permute-start.8 = (f32[3,3,192,512]{3,2,1,0:T(8,128)}, f32[3,3,192,512]{3,2,1,0:T(8,128)}, u32[]{:S(2)}, u32[]{:S(2)}) collective-permute-start(f32[3,3,192,512]{3,2,1,0:T(8,128)} %get-tuple-element.21), channel_id=1, source_target_pairs={{0,1},{1,0},{2,3},{3,2},{4,5},{5,4},{6,7},{7,6},{8,9},{9,8},{10,11... | collective-permute-start | bytes 10616840 | tf_op jit(solution)/shard_map/ppermute | solution.py:345
  202.8 76.8 %collective-permute-start.7 = (f32[3,4,64,1024]{3,2,1,0:T(8,128)}, f32[3,4,64,1024]{3,2,1,0:T(8,128)S(1)}, u32[]{:S(2)}, u32[]{:S(2)}) collective-permute-start(f32[3,4,64,1024]{3,2,1,0:T(8,128)} %get-tuple-element.20), channel_id=1, source_target_pairs={{0,30},{2,4},{4,2},{6,8},{8,6},{10,12},{12,10},{14,16},{16,14},{18... | collective-permute-start | bytes 9437192 | tf_op jit(solution)/shard_map/ppermute | solution.py:396
  207.5 75.2 %collective-permute-start.6 = (f32[3,4,8,1024]{3,2,1,0:T(8,128)}, f32[3,4,8,1024]{3,2,1,0:T(8,128)S(1)}, u32[]{:S(2)}, u32[]{:S(2)}) collective-permute-start(f32[3,4,8,1024]{3,2,1,0:T(8,128)} %get-tuple-element.19), channel_id=1, source_target_pairs={{0,30},{2,4},{4,2},{6,8},{8,6},{10,12},{12,10},{14,16},{16,14},{18... | collective-permute-start | bytes 1179656 | tf_op jit(solution)/shard_map/ppermute | solution.py:396
